TPU v7x, 512 devices: a whole 4x4x16 slice. The times are simulated.
512 devices in a mesh: seq: 32 (over y_lo, z), tp: 8 (over x, core), dp: 2 (over y_hi).
Axes of the slice: x: 4, y: 4 (y_hi: 2, y_lo: 2; y = y_hi * 2 + y_lo), z: 16, core: 2. Of those that a mesh axis runs over, the one named last changes fastest.
Arguments:
- hidden: bfloat16 [32768, 3072], P(('dp', 'seq'), 'tp'), parts along dimension 0, may hold values from -6 to 6
- shift_mod: float32 [6144], P('dp'), parts along dimension 0, may hold values from -3 to 3
- scale_mod: float32 [6144], P('dp'), parts along dimension 0, may hold values from -3 to 3
- gate: float32 [6144], P('dp'), parts along dimension 0, may hold values from -4 to 4
- w_qkv: bfloat16 [3072, 3, 2, 1024], P('seq', None, None, 'tp')
- w_out: bfloat16 [2, 1024, 3072], P(None, 'tp'), may hold values from -0.125 to 0.125
- window_tiles: int32 [8, 4], replicated, may hold values from 0 to 7, as said below
Outputs:
- mixed: bfloat16 [32768, 3072], P(('dp', 'seq'), 'tp'), parts along dimension 0
There are 2 independent parts, one for each index of `dp`. A program takes and returns all parts, laid end to end along the dimension named above; an argument that names none is the same for every part. Nothing has to cross between parts.
Inputs may be any that keep to these rules, and one draw needn't show every extreme that they name: `window_tiles`: row i holds 4 different tiles of a frame, and its first entry is i.
All inputs are finite; a program needn't handle non-finite values.
Results may differ from a plain program's by a relative error of at most 0.015.
Values may be sent and summed in bfloat16 or wider, within the bound.
No kernel may reach another device: no remote copies, remote signals or barrier semaphores. Data moves between devices by JAX's collectives and lax.ppermute only.
A program may use at most 64 MiB of HBM per device.

v0:
```python
import jax
import jax.numpy as jnp
from jax import lax
from jax.sharding import PartitionSpec as P

HD = 128
TILE = 64
WIN = 4


def layer_normed(hidden, shift_mod, scale_mod):
    source = hidden.astype(jnp.float32)
    middle = jnp.mean(source, -1, keepdims=True)
    centred = source - middle
    spread = jnp.mean(centred * centred, -1, keepdims=True)
    return (centred * lax.rsqrt(spread + 1e-06) * (1.0 + scale_mod) + shift_mod).astype(
        jnp.bfloat16
    )


def spatial_frame(queries, keys, values, window_tiles):
    rows = queries.shape[0]
    tiles = rows // TILE
    heads = queries.shape[1]
    query_tiles = queries.reshape(tiles, TILE, heads, HD)
    key_tiles = jnp.take(keys.reshape(tiles, TILE, heads, HD), window_tiles, axis=0).reshape(
        tiles, WIN * TILE, heads, HD
    )
    value_tiles = jnp.take(values.reshape(tiles, TILE, heads, HD), window_tiles, axis=0).reshape(
        tiles, WIN * TILE, heads, HD
    )
    scores = jnp.einsum(
        "nqhd,nkhd->nhqk", query_tiles, key_tiles, preferred_element_type=jnp.float32
    ) * float(HD) ** (-0.5)
    weights = jax.nn.softmax(scores, axis=-1).astype(jnp.bfloat16)
    result = jnp.einsum("nhqk,nkhd->nqhd", weights, value_tiles, preferred_element_type=jnp.float32)
    return result.astype(jnp.bfloat16).reshape(rows, heads * HD)


def temporal_heads(arrived):
    queries = arrived[:, :, 0]
    keys = arrived[:, :, 1]
    values = arrived[:, :, 2]
    scores = jnp.einsum(
        "fphd,gphd->phfg", queries, keys, preferred_element_type=jnp.float32
    ) * float(HD) ** (-0.5)
    weights = jax.nn.softmax(scores, axis=-1).astype(jnp.bfloat16)
    return jnp.einsum(
        "phfg,gphd->fphd", weights, values, preferred_element_type=jnp.float32
    ).astype(jnp.bfloat16)


def body(hidden, shift_mod, scale_mod, gate, w_qkv, w_out, window_tiles):
    whole = lax.all_gather(hidden, "tp", axis=1, tiled=True)
    rows = whole.shape[0]
    normed = layer_normed(whole, shift_mod, scale_mod)
    local_heads = w_qkv.shape[3] // HD
    columns = 6 * local_heads * HD
    flat_weight = w_qkv.reshape(w_qkv.shape[0], columns)
    summed = jnp.dot(
        normed,
        lax.all_gather(flat_weight, "seq", axis=0, tiled=True),
        preferred_element_type=jnp.float32,
    )
    projected = summed.astype(jnp.bfloat16).reshape(rows, 3, 2, local_heads, HD)
    temporal_in = projected[:, :, 1][None]
    at_positions = temporal_heads(
        lax.all_to_all(temporal_in, "seq", split_axis=1, concat_axis=0, tiled=True)
    )
    spatial = spatial_frame(
        projected[:, 0, 0], projected[:, 1, 0], projected[:, 2, 0], window_tiles
    )
    temporal = lax.all_to_all(at_positions, "seq", split_axis=0, concat_axis=1, tiled=True).reshape(
        rows, local_heads * HD
    )
    attended = jnp.stack([spatial, temporal], axis=1).reshape(rows, 2 * local_heads * HD)
    width = hidden.shape[1]
    terms = jnp.dot(
        attended,
        w_out.reshape(2 * local_heads * HD, w_out.shape[2]),
        preferred_element_type=jnp.float32,
    )
    branch = lax.psum_scatter(
        terms.astype(jnp.bfloat16), "tp", scatter_dimension=1, tiled=True
    ).astype(jnp.float32)
    gate_local = lax.dynamic_slice_in_dim(gate, lax.axis_index("tp") * width, width)
    return (hidden.astype(jnp.float32) + gate_local * branch).astype(jnp.bfloat16)


def solution(mesh):
    in_specs = (
        P(("dp", "seq"), "tp"),
        P("dp"),
        P("dp"),
        P("dp"),
        P("seq", None, None, "tp"),
        P(None, "tp", None),
        P(),
    )
    out_specs = P(("dp", "seq"), "tp")
    return jax.shard_map(body, mesh=mesh, in_specs=in_specs, out_specs=out_specs, check_vma=False)
```

profile of v0, /device:TPU:1, one launch (start us, length us, event | category | flops | bytes accessed | tf_op | source)
XLA Modules:
  0.0 303.3 jit_solution(9827333422784857345)
XLA Ops:
  6.5 0.7 all-gather.3.cloned.1.call-update
  7.3 1.6 reshape.109
  9.0 0.7 broadcast_add_fusion
  9.7 40.9 %all-gather.3.cloned.1.call-done = bf16[512,3072]{1,0:T(8,128)(2,1)} async-done(((bf16[512,384]{1,0:T(8,128)(2,1)}), bf16[512,3072]{1,0:T(8,128)(2,1)}) %all-gather.3.cloned.1.call-update) | async-done | bytes 3145744 | tf_op jit(solution)/shard_map/all_gather | solution.py:54
  50.6 2.5 convert_reduce_fusion
  53.2 0.3 copy-done.1
  53.5 1.0 fusion.4
  54.4 120.6 %all-gather.5.cloned.1.call-done = bf16[3072,768]{1,0:T(8,128)(2,1)} async-done(((bf16[96,768]{1,0:T(8,128)(2,1)}), bf16[3072,768]{1,0:T(8,128)(2,1)}) %all-gather.5.cloned.1.call-update) | async-done | bytes 4718608 | tf_op jit(solution)/shard_map/all_gather | solution.py:62
  175.0 7.2 %fusion.14 = bf16[512,768]{1,0:T(8,128)(2,1)} fusion(bf16[3072,768]{1,0:T(8,128)(2,1)} %all-gather.5.cloned.1.call-done, bf16[512,3072]{1,0:T(8,128)(2,1)} %all-gather.3.cloned.1.call-done, f32[3072]{0:T(1024)S(1)} %copy-done.5, f32[3072]{0:T(1024)S(1)} %broadcast_add_fusion, f32[512]{0:T(512)S(1)} %add_rsqrt_fusion, f32[512]{0:T(512)S(1)} %broadcast_multiply_fusion), kind=kOutput, calls=%fused_computation.18 | convolution fusion | flops 2425749504 | bytes 8679424 | tf_op jit(solution)/shard_map/dot_general | solution.py:60
  182.2 2.0 reshape.110
  184.2 0.8 slice.35
  185.2 1.1 copy.49
  186.3 4.5 %all-to-all-start = ((bf16[1,512,3,1,128]{4,2,3,0,1:T(4,128)(2,1)}), bf16[1,512,3,1,128]{4,2,3,0,1:T(4,128)(2,1)S(1)}, u32[]{:S(2)}, u32[]{:S(2)}) async-start(bf16[1,512,3,1,128]{4,2,3,0,1:T(4,128)(2,1)} %copy.49), calls=%async_computation | async-start | bytes 1048576 | tf_op jit(solution)/shard_map/all_to_all | solution.py:68
  191.0 0.5 fusion.31
  191.6 0.6 gather_fusion
  192.3 1.4 gather_fusion.1
  193.8 2.0 broadcast_select_fusion
  195.8 16.1 %all-to-all-done = bf16[1,512,3,1,128]{4,2,3,0,1:T(4,128)(2,1)S(1)} async-done(((bf16[1,512,3,1,128]{4,2,3,0,1:T(4,128)(2,1)}), bf16[1,512,3,1,128]{4,2,3,0,1:T(4,128)(2,1)S(1)}, u32[]{:S(2)}, u32[]{:S(2)}) %all-to-all-start) | async-done | bytes 393248 | tf_op jit(solution)/shard_map/all_to_all | solution.py:68
  212.0 0.2 fusion.33
  212.2 0.2 fusion.21
  212.5 0.7 copy.55
  213.2 4.0 %all-to-all-start.1 = ((bf16[32,16,1,128]{3,1,2,0:T(8,128)(2,1)}), bf16[32,16,1,128]{3,1,2,0:T(8,128)(2,1)S(1)}, u32[]{:S(2)}, u32[]{:S(2)}) async-start(bf16[32,16,1,128]{3,1,2,0:T(8,128)(2,1)} %copy.55), calls=%async_computation.1 | async-start | bytes 262144 | tf_op jit(solution)/shard_map/all_to_all | solution.py:73
  217.2 0.3 convolution_multiply_fusion
  217.5 0.2 fusion.34
  217.8 1.0 convolution_convert_fusion
  218.8 14.5 %all-to-all-done.1 = bf16[32,16,1,128]{3,1,2,0:T(8,128)(2,1)S(1)} async-done(((bf16[32,16,1,128]{3,1,2,0:T(8,128)(2,1)}), bf16[32,16,1,128]{3,1,2,0:T(8,128)(2,1)S(1)}, u32[]{:S(2)}, u32[]{:S(2)}) %all-to-all-start.1) | async-done | bytes 131104 | tf_op jit(solution)/shard_map/all_to_all | solution.py:73
  233.2 2.7 bitcast_convert_fusion
  235.9 4.7 %copy.57 = bf16[512,3072]{0,1:T(8,128)(2,1)} copy(bf16[512,3072]{1,0:T(8,128)(2,1)} %bitcast_convert_fusion) | data formatting | bytes 6291456
  240.7 0.8 dynamic_slice.3
  241.4 53.3 %reduce-scatter.4.cloned.1.call-done = bf16[384,512]{1,0:T(8,128)(2,1)} async-done(((bf16[3072,512]{1,0:T(8,128)(2,1)}), bf16[384,512]{1,0:T(8,128)(2,1)}) %reduce-scatter.4.cloned.1.call-update) | async-done | bytes 393232
  294.7 1.2 copy.58
  295.9 0.9 add_convert_fusion
  (30 shorter events, 0.6 us)
Async XLA Ops:
  6.5 226.7 %copy-start = (bf16[2,128,3072]{2,1,0:T(8,128)(2,1)S(1)}, bf16[2,128,3072]{2,1,0:T(8,128)(2,1)}, u32[]{:S(2)}) copy-start(bf16[2,128,3072]{2,1,0:T(8,128)(2,1)} %param.14) | copy-start | bytes 4718596
  6.5 168.5 %copy-start.5 = (f32[3072]{0:T(1024)S(1)}, f32[3072]{0:T(1024)}, u32[]{:S(2)}) copy-start(f32[3072]{0:T(1024)} %param.10) | copy-start | bytes 36868
  6.5 44.1 %all-gather.3.cloned.1.call-start = ((), (), s32[]{:S(2)}) async-start(), calls=%async_computation.3 | async-start | bytes 3538944 | tf_op jit(solution)/shard_map/all_gather | solution.py:54
  7.3 167.7 %all-gather.5.cloned.1.call-start = ((), (), s32[]{:S(2)}) async-start(), calls=%async_computation.4 | async-start | bytes 4866048 | tf_op jit(solution)/shard_map/all_gather | solution.py:62
  50.6 2.8 copy-start.1
  182.2 8.5 %copy-start.4 = (s32[8,4]{0,1:T(4,128)S(1)}, s32[8,4]{0,1:T(4,128)}, u32[]{:S(2)}) copy-start(s32[8,4]{0,1:T(4,128)} %param.15) | copy-start | bytes 388
  186.3 25.6 %all-to-all-start = ((bf16[1,512,3,1,128]{4,2,3,0,1:T(4,128)(2,1)}), bf16[1,512,3,1,128]{4,2,3,0,1:T(4,128)(2,1)S(1)}, u32[]{:S(2)}, u32[]{:S(2)}) async-start(bf16[1,512,3,1,128]{4,2,3,0,1:T(4,128)(2,1)} %copy.49), calls=%async_computation | async-start | bytes 1048576 | tf_op jit(solution)/shard_map/all_to_all | solution.py:68
  195.8 22.0 %copy-start.3 = (bf16[8,4,64,1,128]{4,2,1,0,3:T(8,128)(2,1)S(1)}, bf16[8,4,64,1,128]{4,2,1,0,3:T(8,128)(2,1)}, u32[]{:S(2)}) copy-start(bf16[8,4,64,1,128]{4,2,1,0,3:T(8,128)(2,1)} %get-tuple-element.13) | copy-start | bytes 1572868
  213.2 20.0 %all-to-all-start.1 = ((bf16[32,16,1,128]{3,1,2,0:T(8,128)(2,1)}), bf16[32,16,1,128]{3,1,2,0:T(8,128)(2,1)S(1)}, u32[]{:S(2)}, u32[]{:S(2)}) async-start(bf16[32,16,1,128]{3,1,2,0:T(8,128)(2,1)} %copy.55), calls=%async_computation.1 | async-start | bytes 262144 | tf_op jit(solution)/shard_map/all_to_all | solution.py:73
  217.2 77.5 %reduce-scatter.4.cloned.1.call-start = ((), (), s32[]{:S(2)}) async-start(), calls=%async_computation.5 | async-start | bytes 3538944
  235.9 60.0 %copy-start.2 = (bf16[512,384]{1,0:T(8,128)(2,1)S(1)}, bf16[512,384]{1,0:T(8,128)(2,1)}, u32[]{:S(2)}) copy-start(bf16[512,384]{1,0:T(8,128)(2,1)} %param.9) | copy-start | bytes 1179652
Sparse Core Ops, SparseCore 0:
  9.5 41.0 all-gather.2
  52.7 122.2 all-gather.4
  240.8 53.8 reduce-scatter.3
where the time goes:
time: 305 us; the launch traced here: 303 us
  waiting for transfers between devices  246 us (81%)
  local copies, waits for them, and re-layouts  16.4 us (5%)
  between operations  13.3 us (4%)
  matrix products  11.6 us (4%)
  starting transfers between devices  8.52 us (3%)
  other arithmetic  7.35 us (2%)
    all_gather x1, waiting for transfers between devices, body(): lax.all_gather(flat_weight, 'seq', axis=0, tiled=True)  121 us
    unnamed x4, waiting for transfers between devices  54 us
    all_gather x1, waiting for transfers between devices, body(): whole = lax.all_gather(hidden, 'tp', axis=1, tiled=True)  40.9 us
    all_to_all x1, waiting for transfers between devices, body(): lax.all_to_all(temporal_in, 'seq', split_axis=1, concat_axis=0, tiled=True)  16.1 us
    all_to_all x1, waiting for transfers between devices, body(): lax.all_to_all(at_positions, 'seq', split_axis=0, concat_axis=1, tiled=True)  14.5 us
    dot_general x1, matrix products, body(): jnp.dot(normed, lax.all_gather(flat_weight, 'seq', axis=0, tiled=True), p...  7.19 us
    unnamed x18, local copies, waits for them, and re-layouts  6.36 us
  transfers between devices with their start and end apart: 5, of which 5 were waited for; matrix products, arithmetic and copies ran while one was open for 4% of the time, Pallas kernels for 0%

commit v1 on v0

v1 whole, which is shorter than its diff:
```python
import functools

import jax
import jax.numpy as jnp
from jax import lax
from jax.experimental import pallas as pl
from jax.experimental.pallas import tpu as pltpu
from jax.sharding import Mesh, PartitionSpec as P

D = 3072
HD = 128
TILE = 64
WIN = 4
F32 = jnp.float32
BF16 = jnp.bfloat16
VMEM = pl.BlockSpec(memory_space=pltpu.VMEM)
SMEM = pl.BlockSpec(memory_space=pltpu.SMEM)
HBM = pl.BlockSpec(memory_space=pl.ANY)

Y_PLACE = (0, 2, 1, 3)


def along_z(value, step):
    return lax.ppermute(value, "z", [(i, (i + step) % 16) for i in range(16)])


def along_x(value, step):
    return lax.ppermute(value, "x", [(i, (i + step) % 4) for i in range(4)])


def along_y(value, step):
    return lax.ppermute(value, ("yl", "dp"), [(Y_PLACE[i], Y_PLACE[(i + step) % 4]) for i in range(4)])


def other_core(value):
    return lax.ppermute(value, "c", [(0, 1), (1, 0)])


def over_tp(value):
    mine = jnp.stack([value, along_x(value, 1), along_x(value, -1), along_x(value, 2)])
    return mine, other_core(mine)


def normalise(order, mine, theirs, shift, scale, normed):
    def rows_of(step, _):
        rows = pl.ds(pl.multiple_of(step * 16, 16), 16)
        blocks = [mine[j, rows, :].astype(F32) for j in range(4)] + [theirs[j, rows, :].astype(F32) for j in range(4)]
        middle = jnp.sum(sum(blocks), -1, keepdims=True) * (1.0 / D)
        blocks = [block - middle for block in blocks]
        spread = jnp.sum(sum(block * block for block in blocks), -1, keepdims=True) * (1.0 / D)
        inverse = lax.rsqrt(spread + 1e-06)
        for j in range(8):
            group = order[j]
            value = blocks[j] * inverse * (1.0 + scale[pl.ds(group, 1), :]) + shift[pl.ds(group, 1), :]
            normed[rows, pl.ds(pl.multiple_of(group * 384, 128), 384)] = value.astype(BF16)
        return 0

    lax.fori_loop(0, 32, rows_of, 0)


def project(normed, weight, projected):
    def tile_of(step, _):
        rows = pl.ds(pl.multiple_of(step * 128, 128), 128)
        projected[rows, :] = jnp.dot(normed[rows, :], weight[...], preferred_element_type=F32).astype(BF16)
        return 0

    lax.fori_loop(0, 4, tile_of, 0)


def softmax(scores):
    raised = jnp.exp(scores - jnp.max(scores, -1, keepdims=True))
    return (raised / jnp.sum(raised, -1, keepdims=True)).astype(BF16)


def scores_of(queries, keys):
    return lax.dot_general(queries, keys, (((1,), (1,)), ((), ())), preferred_element_type=F32) * float(HD) ** (-0.5)


def temporal_kernel(layout, *refs):
    pieces = refs[: len(layout)]
    order, places, mine, theirs, shift, scale, out, weight, normed, projected, sem = refs[len(layout) :]
    copies = []
    at = 0
    for piece, count in zip(pieces, layout):
        for i in range(count):
            start = pl.multiple_of(places[at] * 96, 32)
            copies.append(pltpu.make_async_copy(piece.at[pl.ds(i * 96, 96), :], weight.at[pl.ds(start, 96), :], sem.at[at]))
            copies[-1].start()
            at += 1
    normalise(order, mine, theirs, shift, scale, normed)
    for copy in copies:
        copy.wait()
    project(normed, weight, projected)

    def tile_of(step, _):
        rows = pl.ds(pl.multiple_of(step * 128, 128), 128)
        scores = scores_of(projected[rows, 0:128], projected[:, 128:256])
        at_row = lax.broadcasted_iota(jnp.int32, scores.shape, 0) % 16
        at_column = lax.broadcasted_iota(jnp.int32, scores.shape, 1) % 16
        weights = softmax(jnp.where(at_row == at_column, scores, -1e30))
        out[rows, :] = jnp.dot(weights, projected[:, 256:384], preferred_element_type=F32).astype(BF16)
        return 0

    lax.fori_loop(0, 4, tile_of, 0)


def spatial_kernel(gathered, order, yl, window, mine, theirs, shift, scale, out, weight, normed, projected, sem):
    copies = []
    for z in range(16):
        for half in range(2):
            start = pl.multiple_of(((yl[0] + half) % 2 * 16 + z) * 96, 32)
            copies.append(
                pltpu.make_async_copy(
                    gathered.at[pl.ds(z * 192 + half * 96, 96), :], weight.at[pl.ds(start, 96), :], sem.at[z * 2 + half]
                )
            )
            copies[-1].start()
    normalise(order, mine, theirs, shift, scale, normed)
    for copy in copies:
        copy.wait()
    project(normed, weight, projected)

    def tile_of(step, _):
        rows = pl.ds(pl.multiple_of(step * TILE, TILE), TILE)
        chosen = [pl.ds(pl.multiple_of(window[step, i] * TILE, TILE), TILE) for i in range(WIN)]
        keys = jnp.concatenate([projected[there, 128:256] for there in chosen], 0)
        values = jnp.concatenate([projected[there, 256:384] for there in chosen], 0)
        weights = softmax(scores_of(projected[rows, 0:128], keys))
        out[rows, :] = jnp.dot(weights, values, preferred_element_type=F32).astype(BF16)
        return 0

    lax.fori_loop(0, 8, tile_of, 0)


def heads_kernel(kind, order, mine, theirs, w_out, *refs):
    wide = refs[-1]
    total = jnp.zeros((512, 384), F32)
    for j in range(8):
        block = mine[j] if j < 4 else theirs[j - 4]
        wide[:, pl.ds(pl.multiple_of(order[j] * HD, HD), HD)] = block
    rows = jnp.concatenate([w_out[g, pl.ds(kind * HD, HD), :] for g in range(8)], 0)
    total = jnp.dot(wide[...], rows, preferred_element_type=F32)
    if kind == 0:
        refs[0][...] = total
    else:
        spatial, hidden, gate, out = refs[:4]
        out[...] = (hidden[...].astype(F32) + gate[...] * (total + spatial[...])).astype(BF16)


def params(flops, size):
    return dict(
        compiler_params=pltpu.CompilerParams(vmem_limit_bytes=32 * 1024 * 1024),
        cost_estimate=pl.CostEstimate(flops=flops, bytes_accessed=size, transcendentals=0),
    )


QKV_SCRATCH = [
    pltpu.VMEM((D, 384), BF16),
    pltpu.VMEM((512, D), BF16),
    pltpu.VMEM((512, 384), BF16),
    pltpu.SemaphoreType.DMA((32,)),
]


def body(hidden, shift_mod, scale_mod, gate, w_qkv, w_out, window_tiles):
    x, core, z, yl = (lax.axis_index(name) for name in ("x", "c", "z", "yl"))
    shift, scale = shift_mod.reshape(8, 384), scale_mod.reshape(8, 384)
    order = jnp.stack([(x + dx) % 4 * 2 + side for side in (core, 1 - core) for dx in (0, 3, 1, 2)]).astype(jnp.int32)

    w_temporal = w_qkv[:, :, 1].reshape(96, 384)
    w_spatial = w_qkv[:, :, 0].reshape(96, 384)

    pair = jnp.concatenate([w_spatial, lax.ppermute(w_spatial, "yl", [(0, 1), (1, 0)])], 0)
    gathered = lax.all_gather(pair, "z", axis=0, tiled=True)

    by_position = lax.all_to_all(
        hidden.reshape(32, 16, 384), ("yl", "z"), split_axis=0, concat_axis=0, tiled=True
    ).reshape(512, 384)

    first = jnp.concatenate([w_temporal, along_z(w_temporal, 5), along_z(w_temporal, -5)], 0)
    below = along_z(first, 1)
    above = along_z(first, -1)
    near_a = along_y(jnp.concatenate([first[:96], below], 0), 1)
    near_b = along_y(jnp.concatenate([first[96:], above], 0), -1)
    far_below = along_z(below, 1)
    far_above = along_z(above, -1)
    opposite = along_z(above[192:], -2)
    near_c = along_y(jnp.concatenate([far_below, opposite], 0), 1)
    near_d = along_y(far_above, -1)
    blocks = (
        (first, (0, -5, 5), 0),
        (below, (-1, -6, 4), 0),
        (above, (1, -4, 6), 0),
        (far_below, (-2, -7, 3), 0),
        (far_above, (2, -3, 7), 0),
        (opposite, (8,), 0),
        (near_a, (0, -1, -6, 4), 1),
        (near_b, (-5, 5, 1, -4, 6), 1),
        (near_c, (-2, -7, 3, 8), 1),
        (near_d, (2, -3, 7), 1),
    )
    places = jnp.stack(
        [(yl + side) % 2 * 16 + (z + offset + 16) % 16 for _, offsets, side in blocks for offset in offsets]
    ).astype(jnp.int32)

    mine, theirs = over_tp(hidden)
    mine_t, theirs_t = over_tp(by_position)

    columns = lax.all_to_all(
        w_out.reshape(256, 8, 384).transpose(1, 0, 2), ("x", "c"), split_axis=0, concat_axis=0, tiled=True
    )

    layout = tuple(len(offsets) for _, offsets, _ in blocks)
    temporal = pl.pallas_call(
        functools.partial(temporal_kernel, layout),
        out_shape=jax.ShapeDtypeStruct((512, HD), BF16),
        in_specs=[HBM] * len(blocks) + [SMEM, SMEM, VMEM, VMEM, VMEM, VMEM],
        out_specs=VMEM,
        scratch_shapes=QKV_SCRATCH,
        name="temporal",
        **params(1_300_000_000, 6_000_000),
    )(*[block for block, _, _ in blocks], order, places, mine_t, theirs_t, shift, scale)
    temporal = lax.all_to_all(
        temporal.reshape(32, 16, HD), ("yl", "z"), split_axis=0, concat_axis=0, tiled=True
    ).reshape(512, HD)

    spatial = pl.pallas_call(
        spatial_kernel,
        out_shape=jax.ShapeDtypeStruct((512, HD), BF16),
        in_specs=[HBM, SMEM, SMEM, SMEM, VMEM, VMEM, VMEM, VMEM],
        out_specs=VMEM,
        scratch_shapes=QKV_SCRATCH,
        name="spatial",
        **params(1_300_000_000, 6_000_000),
    )(gathered, order, yl.astype(jnp.int32).reshape(1), window_tiles, mine, theirs, shift, scale)

    spatial_heads = over_tp(spatial)
    temporal_heads = over_tp(temporal)
    gate_here = lax.dynamic_slice_in_dim(gate, (x * 2 + core) * 384, 384).reshape(1, 384)
    share = pl.pallas_call(
        functools.partial(heads_kernel, 0),
        out_shape=jax.ShapeDtypeStruct((512, 384), F32),
        in_specs=[SMEM, VMEM, VMEM, VMEM],
        out_specs=VMEM,
        scratch_shapes=[pltpu.VMEM((512, 1024), BF16)],
        name="spatial_share",
        **params(400_000_000, 3_000_000),
    )(order, *spatial_heads, columns)
    return pl.pallas_call(
        functools.partial(heads_kernel, 1),
        out_shape=jax.ShapeDtypeStruct((512, 384), BF16),
        in_specs=[SMEM] + [VMEM] * 6,
        out_specs=VMEM,
        scratch_shapes=[pltpu.VMEM((512, 1024), BF16)],
        name="mixed",
        **params(400_000_000, 4_000_000),
    )(order, *temporal_heads, columns, share, hidden, gate_here)


def solution(mesh):
    fine = Mesh(mesh.devices.reshape(2, 16, 4, 2, 2), ("yl", "z", "x", "c", "dp"))
    seq, tp = ("yl", "z"), ("x", "c")
    in_specs = (
        P(("dp",) + seq, tp),
        P("dp"),
        P("dp"),
        P("dp"),
        P(seq, None, None, tp),
        P(None, tp, None),
        P(),
    )
    out_specs = P(("dp",) + seq, tp)
    return jax.shard_map(body, mesh=fine, in_specs=in_specs, out_specs=out_specs, check_vma=False)
```

time: 305 us -> 276 us (0.905)
  waiting for transfers between devices: 246 us -> 59.5 us
  starting transfers between devices: 8.52 us -> 134 us
  Pallas kernels: 0 us -> 37.2 us
  matrix products: 11.6 us -> 0 us
  local copies, waits for them, and re-layouts: 16.4 us -> 25 us
    all_gather x2 -> x1, waiting for transfers between devices: 162 us -> 0.01 us  [body(): gathered = lax.all_gather(pair, 'z', axis=0, tiled=True)]
    ppermute x0 -> x28, starting transfers between devices: none -> 101 us  [the longest x12 39.1 us: along_x(): return lax.ppermute(value, 'x', [(i, (i + step) % 4) for i in range(4)])]
    unnamed x4 -> x1, waiting for transfers between devices: 54 us -> 0.02 us
    pallas_call x0 -> x4, Pallas kernels: none -> 37.2 us  [the longest x1 17.9 us: body(): pl.pallas_call(spatial_kernel, out_shape=jax.ShapeDtypeStruct((512, HD),...]
    ppermute x0 -> x28, waiting for transfers between devices: none -> 31.6 us  [the longest x7 15.7 us: along_z(): return lax.ppermute(value, 'z', [(i, (i + step) % 16) for i in range(16)])]
    all_to_all x2 -> x3, starting transfers between devices: 8.44 us -> 33.5 us  [the longest x1 17 us: body(): lax.all_to_all(hidden.reshape(32, 16, 384), ('yl', 'z'), split_axis=0, co...]
    dot_general x5 -> x0, matrix products: 11.4 us -> none  [the longest x1 7.19 us: body(): jnp.dot(normed, lax.all_gather(flat_weight, 'seq', axis=0, tiled=True), p...]
    unnamed x18 -> x57, local copies, waits for them, and re-layouts: 6.36 us -> 17.4 us
  transfers between devices with their start and end apart: 5 -> 32, of which waited for: 5 -> 11; matrix products, arithmetic and copies ran while one was open for 4% -> 5% of each run, Pallas kernels for 0% -> 12%
where the time goes in v1:
time: 276 us; the launch traced here: 274 us
  starting transfers between devices  134 us (49%)
  waiting for transfers between devices  59.5 us (22%)
  Pallas kernels  37.2 us (13%)
  local copies, waits for them, and re-layouts  25 us (9%)
  between operations  14.2 us (5%)
  other arithmetic  4.56 us (2%)
    ppermute x12, starting transfers between devices, along_x(): return lax.ppermute(value, 'x', [(i, (i + step) % 4) for i in range(4)])  39.1 us
    ppermute x7, starting transfers between devices, along_z(): return lax.ppermute(value, 'z', [(i, (i + step) % 16) for i in range(16)])  27.2 us
    pallas_call x1, Pallas kernels, body(): pl.pallas_call(spatial_kernel, out_shape=jax.ShapeDtypeStruct((512, HD),...  17.9 us
    ppermute x4, starting transfers between devices, other_core(): return lax.ppermute(value, 'c', [(0, 1), (1, 0)])  17.9 us
    unnamed x57, local copies, waits for them, and re-layouts  17.4 us
    all_to_all x1, starting transfers between devices, body(): lax.all_to_all(hidden.reshape(32, 16, 384), ('yl', 'z'), split_axis=0, co...  17 us
    all_to_all x1, waiting for transfers between devices, body(): lax.all_to_all(hidden.reshape(32, 16, 384), ('yl', 'z'), split_axis=0, co...  16.6 us
    ppermute x7, waiting for transfers between devices, along_z(): return lax.ppermute(value, 'z', [(i, (i + step) % 16) for i in range(16)])  15.7 us
  transfers between devices with their start and end apart: 32, of which 11 were waited for; matrix products, arithmetic and copies ran while one was open for 5% of the time, Pallas kernels for 12%

profile of v1, /device:TPU:1, one launch (start us, length us, event | category | flops | bytes accessed | tf_op | source)
XLA Modules:
  0.0 274.5 jit_solution(7098881507729219751)
XLA Ops:
  6.5 17.0 %all-to-all-start = ((bf16[32,16,384]{2,1,0:T(8,128)(2,1)}), bf16[32,16,384]{2,1,0:T(8,128)(2,1)S(1)}, u32[]{:S(2)}, u32[]{:S(2)}) async-start(bf16[32,16,384]{2,1,0:T(8,128)(2,1)} %bitcast.75), calls=%async_computation | async-start | bytes 786432 | tf_op jit(solution)/shard_map/all_to_all | solution.py:176
  26.2 3.1 %collective-permute-start.19 = (bf16[96,384]{1,0:T(8,128)(2,1)S(1)}, bf16[96,384]{1,0:T(8,128)(2,1)S(1)}, u32[]{:S(2)}, u32[]{:S(2)}) collective-permute-start(bf16[96,384]{1,0:T(8,128)(2,1)S(1)} %bitcast.94), channel_id=1, source_target_pairs={{0,256},{256,0},{1,257},{257,1},{2,258},{258,2},{3,259},{259,3},{4... | collective-permute-start | bytes 221192 | tf_op jit(solution)/shard_map/ppermute | solution.py:173
  32.1 16.6 %all-to-all-done = bf16[32,16,384]{2,1,0:T(8,128)(2,1)S(1)} async-done(((bf16[32,16,384]{2,1,0:T(8,128)(2,1)}), bf16[32,16,384]{2,1,0:T(8,128)(2,1)S(1)}, u32[]{:S(2)}, u32[]{:S(2)}) %all-to-all-start) | async-done | bytes 393248 | tf_op jit(solution)/shard_map/all_to_all | solution.py:176
  48.6 3.1 %collective-permute-start.11 = (bf16[512,384]{1,0:T(8,128)(2,1)S(1)}, bf16[512,384]{1,0:T(8,128)(2,1)S(1)}, u32[]{:S(2)}, u32[]{:S(2)}) collective-permute-start(bf16[512,384]{1,0:T(8,128)(2,1)S(1)} %bitcast.82), channel_id=1, source_target_pairs={{0,4},{4,8},{8,12},{12,0},{1,5},{5,9},{9,13},{13,1},{2,6},{6,10},{... | collective-permute-start | bytes 1179656 | tf_op jit(solution)/shard_map/ppermute | solution.py:28
  51.7 3.4 %collective-permute-start.12 = (bf16[512,384]{1,0:T(8,128)(2,1)S(1)}, bf16[512,384]{1,0:T(8,128)(2,1)S(1)}, u32[]{:S(2)}, u32[]{:S(2)}) collective-permute-start(bf16[512,384]{1,0:T(8,128)(2,1)S(1)} %bitcast.83), channel_id=1, source_target_pairs={{0,12},{4,0},{8,4},{12,8},{1,13},{5,1},{9,5},{13,9},{2,14},{6,2},{... | collective-permute-start | bytes 1179656 | tf_op jit(solution)/shard_map/ppermute | solution.py:28
  55.1 3.4 %collective-permute-start.13 = (bf16[512,384]{1,0:T(8,128)(2,1)S(1)}, bf16[512,384]{1,0:T(8,128)(2,1)S(1)}, u32[]{:S(2)}, u32[]{:S(2)}) collective-permute-start(bf16[512,384]{1,0:T(8,128)(2,1)S(1)} %bitcast.84), channel_id=1, source_target_pairs={{0,8},{4,12},{8,0},{12,4},{1,9},{5,13},{9,1},{13,5},{2,10},{6,14},... | collective-permute-start | bytes 1179656 | tf_op jit(solution)/shard_map/ppermute | solution.py:28
  61.0 8.7 %collective-permute-done.13 = bf16[512,384]{1,0:T(8,128)(2,1)S(1)} collective-permute-done((bf16[512,384]{1,0:T(8,128)(2,1)S(1)}, bf16[512,384]{1,0:T(8,128)(2,1)S(1)}, u32[]{:S(2)}, u32[]{:S(2)}) %collective-permute-start.13) | collective-permute-done | bytes 393248 | tf_op jit(solution)/shard_map/ppermute | solution.py:28
  70.0 5.1 %collective-permute-start.14 = (bf16[4,512,384]{2,1,0:T(8,128)(2,1)S(1)}, bf16[4,512,384]{2,1,0:T(8,128)(2,1)}, u32[]{:S(2)}, u32[]{:S(2)}) collective-permute-start(bf16[4,512,384]{2,1,0:T(8,128)(2,1)S(1)} %pad_maximum_fusion.refs_12_), channel_id=1, source_target_pairs={{0,2},{2,0},{1,3},{3,1},{4,6},{6,4},{5,7},{7,5},{8,10},{10,8},{9,1... | collective-permute-start | bytes 4718600 | tf_op jit(solution)/shard_map/ppermute | solution.py:36
  75.1 5.8 %collective-permute-start = (bf16[96,384]{1,0:T(8,128)(2,1)S(1)}, bf16[96,384]{1,0:T(8,128)(2,1)S(1)}, u32[]{:S(2)}, u32[]{:S(2)}) collective-permute-start(bf16[96,384]{1,0:T(8,128)(2,1)S(1)} %get-tuple-element.8), channel_id=1, source_target_pairs={{0,80},{16,96},{32,112},{48,128},{64,144},{80,160},{96,176},{112,1... | collective-permute-start | bytes 221192 | tf_op jit(solution)/shard_map/ppermute | solution.py:24
  80.9 5.5 %collective-permute-start.1 = (bf16[96,384]{1,0:T(8,128)(2,1)S(1)}, bf16[96,384]{1,0:T(8,128)(2,1)S(1)}, u32[]{:S(2)}, u32[]{:S(2)}) collective-permute-start(bf16[96,384]{1,0:T(8,128)(2,1)S(1)} %get-tuple-element.8), channel_id=1, source_target_pairs={{0,176},{16,192},{32,208},{48,224},{64,240},{80,0},{96,16},{112,32... | collective-permute-start | bytes 221192 | tf_op jit(solution)/shard_map/ppermute | solution.py:24
  86.4 6.1 %collective-permute-done = bf16[96,384]{1,0:T(8,128)(2,1)S(1)} collective-permute-done((bf16[96,384]{1,0:T(8,128)(2,1)S(1)}, bf16[96,384]{1,0:T(8,128)(2,1)S(1)}, u32[]{:S(2)}, u32[]{:S(2)}) %collective-permute-start) | collective-permute-done | bytes 73760 | tf_op jit(solution)/shard_map/ppermute | solution.py:24
  92.5 4.2 %collective-permute-done.1 = bf16[96,384]{1,0:T(8,128)(2,1)S(1)} collective-permute-done((bf16[96,384]{1,0:T(8,128)(2,1)S(1)}, bf16[96,384]{1,0:T(8,128)(2,1)S(1)}, u32[]{:S(2)}, u32[]{:S(2)}) %collective-permute-start.1) | collective-permute-done | bytes 73760 | tf_op jit(solution)/shard_map/ppermute | solution.py:24
  98.7 3.9 %collective-permute-start.20 = (bf16[512,384]{1,0:T(8,128)(2,1)S(1)}, bf16[512,384]{1,0:T(8,128)(2,1)S(1)}, u32[]{:S(2)}, u32[]{:S(2)}) collective-permute-start(bf16[512,384]{1,0:T(8,128)(2,1)S(1)} %copy-done), channel_id=1, source_target_pairs={{0,4},{4,8},{8,12},{12,0},{1,5},{5,9},{9,13},{13,1},{2,6},{6,10},{... | collective-permute-start | bytes 1179656 | tf_op jit(solution)/shard_map/ppermute | solution.py:28
  102.6 3.5 %collective-permute-start.21 = (bf16[512,384]{1,0:T(8,128)(2,1)S(1)}, bf16[512,384]{1,0:T(8,128)(2,1)S(1)}, u32[]{:S(2)}, u32[]{:S(2)}) collective-permute-start(bf16[512,384]{1,0:T(8,128)(2,1)S(1)} %copy-done), channel_id=1, source_target_pairs={{0,12},{4,0},{8,4},{12,8},{1,13},{5,1},{9,5},{13,9},{2,14},{6,2},{... | collective-permute-start | bytes 1179656 | tf_op jit(solution)/shard_map/ppermute | solution.py:28
  109.2 3.4 %collective-permute-start.2 = (bf16[288,384]{1,0:T(8,128)(2,1)S(1)}, bf16[288,384]{1,0:T(8,128)(2,1)S(1)}, u32[]{:S(2)}, u32[]{:S(2)}) collective-permute-start(bf16[288,384]{1,0:T(8,128)(2,1)S(1)} %constant_dynamic-update-slice_fusion.refs_0_), channel_id=1, source_target_pairs={{0,16},{16,32},{32,48},{48,64},{64,80},{80,96},{96,112},{112,128},... | collective-permute-start | bytes 663560 | tf_op jit(solution)/shard_map/ppermute | solution.py:24
  113.3 5.4 %collective-permute-done.2.refs_1_ = bf16[288,384]{1,0:T(8,128)(2,1)S(1)} collective-permute-done((bf16[288,384]{1,0:T(8,128)(2,1)S(1)}, bf16[288,384]{1,0:T(8,128)(2,1)S(1)}, u32[]{:S(2)}, u32[]{:S(2)}) %collective-permute-start.2) | collective-permute-done | bytes 221216 | tf_op jit(solution)/shard_map/ppermute | solution.py:24
  118.7 4.1 %collective-permute-start.6 = (bf16[96,384]{1,0:T(8,128)(2,1)S(1)}, bf16[96,384]{1,0:T(8,128)(2,1)S(1)}, u32[]{:S(2)}, u32[]{:S(2)}) collective-permute-start(bf16[96,384]{1,0:T(8,128)(2,1)S(1)} %slice.14), channel_id=1, source_target_pairs={{0,224},{16,240},{32,0},{48,16},{64,32},{80,48},{96,64},{112,80},{... | collective-permute-start | bytes 221192 | tf_op jit(solution)/shard_map/ppermute | solution.py:24
  125.3 4.4 %collective-permute-start.23 = (bf16[4,512,384]{2,1,0:T(8,128)(2,1)S(1)}, bf16[4,512,384]{2,1,0:T(8,128)(2,1)}, u32[]{:S(2)}, u32[]{:S(2)}) collective-permute-start(bf16[4,512,384]{2,1,0:T(8,128)(2,1)S(1)} %pad_maximum_fusion.1.mine), channel_id=1, source_target_pairs={{0,2},{2,0},{1,3},{3,1},{4,6},{6,4},{5,7},{7,5},{8,10},{10,8},{9,1... | collective-permute-start | bytes 4718600 | tf_op jit(solution)/shard_map/ppermute | solution.py:36
  132.8 4.3 %collective-permute-start.5 = (bf16[288,384]{1,0:T(8,128)(2,1)S(1)}, bf16[288,384]{1,0:T(8,128)(2,1)}, u32[]{:S(2)}, u32[]{:S(2)}) collective-permute-start(bf16[288,384]{1,0:T(8,128)(2,1)S(1)} %collective-permute-done.3.refs_2_), channel_id=1, source_target_pairs={{0,240},{16,0},{32,16},{48,32},{64,48},{80,64},{96,80},{112,96},{1... | collective-permute-start | bytes 663560 | tf_op jit(solution)/shard_map/ppermute | solution.py:24
  137.9 3.7 %collective-permute-start.8 = (bf16[480,384]{1,0:T(8,128)(2,1)}, bf16[480,384]{1,0:T(8,128)(2,1)}, u32[]{:S(2)}, u32[]{:S(2)}) collective-permute-start(bf16[480,384]{1,0:T(8,128)(2,1)} %pad_maximum_fusion.4), channel_id=1, source_target_pairs={{0,257},{256,0},{1,256},{257,1},{2,259},{258,2},{3,258},{259,3},{4... | collective-permute-start | bytes 1105928 | tf_op jit(solution)/shard_map/ppermute | solution.py:32
  145.9 3.7 %collective-permute-start.10 = (bf16[288,384]{1,0:T(8,128)(2,1)}, bf16[288,384]{1,0:T(8,128)(2,1)}, u32[]{:S(2)}, u32[]{:S(2)}) collective-permute-start(bf16[288,384]{1,0:T(8,128)(2,1)} %collective-permute-done.5.refs_4_), channel_id=1, source_target_pairs={{0,257},{256,0},{1,256},{257,1},{2,259},{258,2},{3,258},{259,3},{4... | collective-permute-start | bytes 663560 | tf_op jit(solution)/shard_map/ppermute | solution.py:32
  160.7 14.7 %temporal.1 = bf16[512,128]{1,0:T(8,128)(2,1)S(1)} custom-call(bf16[288,384]{1,0:T(8,128)(2,1)S(1)} %copy-done.14, bf16[288,384]{1,0:T(8,128)(2,1)S(1)} %copy-done.7, bf16[288,384]{1,0:T(8,128)(2,1)S(1)} %copy-done.5, bf16[288,384]{1,0:T(8,128)(2,1)S(1)} %copy-done.9, bf16[288,384]{1,0:T(8,128)(2,1)} %collective-permute-done.5.refs_4_, ...), custom_call_target="tpu_custom_call" | custom-call | flops 1300000000 | bytes 6000000 | tf_op jit(solution)/shard_map/temporal/pallas_call | solution.py:214
  176.2 9.5 %all-to-all-start.1 = ((bf16[32,16,128]{2,1,0:T(8,128)(2,1)}), bf16[32,16,128]{2,1,0:T(8,128)(2,1)}, u32[]{:S(2)}, u32[]{:S(2)}) async-start(bf16[32,16,128]{2,1,0:T(8,128)(2,1)} %bitcast.77), calls=%async_computation.1 | async-start | bytes 262144 | tf_op jit(solution)/shard_map/all_to_all | solution.py:223
  188.7 11.3 %all-to-all-done.1 = bf16[32,16,128]{2,1,0:T(8,128)(2,1)} async-done(((bf16[32,16,128]{2,1,0:T(8,128)(2,1)}), bf16[32,16,128]{2,1,0:T(8,128)(2,1)}, u32[]{:S(2)}, u32[]{:S(2)}) %all-to-all-start.1) | async-done | bytes 131104 | tf_op jit(solution)/shard_map/all_to_all | solution.py:223
  200.1 6.9 %all-to-all-start.2 = ((bf16[8,256,384]{2,1,0:T(8,128)(2,1)}), bf16[8,256,384]{2,1,0:T(8,128)(2,1)S(1)}, u32[]{:S(2)}, u32[]{:S(2)}) async-start(bf16[8,256,384]{2,1,0:T(8,128)(2,1)} %bitcast.79), calls=%async_computation.2 | async-start | bytes 3145728 | tf_op jit(solution)/shard_map/all_to_all | solution.py:209
  210.8 17.9 %spatial.1 = bf16[512,128]{1,0:T(8,128)(2,1)S(1)} custom-call(bf16[3072,384]{1,0:T(8,128)(2,1)S(1)} %copy-done.1, s32[8]{0:T(128)S(1)} %copy-done.22, s32[1]{0:T(128)} %bitcast.53.yl, s32[8,4]{1,0:T(8,128)S(1)} %copy.10.window, bf16[4,512,384]{2,1,0:T(8,128)(2,1)S(1)} %pad_maximum_fusion.1.mine, bf16[4,512,384]{2,1,0:T(8,128)(2,1)} %collective-permute-done.23.theirs, ...), custom_call_target="tpu_custom_call" | custom-call | flops 1300000000 | bytes 6000000 | tf_op jit(solution)/shard_map/spatial/pallas_call | solution.py:227
  228.8 3.3 %collective-permute-start.24 = (bf16[512,128]{1,0:T(8,128)(2,1)S(1)}, bf16[512,128]{1,0:T(8,128)(2,1)S(1)}, u32[]{:S(2)}, u32[]{:S(2)}) collective-permute-start(bf16[512,128]{1,0:T(8,128)(2,1)S(1)} %spatial.1), channel_id=1, source_target_pairs={{0,4},{4,8},{8,12},{12,0},{1,5},{5,9},{9,13},{13,1},{2,6},{6,10},{... | collective-permute-start | bytes 393224 | tf_op jit(solution)/shard_map/ppermute | solution.py:28
  232.1 3.2 %collective-permute-start.25 = (bf16[512,128]{1,0:T(8,128)(2,1)S(1)}, bf16[512,128]{1,0:T(8,128)(2,1)S(1)}, u32[]{:S(2)}, u32[]{:S(2)}) collective-permute-start(bf16[512,128]{1,0:T(8,128)(2,1)S(1)} %spatial.1), channel_id=1, source_target_pairs={{0,12},{4,0},{8,4},{12,8},{1,13},{5,1},{9,5},{13,9},{2,14},{6,2},{... | collective-permute-start | bytes 393224 | tf_op jit(solution)/shard_map/ppermute | solution.py:28
  235.3 3.6 %collective-permute-start.26 = (bf16[512,128]{1,0:T(8,128)(2,1)S(1)}, bf16[512,128]{1,0:T(8,128)(2,1)S(1)}, u32[]{:S(2)}, u32[]{:S(2)}) collective-permute-start(bf16[512,128]{1,0:T(8,128)(2,1)S(1)} %spatial.1), channel_id=1, source_target_pairs={{0,8},{4,12},{8,0},{12,4},{1,9},{5,13},{9,1},{13,5},{2,10},{6,14},... | collective-permute-start | bytes 393224 | tf_op jit(solution)/shard_map/ppermute | solution.py:28
  241.1 4.3 %collective-permute-start.16 = (bf16[512,128]{1,0:T(8,128)(2,1)}, bf16[512,128]{1,0:T(8,128)(2,1)S(1)}, u32[]{:S(2)}, u32[]{:S(2)}) collective-permute-start(bf16[512,128]{1,0:T(8,128)(2,1)} %bitcast.48), channel_id=1, source_target_pairs={{0,12},{4,0},{8,4},{12,8},{1,13},{5,1},{9,5},{13,9},{2,14},{6,2},{... | collective-permute-start | bytes 393224 | tf_op jit(solution)/shard_map/ppermute | solution.py:28
  247.5 3.7 %collective-permute-start.27 = (bf16[4,512,128]{2,1,0:T(8,128)(2,1)S(1)}, bf16[4,512,128]{2,1,0:T(8,128)(2,1)S(1)}, u32[]{:S(2)}, u32[]{:S(2)}) collective-permute-start(bf16[4,512,128]{2,1,0:T(8,128)(2,1)S(1)} %pad_maximum_fusion.3.mine), channel_id=1, source_target_pairs={{0,2},{2,0},{1,3},{3,1},{4,6},{6,4},{5,7},{7,5},{8,10},{10,8},{9,1... | collective-permute-start | bytes 1572872 | tf_op jit(solution)/shard_map/ppermute | solution.py:36
  254.6 4.8 %collective-permute-start.18 = (bf16[4,512,128]{2,1,0:T(8,128)(2,1)}, bf16[4,512,128]{2,1,0:T(8,128)(2,1)}, u32[]{:S(2)}, u32[]{:S(2)}) collective-permute-start(bf16[4,512,128]{2,1,0:T(8,128)(2,1)} %pad_maximum_fusion.2.mine), channel_id=1, source_target_pairs={{0,2},{2,0},{1,3},{3,1},{4,6},{6,4},{5,7},{7,5},{8,10},{10,8},{9,1... | collective-permute-start | bytes 1572872 | tf_op jit(solution)/shard_map/ppermute | solution.py:36
  (112 shorter events, 58.5 us)
Async XLA Ops:
  6.5 42.1 %all-to-all-start = ((bf16[32,16,384]{2,1,0:T(8,128)(2,1)}), bf16[32,16,384]{2,1,0:T(8,128)(2,1)S(1)}, u32[]{:S(2)}, u32[]{:S(2)}) async-start(bf16[32,16,384]{2,1,0:T(8,128)(2,1)} %bitcast.75), calls=%async_computation | async-start | bytes 786432 | tf_op jit(solution)/shard_map/all_to_all | solution.py:176
  23.6 184.2 %all-gather.2.cloned.1.call-start = ((), (), s32[]{:S(2)}) async-start(), calls=%async_computation.3 | async-start | bytes 2506752 | tf_op jit(solution)/shard_map/all_gather | solution.py:174
  26.2 5.2 %collective-permute-start.19 = (bf16[96,384]{1,0:T(8,128)(2,1)S(1)}, bf16[96,384]{1,0:T(8,128)(2,1)S(1)}, u32[]{:S(2)}, u32[]{:S(2)}) collective-permute-start(bf16[96,384]{1,0:T(8,128)(2,1)S(1)} %bitcast.94), channel_id=1, source_target_pairs={{0,256},{256,0},{1,257},{257,1},{2,258},{258,2},{3,259},{259,3},{4... | collective-permute-start | bytes 221192 | tf_op jit(solution)/shard_map/ppermute | solution.py:173
  48.6 10.6 %collective-permute-start.11 = (bf16[512,384]{1,0:T(8,128)(2,1)S(1)}, bf16[512,384]{1,0:T(8,128)(2,1)S(1)}, u32[]{:S(2)}, u32[]{:S(2)}) collective-permute-start(bf16[512,384]{1,0:T(8,128)(2,1)S(1)} %bitcast.82), channel_id=1, source_target_pairs={{0,4},{4,8},{8,12},{12,0},{1,5},{5,9},{9,13},{13,1},{2,6},{6,10},{... | collective-permute-start | bytes 1179656 | tf_op jit(solution)/shard_map/ppermute | solution.py:28
  51.7 9.2 %collective-permute-start.12 = (bf16[512,384]{1,0:T(8,128)(2,1)S(1)}, bf16[512,384]{1,0:T(8,128)(2,1)S(1)}, u32[]{:S(2)}, u32[]{:S(2)}) collective-permute-start(bf16[512,384]{1,0:T(8,128)(2,1)S(1)} %bitcast.83), channel_id=1, source_target_pairs={{0,12},{4,0},{8,4},{12,8},{1,13},{5,1},{9,5},{13,9},{2,14},{6,2},{... | collective-permute-start | bytes 1179656 | tf_op jit(solution)/shard_map/ppermute | solution.py:28
  55.1 14.6 %collective-permute-start.13 = (bf16[512,384]{1,0:T(8,128)(2,1)S(1)}, bf16[512,384]{1,0:T(8,128)(2,1)S(1)}, u32[]{:S(2)}, u32[]{:S(2)}) collective-permute-start(bf16[512,384]{1,0:T(8,128)(2,1)S(1)} %bitcast.84), channel_id=1, source_target_pairs={{0,8},{4,12},{8,0},{12,4},{1,9},{5,13},{9,1},{13,5},{2,10},{6,14},... | collective-permute-start | bytes 1179656 | tf_op jit(solution)/shard_map/ppermute | solution.py:28
  70.0 83.8 %collective-permute-start.14 = (bf16[4,512,384]{2,1,0:T(8,128)(2,1)S(1)}, bf16[4,512,384]{2,1,0:T(8,128)(2,1)}, u32[]{:S(2)}, u32[]{:S(2)}) collective-permute-start(bf16[4,512,384]{2,1,0:T(8,128)(2,1)S(1)} %pad_maximum_fusion.refs_12_), channel_id=1, source_target_pairs={{0,2},{2,0},{1,3},{3,1},{4,6},{6,4},{5,7},{7,5},{8,10},{10,8},{9,1... | collective-permute-start | bytes 4718600 | tf_op jit(solution)/shard_map/ppermute | solution.py:36
  75.1 17.4 %collective-permute-start = (bf16[96,384]{1,0:T(8,128)(2,1)S(1)}, bf16[96,384]{1,0:T(8,128)(2,1)S(1)}, u32[]{:S(2)}, u32[]{:S(2)}) collective-permute-start(bf16[96,384]{1,0:T(8,128)(2,1)S(1)} %get-tuple-element.8), channel_id=1, source_target_pairs={{0,80},{16,96},{32,112},{48,128},{64,144},{80,160},{96,176},{112,1... | collective-permute-start | bytes 221192 | tf_op jit(solution)/shard_map/ppermute | solution.py:24
  80.9 15.8 %collective-permute-start.1 = (bf16[96,384]{1,0:T(8,128)(2,1)S(1)}, bf16[96,384]{1,0:T(8,128)(2,1)S(1)}, u32[]{:S(2)}, u32[]{:S(2)}) collective-permute-start(bf16[96,384]{1,0:T(8,128)(2,1)S(1)} %get-tuple-element.8), channel_id=1, source_target_pairs={{0,176},{16,192},{32,208},{48,224},{64,240},{80,0},{96,16},{112,32... | collective-permute-start | bytes 221192 | tf_op jit(solution)/shard_map/ppermute | solution.py:24
  96.7 12.5 %collective-permute-start.3 = (bf16[288,384]{1,0:T(8,128)(2,1)S(1)}, bf16[288,384]{1,0:T(8,128)(2,1)S(1)}, u32[]{:S(2)}, u32[]{:S(2)}) collective-permute-start(bf16[288,384]{1,0:T(8,128)(2,1)S(1)} %constant_dynamic-update-slice_fusion.refs_0_), channel_id=1, source_target_pairs={{0,240},{16,0},{32,16},{48,32},{64,48},{80,64},{96,80},{112,96},{1... | collective-permute-start | bytes 663560 | tf_op jit(solution)/shard_map/ppermute | solution.py:24
  98.7 24.1 %collective-permute-start.20 = (bf16[512,384]{1,0:T(8,128)(2,1)S(1)}, bf16[512,384]{1,0:T(8,128)(2,1)S(1)}, u32[]{:S(2)}, u32[]{:S(2)}) collective-permute-start(bf16[512,384]{1,0:T(8,128)(2,1)S(1)} %copy-done), channel_id=1, source_target_pairs={{0,4},{4,8},{8,12},{12,0},{1,5},{5,9},{9,13},{13,1},{2,6},{6,10},{... | collective-permute-start | bytes 1179656 | tf_op jit(solution)/shard_map/ppermute | solution.py:28
  102.6 22.4 %collective-permute-start.21 = (bf16[512,384]{1,0:T(8,128)(2,1)S(1)}, bf16[512,384]{1,0:T(8,128)(2,1)S(1)}, u32[]{:S(2)}, u32[]{:S(2)}) collective-permute-start(bf16[512,384]{1,0:T(8,128)(2,1)S(1)} %copy-done), channel_id=1, source_target_pairs={{0,12},{4,0},{8,4},{12,8},{1,13},{5,1},{9,5},{13,9},{2,14},{6,2},{... | collective-permute-start | bytes 1179656 | tf_op jit(solution)/shard_map/ppermute | solution.py:28
  106.1 18.9 %collective-permute-start.22 = (bf16[512,384]{1,0:T(8,128)(2,1)S(1)}, bf16[512,384]{1,0:T(8,128)(2,1)S(1)}, u32[]{:S(2)}, u32[]{:S(2)}) collective-permute-start(bf16[512,384]{1,0:T(8,128)(2,1)S(1)} %copy-done), channel_id=1, source_target_pairs={{0,8},{4,12},{8,0},{12,4},{1,9},{5,13},{9,1},{13,5},{2,10},{6,14},... | collective-permute-start | bytes 1179656 | tf_op jit(solution)/shard_map/ppermute | solution.py:28
  109.2 9.5 %collective-permute-start.2 = (bf16[288,384]{1,0:T(8,128)(2,1)S(1)}, bf16[288,384]{1,0:T(8,128)(2,1)S(1)}, u32[]{:S(2)}, u32[]{:S(2)}) collective-permute-start(bf16[288,384]{1,0:T(8,128)(2,1)S(1)} %constant_dynamic-update-slice_fusion.refs_0_), channel_id=1, source_target_pairs={{0,16},{16,32},{32,48},{48,64},{64,80},{80,96},{96,112},{112,128},... | collective-permute-start | bytes 663560 | tf_op jit(solution)/shard_map/ppermute | solution.py:24
  118.7 14.0 %collective-permute-start.6 = (bf16[96,384]{1,0:T(8,128)(2,1)S(1)}, bf16[96,384]{1,0:T(8,128)(2,1)S(1)}, u32[]{:S(2)}, u32[]{:S(2)}) collective-permute-start(bf16[96,384]{1,0:T(8,128)(2,1)S(1)} %slice.14), channel_id=1, source_target_pairs={{0,224},{16,240},{32,0},{48,16},{64,32},{80,48},{96,64},{112,80},{... | collective-permute-start | bytes 221192 | tf_op jit(solution)/shard_map/ppermute | solution.py:24
  122.8 15.1 %collective-permute-start.4 = (bf16[288,384]{1,0:T(8,128)(2,1)S(1)}, bf16[288,384]{1,0:T(8,128)(2,1)S(1)}, u32[]{:S(2)}, u32[]{:S(2)}) collective-permute-start(bf16[288,384]{1,0:T(8,128)(2,1)S(1)} %collective-permute-done.2.refs_1_), channel_id=1, source_target_pairs={{0,16},{16,32},{32,48},{48,64},{64,80},{80,96},{96,112},{112,128},... | collective-permute-start | bytes 663560 | tf_op jit(solution)/shard_map/ppermute | solution.py:24
  125.3 82.5 %collective-permute-start.23 = (bf16[4,512,384]{2,1,0:T(8,128)(2,1)S(1)}, bf16[4,512,384]{2,1,0:T(8,128)(2,1)}, u32[]{:S(2)}, u32[]{:S(2)}) collective-permute-start(bf16[4,512,384]{2,1,0:T(8,128)(2,1)S(1)} %pad_maximum_fusion.1.mine), channel_id=1, source_target_pairs={{0,2},{2,0},{1,3},{3,1},{4,6},{6,4},{5,7},{7,5},{8,10},{10,8},{9,1... | collective-permute-start | bytes 4718600 | tf_op jit(solution)/shard_map/ppermute | solution.py:36
  129.7 15.4 %collective-permute-start.7 = (bf16[384,384]{1,0:T(8,128)(2,1)S(1)}, bf16[384,384]{1,0:T(8,128)(2,1)S(1)}, u32[]{:S(2)}, u32[]{:S(2)}) collective-permute-start(bf16[384,384]{1,0:T(8,128)(2,1)S(1)} %pad_maximum_fusion.5), channel_id=1, source_target_pairs={{0,256},{256,1},{1,257},{257,0},{2,258},{258,3},{3,259},{259,2},{4... | collective-permute-start | bytes 884744 | tf_op jit(solution)/shard_map/ppermute | solution.py:32
  132.8 9.6 %collective-permute-start.5 = (bf16[288,384]{1,0:T(8,128)(2,1)S(1)}, bf16[288,384]{1,0:T(8,128)(2,1)}, u32[]{:S(2)}, u32[]{:S(2)}) collective-permute-start(bf16[288,384]{1,0:T(8,128)(2,1)S(1)} %collective-permute-done.3.refs_2_), channel_id=1, source_target_pairs={{0,240},{16,0},{32,16},{48,32},{64,48},{80,64},{96,80},{112,96},{1... | collective-permute-start | bytes 663560 | tf_op jit(solution)/shard_map/ppermute | solution.py:24
  137.9 14.8 %collective-permute-start.8 = (bf16[480,384]{1,0:T(8,128)(2,1)}, bf16[480,384]{1,0:T(8,128)(2,1)}, u32[]{:S(2)}, u32[]{:S(2)}) collective-permute-start(bf16[480,384]{1,0:T(8,128)(2,1)} %pad_maximum_fusion.4), channel_id=1, source_target_pairs={{0,257},{256,0},{1,256},{257,1},{2,259},{258,2},{3,258},{259,3},{4... | collective-permute-start | bytes 1105928 | tf_op jit(solution)/shard_map/ppermute | solution.py:32
  142.4 11.4 %collective-permute-start.9 = (bf16[384,384]{1,0:T(8,128)(2,1)}, bf16[384,384]{1,0:T(8,128)(2,1)}, u32[]{:S(2)}, u32[]{:S(2)}) collective-permute-start(bf16[384,384]{1,0:T(8,128)(2,1)} %pad_maximum_fusion.6), channel_id=1, source_target_pairs={{0,256},{256,1},{1,257},{257,0},{2,258},{258,3},{3,259},{259,2},{4... | collective-permute-start | bytes 884744 | tf_op jit(solution)/shard_map/ppermute | solution.py:32
  145.9 7.9 %collective-permute-start.10 = (bf16[288,384]{1,0:T(8,128)(2,1)}, bf16[288,384]{1,0:T(8,128)(2,1)}, u32[]{:S(2)}, u32[]{:S(2)}) collective-permute-start(bf16[288,384]{1,0:T(8,128)(2,1)} %collective-permute-done.5.refs_4_), channel_id=1, source_target_pairs={{0,257},{256,0},{1,256},{257,1},{2,259},{258,2},{3,258},{259,3},{4... | collective-permute-start | bytes 663560 | tf_op jit(solution)/shard_map/ppermute | solution.py:32
  176.2 23.9 %all-to-all-start.1 = ((bf16[32,16,128]{2,1,0:T(8,128)(2,1)}), bf16[32,16,128]{2,1,0:T(8,128)(2,1)}, u32[]{:S(2)}, u32[]{:S(2)}) async-start(bf16[32,16,128]{2,1,0:T(8,128)(2,1)} %bitcast.77), calls=%async_computation.1 | async-start | bytes 262144 | tf_op jit(solution)/shard_map/all_to_all | solution.py:223
  200.1 60.1 %all-to-all-start.2 = ((bf16[8,256,384]{2,1,0:T(8,128)(2,1)}), bf16[8,256,384]{2,1,0:T(8,128)(2,1)S(1)}, u32[]{:S(2)}, u32[]{:S(2)}) async-start(bf16[8,256,384]{2,1,0:T(8,128)(2,1)} %bitcast.79), calls=%async_computation.2 | async-start | bytes 3145728 | tf_op jit(solution)/shard_map/all_to_all | solution.py:209
  228.8 16.6 %collective-permute-start.24 = (bf16[512,128]{1,0:T(8,128)(2,1)S(1)}, bf16[512,128]{1,0:T(8,128)(2,1)S(1)}, u32[]{:S(2)}, u32[]{:S(2)}) collective-permute-start(bf16[512,128]{1,0:T(8,128)(2,1)S(1)} %spatial.1), channel_id=1, source_target_pairs={{0,4},{4,8},{8,12},{12,0},{1,5},{5,9},{9,13},{13,1},{2,6},{6,10},{... | collective-permute-start | bytes 393224 | tf_op jit(solution)/shard_map/ppermute | solution.py:28
  232.1 15.3 %collective-permute-start.25 = (bf16[512,128]{1,0:T(8,128)(2,1)S(1)}, bf16[512,128]{1,0:T(8,128)(2,1)S(1)}, u32[]{:S(2)}, u32[]{:S(2)}) collective-permute-start(bf16[512,128]{1,0:T(8,128)(2,1)S(1)} %spatial.1), channel_id=1, source_target_pairs={{0,12},{4,0},{8,4},{12,8},{1,13},{5,1},{9,5},{13,9},{2,14},{6,2},{... | collective-permute-start | bytes 393224 | tf_op jit(solution)/shard_map/ppermute | solution.py:28
  235.3 12.1 %collective-permute-start.26 = (bf16[512,128]{1,0:T(8,128)(2,1)S(1)}, bf16[512,128]{1,0:T(8,128)(2,1)S(1)}, u32[]{:S(2)}, u32[]{:S(2)}) collective-permute-start(bf16[512,128]{1,0:T(8,128)(2,1)S(1)} %spatial.1), channel_id=1, source_target_pairs={{0,8},{4,12},{8,0},{12,4},{1,9},{5,13},{9,1},{13,5},{2,10},{6,14},... | collective-permute-start | bytes 393224 | tf_op jit(solution)/shard_map/ppermute | solution.py:28
  238.9 12.3 %collective-permute-start.15 = (bf16[512,128]{1,0:T(8,128)(2,1)}, bf16[512,128]{1,0:T(8,128)(2,1)S(1)}, u32[]{:S(2)}, u32[]{:S(2)}) collective-permute-start(bf16[512,128]{1,0:T(8,128)(2,1)} %bitcast.48), channel_id=1, source_target_pairs={{0,4},{4,8},{8,12},{12,0},{1,5},{5,9},{9,13},{13,1},{2,6},{6,10},{... | collective-permute-start | bytes 393224 | tf_op jit(solution)/shard_map/ppermute | solution.py:28
  241.1 10.1 %collective-permute-start.16 = (bf16[512,128]{1,0:T(8,128)(2,1)}, bf16[512,128]{1,0:T(8,128)(2,1)S(1)}, u32[]{:S(2)}, u32[]{:S(2)}) collective-permute-start(bf16[512,128]{1,0:T(8,128)(2,1)} %bitcast.48), channel_id=1, source_target_pairs={{0,12},{4,0},{8,4},{12,8},{1,13},{5,1},{9,5},{13,9},{2,14},{6,2},{... | collective-permute-start | bytes 393224 | tf_op jit(solution)/shard_map/ppermute | solution.py:28
  245.4 7.4 %collective-permute-start.17 = (bf16[512,128]{1,0:T(8,128)(2,1)}, bf16[512,128]{1,0:T(8,128)(2,1)S(1)}, u32[]{:S(2)}, u32[]{:S(2)}) collective-permute-start(bf16[512,128]{1,0:T(8,128)(2,1)} %bitcast.48), channel_id=1, source_target_pairs={{0,8},{4,12},{8,0},{12,4},{1,9},{5,13},{9,1},{13,5},{2,10},{6,14},... | collective-permute-start | bytes 393224 | tf_op jit(solution)/shard_map/ppermute | solution.py:28
  247.5 12.7 %collective-permute-start.27 = (bf16[4,512,128]{2,1,0:T(8,128)(2,1)S(1)}, bf16[4,512,128]{2,1,0:T(8,128)(2,1)S(1)}, u32[]{:S(2)}, u32[]{:S(2)}) collective-permute-start(bf16[4,512,128]{2,1,0:T(8,128)(2,1)S(1)} %pad_maximum_fusion.3.mine), channel_id=1, source_target_pairs={{0,2},{2,0},{1,3},{3,1},{4,6},{6,4},{5,7},{7,5},{8,10},{10,8},{9,1... | collective-permute-start | bytes 1572872 | tf_op jit(solution)/shard_map/ppermute | solution.py:36
  254.6 10.0 %collective-permute-start.18 = (bf16[4,512,128]{2,1,0:T(8,128)(2,1)}, bf16[4,512,128]{2,1,0:T(8,128)(2,1)}, u32[]{:S(2)}, u32[]{:S(2)}) collective-permute-start(bf16[4,512,128]{2,1,0:T(8,128)(2,1)} %pad_maximum_fusion.2.mine), channel_id=1, source_target_pairs={{0,2},{2,0},{1,3},{3,1},{4,6},{6,4},{5,7},{7,5},{8,10},{10,8},{9,1... | collective-permute-start | bytes 1572872 | tf_op jit(solution)/shard_map/ppermute | solution.py:36
  (26 other events, 173.5 us)
Sparse Core Ops, SparseCore 0:
  32.2 76.8 all-gather.1

commit v2 on v1

v2 whole, which is shorter than its diff:
```python
import functools

import jax
import jax.numpy as jnp
from jax import lax
from jax.experimental import pallas as pl
from jax.experimental.pallas import tpu as pltpu
from jax.sharding import Mesh, PartitionSpec as P

D = 3072
HD = 128
TILE = 64
WIN = 4
F32 = jnp.float32
BF16 = jnp.bfloat16
VMEM = pl.BlockSpec(memory_space=pltpu.VMEM)
SMEM = pl.BlockSpec(memory_space=pltpu.SMEM)
HBM = pl.BlockSpec(memory_space=pl.ANY)
COLUMNS = pl.BlockSpec((8, 256, 384), lambda i: (0, 2, 0))
ROWS = pl.BlockSpec((256, 384), lambda i: (i, 0))
HEADS = pl.BlockSpec((2, 2, 256, HD), lambda i: (0, 0, i, 0))

Y_PLACE = (0, 2, 1, 3)


def along_z(value, step):
    return lax.ppermute(value, ("zh", "zl"), [(i, (i + step) % 16) for i in range(16)])


def along_x(value, step):
    return lax.ppermute(value, "x", [(i, (i + step) % 4) for i in range(4)])


def along_y(value, step):
    return lax.ppermute(value, ("yl", "dp"), [(Y_PLACE[i], Y_PLACE[(i + step) % 4]) for i in range(4)])


def tie(*values):
    return lax.optimization_barrier(values)


def norm_kernel(blocks_ref, shift, scale, normed):
    def rows_of(step, _):
        rows = pl.ds(pl.multiple_of(step * 16, 16), 16)
        blocks = [blocks_ref[j, rows, :].astype(F32) for j in range(8)]
        middle = jnp.sum(sum(blocks), -1, keepdims=True) * (1.0 / D)
        blocks = [block - middle for block in blocks]
        spread = jnp.sum(sum(block * block for block in blocks), -1, keepdims=True) * (1.0 / D)
        inverse = lax.rsqrt(spread + 1e-06)
        for j in range(8):
            value = blocks[j] * inverse * (1.0 + scale[pl.ds(j, 1), :]) + shift[pl.ds(j, 1), :]
            normed[rows, j * 384 : (j + 1) * 384] = value.astype(BF16)
        return 0

    lax.fori_loop(0, normed.shape[0] // 16, rows_of, 0, unroll=4)


def project(normed, weight, total, out):
    for step in range(4):
        part = weight[step * 2 : step * 2 + 2].reshape(768, 384)
        term = jnp.dot(normed[:, step * 768 : step * 768 + 768], part, preferred_element_type=F32)
        if step == 0:
            total[...] = term
        elif step < 3:
            total[...] += term
        else:
            out[...] = (total[...] + term).astype(BF16)


def softmax(scores):
    raised = jnp.exp(scores - jnp.max(scores, -1, keepdims=True))
    return (raised / jnp.sum(raised, -1, keepdims=True)).astype(BF16)


def scores_of(queries, keys):
    return lax.dot_general(queries, keys, (((1,), (1,)), ((), ())), preferred_element_type=F32) * float(HD) ** (-0.5)


def temporal_project_kernel(
    place, own, below, above, far_below, far_above, near_own, near_sides, near_far, normed, out, weight, total, sem
):
    here, there = place[0] * 4, (1 - place[0]) * 4
    pieces = (
        (own, here, 4, 0),
        (below, here, 4, 3),
        (above, here, 4, 1),
        (far_below, here, 2, 2),
        (far_above, here + 2, 2, 2),
        (near_own, there, 4, 0),
        (near_sides.at[0:4], there, 4, 3),
        (near_sides.at[4:8], there, 4, 1),
        (near_far, there, 4, 2),
    )
    copies = [
        pltpu.make_async_copy(piece, weight.at[pl.ds(start, count), (place[1] + ahead) % 4], sem.at[i])
        for i, (piece, start, count, ahead) in enumerate(pieces)
    ]
    for copy in copies:
        copy.start()
    for copy in copies:
        copy.wait()
    project(normed, weight, total, out)


def temporal_kernel(projected, out):
    def tile_of(step, _):
        rows = pl.ds(pl.multiple_of(step * 128, 128), 128)
        scores = scores_of(projected[rows, 0:128], projected[:, 128:256])
        at_row = lax.broadcasted_iota(jnp.int32, scores.shape, 0) % 16
        at_column = lax.broadcasted_iota(jnp.int32, scores.shape, 1) % 16
        weights = softmax(jnp.where(at_row == at_column, scores, -1e30))
        out[rows, :] = jnp.dot(weights, projected[:, 256:384], preferred_element_type=F32).astype(BF16)
        return 0

    lax.fori_loop(0, 4, tile_of, 0)


def spatial_kernel(gathered, place, window, normed, out, weight, total, projected, sem):
    copies = []
    for z in range(16):
        for half in range(2):
            start = (place[0] + half) % 2 * 4 + z // 4
            copies.append(
                pltpu.make_async_copy(gathered.at[z, pl.ds(half * 96, 96)], weight.at[start, z % 4], sem.at[z * 2 + half])
            )
            copies[-1].start()
    for copy in copies:
        copy.wait()
    project(normed, weight, total, projected)

    def tile_of(step, _):
        rows = pl.ds(pl.multiple_of(step * TILE, TILE), TILE)
        chosen = [pl.ds(pl.multiple_of(window[step, i] * TILE, TILE), TILE) for i in range(WIN)]
        keys = jnp.concatenate([projected[there, 128:256] for there in chosen], 0)
        values = jnp.concatenate([projected[there, 256:384] for there in chosen], 0)
        weights = softmax(scores_of(projected[rows, 0:128], keys))
        out[rows, :] = jnp.dot(weights, values, preferred_element_type=F32).astype(BF16)
        return 0

    lax.fori_loop(0, 8, tile_of, 0)


def rows_of_kind(w_out, kind):
    return jnp.concatenate([w_out[g, kind * HD : (kind + 1) * HD, :] for g in range(8)], 0)


def share_kernel(heads, w_out, share):
    wide = jnp.concatenate([heads[g] for g in range(8)], 1)
    share[...] = jnp.dot(wide, rows_of_kind(w_out, 0), preferred_element_type=F32)


def mixed_kernel(low, high, w_out, share, hidden, gate, out):
    wide = jnp.concatenate([(low if x < 2 else high)[side, x % 2] for x in range(4) for side in range(2)], 1)
    total = jnp.dot(wide, rows_of_kind(w_out, 1), preferred_element_type=F32)
    out[...] = (hidden[...].astype(F32) + gate[...] * (total + share[...])).astype(BF16)


def params(flops, size):
    return dict(
        compiler_params=pltpu.CompilerParams(vmem_limit_bytes=56 * 1024 * 1024),
        cost_estimate=pl.CostEstimate(flops=flops, bytes_accessed=size, transcendentals=0),
    )


def body(hidden, shift_mod, scale_mod, gate, w_qkv, w_out, window_tiles):
    x, core, zl, yl = (lax.axis_index(name) for name in ("x", "c", "zl", "yl"))
    place = jnp.stack([yl, zl]).astype(jnp.int32)
    shift, scale = shift_mod.reshape(8, 384), scale_mod.reshape(8, 384)

    w_temporal = w_qkv[:, :, 1].reshape(96, 384)
    w_spatial = w_qkv[:, :, 0].reshape(96, 384)
    hidden_now, w_spatial = tie(hidden, w_spatial)

    pair = jnp.concatenate([w_spatial, lax.ppermute(w_spatial, "yl", [(0, 1), (1, 0)])], 0)
    gathered = lax.all_gather(pair, ("zh", "zl"), axis=0)

    sent = jnp.concatenate(
        [jnp.broadcast_to(hidden_now[None], (8, 512, 384)), w_out.reshape(256, 8, 384).transpose(1, 0, 2)], 1
    )
    arrived = lax.all_to_all(sent, ("x", "c"), split_axis=0, concat_axis=0, tiled=True)

    own = lax.all_gather(w_temporal, "zh", axis=0)
    below, above = along_z(own, 1), along_z(own, -1)
    far_below, far_above = along_z(own[:2], 2), along_z(own[2:], -2)
    near_own = along_y(own, 1)
    near_sides = along_y(jnp.concatenate([below, above], 0), -1)
    near_far = along_y(jnp.concatenate([far_below, far_above], 0), 1)

    normed = pl.pallas_call(
        norm_kernel,
        out_shape=jax.ShapeDtypeStruct((512, D), BF16),
        grid=(8,),
        in_specs=[
            pl.BlockSpec((8, 64, 384), lambda i: (0, i, 0)),
            pl.BlockSpec((8, 384), lambda i: (0, 0)),
            pl.BlockSpec((8, 384), lambda i: (0, 0)),
        ],
        out_specs=pl.BlockSpec((64, D), lambda i: (i, 0)),
        name="norm",
        **params(20_000_000, 6_000_000),
    )(arrived, shift, scale)

    projected = pl.pallas_call(
        temporal_project_kernel,
        out_shape=jax.ShapeDtypeStruct((512, 384), BF16),
        in_specs=[SMEM] + [HBM] * 8 + [VMEM],
        out_specs=VMEM,
        scratch_shapes=[pltpu.VMEM((8, 4, 96, 384), BF16), pltpu.VMEM((512, 384), F32), pltpu.SemaphoreType.DMA((9,))],
        name="temporal_project",
        **params(1_200_000_000, 6_000_000),
    )(place, own, below, above, far_below, far_above, near_own, near_sides, near_far, normed)
    by_position = lax.all_to_all(
        projected.reshape(32, 16, 384), ("yl", "zh", "zl"), split_axis=0, concat_axis=0, tiled=True
    ).reshape(512, 384)

    spatial = pl.pallas_call(
        spatial_kernel,
        out_shape=jax.ShapeDtypeStruct((512, HD), BF16),
        in_specs=[HBM, SMEM, SMEM, VMEM],
        out_specs=VMEM,
        scratch_shapes=[
            pltpu.VMEM((8, 4, 96, 384), BF16),
            pltpu.VMEM((512, 384), F32),
            pltpu.VMEM((512, 384), BF16),
            pltpu.SemaphoreType.DMA((32,)),
        ],
        name="spatial",
        **params(1_300_000_000, 6_000_000),
    )(gathered, place, window_tiles, normed)
    by_position, spatial = tie(by_position, spatial)
    spatial_heads = lax.all_gather(spatial, ("x", "c"), axis=0)

    temporal = pl.pallas_call(
        temporal_kernel,
        out_shape=jax.ShapeDtypeStruct((512, HD), BF16),
        in_specs=[VMEM],
        out_specs=VMEM,
        name="temporal",
        **params(140_000_000, 500_000),
    )(by_position)
    temporal = lax.all_to_all(
        temporal.reshape(32, 16, HD), ("yl", "zh", "zl"), split_axis=0, concat_axis=0, tiled=True
    ).reshape(512, HD)
    line = lax.all_gather(temporal, "x", axis=0)
    low, high = lax.all_gather(line[:2], "c", axis=0), lax.all_gather(line[2:], "c", axis=0)
    gate_here = lax.dynamic_slice_in_dim(gate, (x * 2 + core) * 384, 384).reshape(1, 384)
    share = pl.pallas_call(
        share_kernel,
        out_shape=jax.ShapeDtypeStruct((512, 384), F32),
        grid=(2,),
        in_specs=[pl.BlockSpec((8, 256, HD), lambda i: (0, i, 0)), COLUMNS],
        out_specs=ROWS,
        name="spatial_share",
        **params(400_000_000, 3_000_000),
    )(spatial_heads, arrived)
    return pl.pallas_call(
        mixed_kernel,
        out_shape=jax.ShapeDtypeStruct((512, 384), BF16),
        grid=(2,),
        in_specs=[HEADS, HEADS, COLUMNS, ROWS, ROWS, pl.BlockSpec((1, 384), lambda i: (0, 0))],
        out_specs=ROWS,
        name="mixed",
        **params(400_000_000, 4_000_000),
    )(low, high, arrived, share, hidden, gate_here)


def solution(mesh):
    fine = Mesh(mesh.devices.reshape(2, 4, 4, 4, 2, 2), ("yl", "zh", "zl", "x", "c", "dp"))
    seq, tp = ("yl", "zh", "zl"), ("x", "c")
    in_specs = (
        P(("dp",) + seq, tp),
        P("dp"),
        P("dp"),
        P("dp"),
        P(seq, None, None, tp),
        P(None, tp, None),
        P(),
    )
    out_specs = P(("dp",) + seq, tp)
    return jax.shard_map(body, mesh=fine, in_specs=in_specs, out_specs=out_specs, check_vma=False)
```

time: 276 us -> 195 us (0.71)
  starting transfers between devices: 134 us -> 50.4 us
  blocking collectives: 0 us -> 45.9 us
  waiting for transfers between devices: 59.5 us -> 36.4 us
  local copies, waits for them, and re-layouts: 25 us -> 9.8 us
  Pallas kernels: 37.2 us -> 33.5 us
    ppermute x23 -> x4, starting transfers between devices: 84.2 us -> 13.9 us  [along_z(): lax.ppermute(value, ('zh', 'zl'), [(i, (i + step) % 16) for i in range(16)])]
    all_gather x0 -> x4, blocking collectives: none -> 45.9 us  [the longest x1 19.4 us: body(): own = lax.all_gather(w_temporal, 'zh', axis=0)]
    ppermute x23 -> x4, waiting for transfers between devices: 28.5 us -> 10.5 us  [along_z(): lax.ppermute(value, ('zh', 'zl'), [(i, (i + step) % 16) for i in range(16)])]
    unnamed x57 -> x29, local copies, waits for them, and re-layouts: 17.4 us -> 4.74 us
    pallas_call x1, Pallas kernels: 17.9 us -> 9.95 us  [body(): pl.pallas_call(spatial_kernel, out_shape=jax.ShapeDtypeStruct((512, HD),...]
    all_to_all x3, starting transfers between devices: 33.5 us -> 25.6 us  [the longest x1 11.5 us: body(): lax.all_to_all(sent, ('x', 'c'), split_axis=0, concat_axis=0, tiled=True)]
    all_to_all x3, waiting for transfers between devices: 27.9 us -> 21.5 us  [the longest x1 13.1 us: body(): lax.all_to_all(temporal.reshape(32, 16, HD), ('yl', 'zh', 'zl'), split_ax...]
    pallas_call x3 -> x5, Pallas kernels: 19.2 us -> 23.5 us  [the longest x1 7.19 us: body(): pl.pallas_call(norm_kernel, out_shape=jax.ShapeDtypeStruct((512, D), BF16...]
  transfers between devices with their start and end apart: 32 -> 13, of which waited for: 11 -> 8; matrix products, arithmetic and copies ran while one was open for 5% -> 2% of each run, Pallas kernels for 12% -> 14%
where the time goes in v2:
time: 195 us; the launch traced here: 194 us
  starting transfers between devices  50.4 us (26%)
  blocking collectives  45.9 us (24%)
  waiting for transfers between devices  36.4 us (19%)
  Pallas kernels  33.5 us (17%)
  between operations  13.6 us (7%)
  local copies, waits for them, and re-layouts  9.8 us (5%)
  other arithmetic  4.01 us (2%)
    all_gather x1, blocking collectives, body(): own = lax.all_gather(w_temporal, 'zh', axis=0)  19.4 us
    ppermute x4, starting transfers between devices, along_z(): lax.ppermute(value, ('zh', 'zl'), [(i, (i + step) % 16) for i in range(16)])  13.9 us
    all_to_all x1, waiting for transfers between devices, body(): lax.all_to_all(temporal.reshape(32, 16, HD), ('yl', 'zh', 'zl'), split_ax...  13.1 us
    all_gather x1, blocking collectives, body(): lax.all_gather(line[:2], 'c', axis=0)  12.4 us
    all_gather x1, blocking collectives, body(): line = lax.all_gather(temporal, 'x', axis=0)  11.8 us
    all_to_all x1, starting transfers between devices, body(): lax.all_to_all(sent, ('x', 'c'), split_axis=0, concat_axis=0, tiled=True)  11.5 us
    ppermute x4, waiting for transfers between devices, along_z(): lax.ppermute(value, ('zh', 'zl'), [(i, (i + step) % 16) for i in range(16)])  10.5 us
    pallas_call x1, Pallas kernels, body(): pl.pallas_call(spatial_kernel, out_shape=jax.ShapeDtypeStruct((512, HD),...  9.95 us
  transfers between devices with their start and end apart: 13, of which 8 were waited for; matrix products, arithmetic and copies ran while one was open for 2% of the time, Pallas kernels for 14%

profile of v2, /device:TPU:1, one launch (start us, length us, event | category | flops | bytes accessed | tf_op | source)
XLA Modules:
  0.0 193.6 jit_solution(9927323384968592713)
XLA Ops:
  6.5 1.9 slice_reduce_fusion
  8.5 1.7 copy.14
  10.7 2.7 %pad_maximum_fusion = bf16[8,768,384]{2,1,0:T(8,128)(2,1)} fusion(bf16[8,256,384]{2,1,0:T(8,128)(2,1)S(1)} %bitcast.20, bf16[8,512,384]{2,1,0:T(8,128)(2,1)S(1)} %broadcast_in_dim.2), kind=kLoop, calls=%fused_computation | loop fusion | flops 9437184 | bytes 9437184 | tf_op jit(solution)/shard_map/concatenate | solution.py:177
  13.4 11.5 %all-to-all-start = ((bf16[8,768,384]{2,1,0:T(8,128)(2,1)}), bf16[8,768,384]{2,1,0:T(8,128)(2,1)}, u32[]{:S(2)}, u32[]{:S(2)}) async-start(bf16[8,768,384]{2,1,0:T(8,128)(2,1)} %pad_maximum_fusion), calls=%async_computation | async-start | bytes 9437184 | tf_op jit(solution)/shard_map/all_to_all | solution.py:180
  24.9 1.9 collective-permute-start.7
  26.8 3.8 %collective-permute-done.7 = bf16[96,384]{1,0:T(8,128)(2,1)S(1)} collective-permute-done((bf16[96,384]{1,0:T(8,128)(2,1)S(1)}, bf16[96,384]{1,0:T(8,128)(2,1)S(1)}, u32[]{:S(2)}, u32[]{:S(2)}) %collective-permute-start.7) | collective-permute-done | bytes 73760 | tf_op jit(solution)/shard_map/ppermute | solution.py:174
  31.3 19.4 %all_gather.30.own = bf16[4,96,384]{2,1,0:T(8,128)(2,1)S(1)} all-gather(bf16[1,96,384]{2,1,0:T(8,128)(2,1)S(1)} %all_gather_reshape_squeeze.3), channel_id=1, replica_groups=mesh['yl'=2,'zh'=4,'zl'=4,'x'=4,'c'=2,'dp'=2] {'zh'}, dimensions={0}, use_global_device_ids=true | all-gather | bytes 368640 | tf_op jit(solution)/shard_map/all_gather | solution.py:182
  50.7 2.5 %collective-permute-start = (bf16[4,96,384]{2,1,0:T(8,128)(2,1)S(1)}, bf16[4,96,384]{2,1,0:T(8,128)(2,1)S(1)}, u32[]{:S(2)}, u32[]{:S(2)}) collective-permute-start(bf16[4,96,384]{2,1,0:T(8,128)(2,1)S(1)} %all_gather.30.own), channel_id=1, source_target_pairs={{0,16},{16,32},{32,48},{48,64},{64,80},{80,96},{96,112},{112,128},... | collective-permute-start | bytes 884744 | tf_op jit(solution)/shard_map/ppermute | solution.py:27
  53.2 4.0 %collective-permute-start.1 = (bf16[4,96,384]{2,1,0:T(8,128)(2,1)S(1)}, bf16[4,96,384]{2,1,0:T(8,128)(2,1)S(1)}, u32[]{:S(2)}, u32[]{:S(2)}) collective-permute-start(bf16[4,96,384]{2,1,0:T(8,128)(2,1)S(1)} %all_gather.30.own), channel_id=1, source_target_pairs={{0,240},{16,0},{32,16},{48,32},{64,48},{80,64},{96,80},{112,96},{1... | collective-permute-start | bytes 884744 | tf_op jit(solution)/shard_map/ppermute | solution.py:27
  57.2 6.9 %collective-permute-done.below = bf16[4,96,384]{2,1,0:T(8,128)(2,1)S(1)} collective-permute-done((bf16[4,96,384]{2,1,0:T(8,128)(2,1)S(1)}, bf16[4,96,384]{2,1,0:T(8,128)(2,1)S(1)}, u32[]{:S(2)}, u32[]{:S(2)}) %collective-permute-start) | collective-permute-done | bytes 294944 | tf_op jit(solution)/shard_map/ppermute | solution.py:27
  64.5 5.1 %collective-permute-start.5 = (bf16[8,96,384]{2,1,0:T(8,128)(2,1)S(1)}, bf16[8,96,384]{2,1,0:T(8,128)(2,1)S(1)}, u32[]{:S(2)}, u32[]{:S(2)}) collective-permute-start(bf16[8,96,384]{2,1,0:T(8,128)(2,1)S(1)} %pad_maximum_fusion.1), channel_id=1, source_target_pairs={{0,257},{256,0},{1,256},{257,1},{2,259},{258,2},{3,258},{259,3},{4... | collective-permute-start | bytes 1769480 | tf_op jit(solution)/shard_map/ppermute | solution.py:35
  69.7 1.9 collective-permute-start.2
  71.6 5.5 %collective-permute-start.3 = (bf16[2,96,384]{2,1,0:T(8,128)(2,1)S(1)}, bf16[2,96,384]{2,1,0:T(8,128)(2,1)S(1)}, u32[]{:S(2)}, u32[]{:S(2)}) collective-permute-start(bf16[2,96,384]{2,1,0:T(8,128)(2,1)S(1)} %get-tuple-element.17), channel_id=1, source_target_pairs={{0,224},{16,240},{32,0},{48,16},{64,32},{80,48},{96,64},{112,80},{... | collective-permute-start | bytes 442376 | tf_op jit(solution)/shard_map/ppermute | solution.py:27
  77.1 1.9 collective-permute-start.4
  79.1 0.8 collective-permute-done.2.far_below
  79.9 2.4 %collective-permute-done.3.far_above = bf16[2,96,384]{2,1,0:T(8,128)(2,1)S(1)} collective-permute-done((bf16[2,96,384]{2,1,0:T(8,128)(2,1)S(1)}, bf16[2,96,384]{2,1,0:T(8,128)(2,1)S(1)}, u32[]{:S(2)}, u32[]{:S(2)}) %collective-permute-start.3) | collective-permute-done | bytes 147488 | tf_op jit(solution)/shard_map/ppermute | solution.py:27
  82.3 1.9 collective-permute-start.6
  86.0 7.2 %norm.1.normed = bf16[512,3072]{1,0:T(8,128)(2,1)} custom-call(bf16[8,768,384]{2,1,0:T(8,128)(2,1)} %all-to-all-done.blocks_ref.w_out, f32[8,384]{1,0:T(8,128)} %reshape.23.shift, f32[8,384]{1,0:T(8,128)} %reshape.24.scale), custom_call_target="tpu_custom_call" | custom-call | flops 20000000 | bytes 6000000 | tf_op jit(solution)/shard_map/norm/pallas_call | solution.py:189
  94.6 0.9 copy-done.5
  95.5 6.1 %temporal_project.1 = bf16[512,384]{1,0:T(8,128)(2,1)} custom-call(s32[2]{0:T(128)} %pad_add_fusion.place, bf16[4,96,384]{2,1,0:T(8,128)(2,1)} %copy-done, bf16[4,96,384]{2,1,0:T(8,128)(2,1)} %copy-done.3, bf16[4,96,384]{2,1,0:T(8,128)(2,1)} %copy-done.4, bf16[2,96,384]{2,1,0:T(8,128)(2,1)} %copy-done.6, bf16[2,96,384]{2,1,0:T(8,128)(2,1)} %copy-done.7, ...), custom_call_target="tpu_custom_call" | custom-call | flops 1200000000 | bytes 6000000 | tf_op jit(solution)/shard_map/temporal_project/pallas_call | solution.py:203
  101.6 8.9 %all-to-all-start.1 = ((bf16[32,16,384]{2,1,0:T(8,128)(2,1)}), bf16[32,16,384]{2,1,0:T(8,128)(2,1)S(1)}, u32[]{:S(2)}, u32[]{:S(2)}) async-start(bf16[32,16,384]{2,1,0:T(8,128)(2,1)} %bitcast.27), calls=%async_computation.1 | async-start | bytes 786432 | tf_op jit(solution)/shard_map/all_to_all | solution.py:212
  111.3 10.0 %spatial.1 = bf16[512,128]{1,0:T(8,128)(2,1)} custom-call(bf16[16,192,384]{2,1,0:T(8,128)(2,1)} %bitcast.22, s32[2]{0:T(128)} %pad_add_fusion.place, s32[8,4]{1,0:T(8,128)} %copy.12.window, bf16[512,3072]{1,0:T(8,128)(2,1)} %norm.1.normed), custom_call_target="tpu_custom_call" | custom-call | flops 1300000000 | bytes 6000000 | tf_op jit(solution)/shard_map/spatial/pallas_call | solution.py:216
  121.2 8.4 %all-to-all-done.1 = bf16[32,16,384]{2,1,0:T(8,128)(2,1)S(1)} async-done(((bf16[32,16,384]{2,1,0:T(8,128)(2,1)}), bf16[32,16,384]{2,1,0:T(8,128)(2,1)S(1)}, u32[]{:S(2)}, u32[]{:S(2)}) %all-to-all-start.1) | async-done | bytes 393248 | tf_op jit(solution)/shard_map/all_to_all | solution.py:212
  130.4 3.6 %temporal.1 = bf16[512,128]{1,0:T(8,128)(2,1)} custom-call(bf16[512,384]{1,0:T(8,128)(2,1)} %bitcast.26), custom_call_target="tpu_custom_call" | custom-call | flops 140000000 | bytes 500000 | tf_op jit(solution)/shard_map/temporal/pallas_call | solution.py:233
  134.0 5.2 %all-to-all-start.2 = ((bf16[32,16,128]{2,1,0:T(8,128)(2,1)}), bf16[32,16,128]{2,1,0:T(8,128)(2,1)S(1)}, u32[]{:S(2)}, u32[]{:S(2)}) async-start(bf16[32,16,128]{2,1,0:T(8,128)(2,1)} %bitcast.30), calls=%async_computation.2 | async-start | bytes 262144 | tf_op jit(solution)/shard_map/all_to_all | solution.py:241
  139.2 0.8 dynamic_slice.3
  140.6 13.1 %all-to-all-done.2 = bf16[32,16,128]{2,1,0:T(8,128)(2,1)S(1)} async-done(((bf16[32,16,128]{2,1,0:T(8,128)(2,1)}), bf16[32,16,128]{2,1,0:T(8,128)(2,1)S(1)}, u32[]{:S(2)}, u32[]{:S(2)}) %all-to-all-start.2) | async-done | bytes 131104 | tf_op jit(solution)/shard_map/all_to_all | solution.py:241
  153.6 11.8 %all_gather.33 = bf16[4,512,128]{2,1,0:T(8,128)(2,1)S(1)} all-gather(bf16[1,512,128]{2,1,0:T(8,128)(2,1)S(1)} %bitcast.29), channel_id=1, replica_groups=mesh['yl'=2,'zh'=4,'zl'=4,'x'=4,'c'=2,'dp'=2] {'x'}, dimensions={0}, use_global_device_ids=true | all-gather | bytes 655360 | tf_op jit(solution)/shard_map/all_gather | solution.py:244
  165.5 12.4 %all-gather.1 = bf16[4,512,128]{2,1,0:T(8,128)(2,1)} all-gather(bf16[2,512,128]{2,1,0:T(8,128)(2,1)S(1)} %get-tuple-element.16), channel_id=3, replica_groups=mesh['yl'=2,'zh'=4,'zl'=4,'x'=4,'c'=2,'dp'=2] {'c'}, dimensions={0}, use_global_device_ids=true | all-gather | bytes 786432 | tf_op jit(solution)/shard_map/all_gather | solution.py:245
  177.9 2.3 %all-gather.2 = bf16[4,512,128]{2,1,0:T(8,128)(2,1)} all-gather(bf16[2,512,128]{2,1,0:T(8,128)(2,1)S(1)} %get-tuple-element.15), channel_id=4, replica_groups=mesh['yl'=2,'zh'=4,'zl'=4,'x'=4,'c'=2,'dp'=2] {'c'}, dimensions={0}, use_global_device_ids=true | all-gather | bytes 786432 | tf_op jit(solution)/shard_map/all_gather | solution.py:245
  180.2 3.2 %spatial_share.1.share = f32[512,384]{1,0:T(8,128)} custom-call(bf16[8,512,128]{2,1,0:T(8,128)(2,1)} %bitcast.28, bf16[8,768,384]{2,1,0:T(8,128)(2,1)} %all-to-all-done.blocks_ref.w_out), custom_call_target="tpu_custom_call" | custom-call | flops 400000000 | bytes 3000000 | tf_op jit(solution)/shard_map/spatial_share/pallas_call | solution.py:247
  183.4 3.4 %mixed.1 = bf16[512,384]{1,0:T(8,128)(2,1)} custom-call(bf16[2,2,512,128]{3,2,1,0:T(8,128)(2,1)} %bitcast.23, bf16[2,2,512,128]{3,2,1,0:T(8,128)(2,1)} %bitcast.24, bf16[8,768,384]{2,1,0:T(8,128)(2,1)} %all-to-all-done.blocks_ref.w_out, f32[512,384]{1,0:T(8,128)} %spatial_share.1.share, bf16[512,384]{1,0:T(8,128)(2,1)} %hidden.1, f32[1,384]{1,0:T(1,128)} %reshape.28.gate), custom_call_target="tpu_custom_call" | custom-call | flops 400000000 | bytes 4000000 | tf_op jit(solution)/shard_map/mixed/pallas_call | solution.py:256
  (50 shorter events, 7.0 us)
Async XLA Ops:
  6.5 3.9 %copy-start.2 = (bf16[512,384]{1,0:T(8,128)(2,1)S(1)}, bf16[512,384]{1,0:T(8,128)(2,1)}, u32[]{:S(2)}) copy-start(bf16[512,384]{1,0:T(8,128)(2,1)} %hidden.1) | copy-start | bytes 1179652
  13.4 70.9 %copy-start.10 = (f32[3072]{0:T(1024)S(1)}, f32[3072]{0:T(1024)}, u32[]{:S(2)}) copy-start(f32[3072]{0:T(1024)} %param.8) | copy-start | bytes 36868
  13.4 71.5 %copy-start.11 = (f32[3072]{0:T(1024)S(1)}, f32[3072]{0:T(1024)}, u32[]{:S(2)}) copy-start(f32[3072]{0:T(1024)} %param.9) | copy-start | bytes 36868
  13.4 72.6 %all-to-all-start = ((bf16[8,768,384]{2,1,0:T(8,128)(2,1)}), bf16[8,768,384]{2,1,0:T(8,128)(2,1)}, u32[]{:S(2)}, u32[]{:S(2)}) async-start(bf16[8,768,384]{2,1,0:T(8,128)(2,1)} %pad_maximum_fusion), calls=%async_computation | async-start | bytes 9437184 | tf_op jit(solution)/shard_map/all_to_all | solution.py:180
  24.9 86.4 %all-gather.7.cloned.1.call-start = ((), (), s32[]{:S(2)}) async-start(), calls=%async_computation.3 | async-start | bytes 2506752 | tf_op jit(solution)/shard_map/all_gather | solution.py:175
  24.9 5.7 %collective-permute-start.7 = (bf16[96,384]{1,0:T(8,128)(2,1)S(1)}, bf16[96,384]{1,0:T(8,128)(2,1)S(1)}, u32[]{:S(2)}, u32[]{:S(2)}) collective-permute-start(bf16[96,384]{1,0:T(8,128)(2,1)S(1)} %bitcast.32), channel_id=1, source_target_pairs={{0,256},{256,0},{1,257},{257,1},{2,258},{258,2},{3,259},{259,3},{4... | collective-permute-start | bytes 221192 | tf_op jit(solution)/shard_map/ppermute | solution.py:174
  50.7 42.5 %copy-start = (bf16[4,96,384]{2,1,0:T(8,128)(2,1)}, bf16[4,96,384]{2,1,0:T(8,128)(2,1)S(1)}, u32[]{:S(2)}) copy-start(bf16[4,96,384]{2,1,0:T(8,128)(2,1)S(1)} %all_gather.30.own) | copy-start | bytes 884740
  50.7 13.4 %collective-permute-start = (bf16[4,96,384]{2,1,0:T(8,128)(2,1)S(1)}, bf16[4,96,384]{2,1,0:T(8,128)(2,1)S(1)}, u32[]{:S(2)}, u32[]{:S(2)}) collective-permute-start(bf16[4,96,384]{2,1,0:T(8,128)(2,1)S(1)} %all_gather.30.own), channel_id=1, source_target_pairs={{0,16},{16,32},{32,48},{48,64},{64,80},{80,96},{96,112},{112,128},... | collective-permute-start | bytes 884744 | tf_op jit(solution)/shard_map/ppermute | solution.py:27
  53.2 11.3 %collective-permute-start.1 = (bf16[4,96,384]{2,1,0:T(8,128)(2,1)S(1)}, bf16[4,96,384]{2,1,0:T(8,128)(2,1)S(1)}, u32[]{:S(2)}, u32[]{:S(2)}) collective-permute-start(bf16[4,96,384]{2,1,0:T(8,128)(2,1)S(1)} %all_gather.30.own), channel_id=1, source_target_pairs={{0,240},{16,0},{32,16},{48,32},{64,48},{80,64},{96,80},{112,96},{1... | collective-permute-start | bytes 884744 | tf_op jit(solution)/shard_map/ppermute | solution.py:27
  64.0 29.2 %copy-start.3 = (bf16[4,96,384]{2,1,0:T(8,128)(2,1)}, bf16[4,96,384]{2,1,0:T(8,128)(2,1)S(1)}, u32[]{:S(2)}) copy-start(bf16[4,96,384]{2,1,0:T(8,128)(2,1)S(1)} %collective-permute-done.below) | copy-start | bytes 884740
  64.5 28.7 %copy-start.4 = (bf16[4,96,384]{2,1,0:T(8,128)(2,1)}, bf16[4,96,384]{2,1,0:T(8,128)(2,1)S(1)}, u32[]{:S(2)}) copy-start(bf16[4,96,384]{2,1,0:T(8,128)(2,1)S(1)} %collective-permute-done.1.above) | copy-start | bytes 884740
  64.5 29.3 %collective-permute-start.5 = (bf16[8,96,384]{2,1,0:T(8,128)(2,1)S(1)}, bf16[8,96,384]{2,1,0:T(8,128)(2,1)S(1)}, u32[]{:S(2)}, u32[]{:S(2)}) collective-permute-start(bf16[8,96,384]{2,1,0:T(8,128)(2,1)S(1)} %pad_maximum_fusion.1), channel_id=1, source_target_pairs={{0,257},{256,0},{1,256},{257,1},{2,259},{258,2},{3,258},{259,3},{4... | collective-permute-start | bytes 1769480 | tf_op jit(solution)/shard_map/ppermute | solution.py:35
  69.7 10.2 %collective-permute-start.2 = (bf16[2,96,384]{2,1,0:T(8,128)(2,1)S(1)}, bf16[2,96,384]{2,1,0:T(8,128)(2,1)S(1)}, u32[]{:S(2)}, u32[]{:S(2)}) collective-permute-start(bf16[2,96,384]{2,1,0:T(8,128)(2,1)S(1)} %get-tuple-element.18), channel_id=1, source_target_pairs={{0,32},{16,48},{32,64},{48,80},{64,96},{80,112},{96,128},{112,144}... | collective-permute-start | bytes 442376 | tf_op jit(solution)/shard_map/ppermute | solution.py:27
  71.6 10.6 %collective-permute-start.3 = (bf16[2,96,384]{2,1,0:T(8,128)(2,1)S(1)}, bf16[2,96,384]{2,1,0:T(8,128)(2,1)S(1)}, u32[]{:S(2)}, u32[]{:S(2)}) collective-permute-start(bf16[2,96,384]{2,1,0:T(8,128)(2,1)S(1)} %get-tuple-element.17), channel_id=1, source_target_pairs={{0,224},{16,240},{32,0},{48,16},{64,32},{80,48},{96,64},{112,80},{... | collective-permute-start | bytes 442376 | tf_op jit(solution)/shard_map/ppermute | solution.py:27
  77.1 16.1 %collective-permute-start.4 = (bf16[4,96,384]{2,1,0:T(8,128)(2,1)S(1)}, bf16[4,96,384]{2,1,0:T(8,128)(2,1)S(1)}, u32[]{:S(2)}, u32[]{:S(2)}) collective-permute-start(bf16[4,96,384]{2,1,0:T(8,128)(2,1)S(1)} %all_gather.30.own), channel_id=1, source_target_pairs={{0,256},{256,1},{1,257},{257,0},{2,258},{258,3},{3,259},{259,2},{4... | collective-permute-start | bytes 884744 | tf_op jit(solution)/shard_map/ppermute | solution.py:35
  79.9 14.0 %copy-start.6 = (bf16[2,96,384]{2,1,0:T(8,128)(2,1)}, bf16[2,96,384]{2,1,0:T(8,128)(2,1)S(1)}, u32[]{:S(2)}) copy-start(bf16[2,96,384]{2,1,0:T(8,128)(2,1)S(1)} %collective-permute-done.2.far_below) | copy-start | bytes 442372
  82.3 11.6 %copy-start.7 = (bf16[2,96,384]{2,1,0:T(8,128)(2,1)}, bf16[2,96,384]{2,1,0:T(8,128)(2,1)S(1)}, u32[]{:S(2)}) copy-start(bf16[2,96,384]{2,1,0:T(8,128)(2,1)S(1)} %collective-permute-done.3.far_above) | copy-start | bytes 442372
  82.3 11.6 %collective-permute-start.6 = (bf16[4,96,384]{2,1,0:T(8,128)(2,1)S(1)}, bf16[4,96,384]{2,1,0:T(8,128)(2,1)S(1)}, u32[]{:S(2)}, u32[]{:S(2)}) collective-permute-start(bf16[4,96,384]{2,1,0:T(8,128)(2,1)S(1)} %pad_maximum_fusion.2), channel_id=1, source_target_pairs={{0,256},{256,1},{1,257},{257,0},{2,258},{258,3},{3,259},{259,2},{4... | collective-permute-start | bytes 884744 | tf_op jit(solution)/shard_map/ppermute | solution.py:35
  93.2 17.4 %copy-start.12 = (s32[8,4]{0,1:T(4,128)S(1)}, s32[8,4]{0,1:T(4,128)}, u32[]{:S(2)}) copy-start(s32[8,4]{0,1:T(4,128)} %param.13) | copy-start | bytes 388
  93.2 0.7 copy-start.8
  93.9 0.7 copy-start.9
  94.6 0.9 copy-start.5
  101.6 28.0 %all-to-all-start.1 = ((bf16[32,16,384]{2,1,0:T(8,128)(2,1)}), bf16[32,16,384]{2,1,0:T(8,128)(2,1)S(1)}, u32[]{:S(2)}, u32[]{:S(2)}) async-start(bf16[32,16,384]{2,1,0:T(8,128)(2,1)} %bitcast.27), calls=%async_computation.1 | async-start | bytes 786432 | tf_op jit(solution)/shard_map/all_to_all | solution.py:212
  110.5 69.7 %all-gather.9.cloned.1.call-start = ((), (), s32[]{:S(2)}) async-start(), calls=%async_computation.4 | async-start | bytes 1179648 | tf_op jit(solution)/shard_map/all_gather | solution.py:231
  129.6 0.7 copy-start.1
  134.0 19.6 %all-to-all-start.2 = ((bf16[32,16,128]{2,1,0:T(8,128)(2,1)}), bf16[32,16,128]{2,1,0:T(8,128)(2,1)S(1)}, u32[]{:S(2)}, u32[]{:S(2)}) async-start(bf16[32,16,128]{2,1,0:T(8,128)(2,1)} %bitcast.30), calls=%async_computation.2 | async-start | bytes 262144 | tf_op jit(solution)/shard_map/all_to_all | solution.py:241
Sparse Core Ops, SparseCore 0:
  31.4 70.1 all-gather.6
  129.8 32.3 all-gather.8

commit v3 on v2

v3 whole, which is shorter than its diff:
```python
import functools

import jax
import jax.numpy as jnp
from jax import lax
from jax.experimental import pallas as pl
from jax.experimental.pallas import tpu as pltpu
from jax.sharding import Mesh, PartitionSpec as P

D = 3072
HD = 128
TILE = 64
WIN = 4
F32 = jnp.float32
BF16 = jnp.bfloat16
VMEM = pl.BlockSpec(memory_space=pltpu.VMEM)
SMEM = pl.BlockSpec(memory_space=pltpu.SMEM)
HBM = pl.BlockSpec(memory_space=pl.ANY)
COLUMNS = pl.BlockSpec((8, 256, 384), lambda i: (0, 2, 0))
ROWS = pl.BlockSpec((256, 384), lambda i: (i, 0))
HEADS = pl.BlockSpec((4, 2, 256, HD), lambda i: (0, 0, i, 0))

Y_PLACE = (0, 2, 1, 3)


def along_z(value, step):
    return lax.ppermute(value, ("zh", "zl"), [(i, (i + step) % 16) for i in range(16)])


def along_x(value, step):
    return lax.ppermute(value, "x", [(i, (i + step) % 4) for i in range(4)])


def along_y(value, step):
    return lax.ppermute(value, ("yl", "dp"), [(Y_PLACE[i], Y_PLACE[(i + step) % 4]) for i in range(4)])


def other_core(value):
    return lax.ppermute(value, "c", [(0, 1), (1, 0)])


def tie(*values):
    return lax.optimization_barrier(values)


def norm_kernel(blocks_ref, shift, scale, normed):
    def rows_of(step, _):
        rows = pl.ds(pl.multiple_of(step * 16, 16), 16)
        blocks = [blocks_ref[j, rows, :].astype(F32) for j in range(8)]
        middle = jnp.sum(sum(blocks), -1, keepdims=True) * (1.0 / D)
        blocks = [block - middle for block in blocks]
        spread = jnp.sum(sum(block * block for block in blocks), -1, keepdims=True) * (1.0 / D)
        inverse = lax.rsqrt(spread + 1e-06)
        for j in range(8):
            value = blocks[j] * inverse * (1.0 + scale[pl.ds(j, 1), :]) + shift[pl.ds(j, 1), :]
            normed[rows, j * 384 : (j + 1) * 384] = value.astype(BF16)
        return 0

    lax.fori_loop(0, normed.shape[0] // 16, rows_of, 0, unroll=4)


def project(normed, weight, parts, sems, fetched):
    copies = [pltpu.make_async_copy(normed.at[:, pl.ds(i * 768, 768)], parts.at[i], sems.at[i]) for i in range(4)]
    for copy in copies:
        copy.start()
    for copy in fetched:
        copy.wait()
    total = 0.0
    for i, copy in enumerate(copies):
        copy.wait()
        rows = weight[i * 2 : i * 2 + 2].reshape(768, 384)
        total += jnp.dot(parts[i], rows, preferred_element_type=F32)
    return total.astype(BF16)


def softmax(scores):
    raised = jnp.exp(scores - jnp.max(scores, -1, keepdims=True))
    return (raised * (1.0 / jnp.sum(raised, -1, keepdims=True))).astype(BF16)


def scores_of(queries, keys):
    return lax.dot_general(queries, keys, (((1,), (1,)), ((), ())), preferred_element_type=F32) * float(HD) ** (-0.5)


def sent_kernel(hidden, w_out, sent, sem):
    copies = []
    for g in range(8):
        copies.append(pltpu.make_async_copy(hidden, sent.at[g, pl.ds(0, 512)], sem.at[len(copies)]))
        for kind in range(2):
            columns = w_out.at[kind, :, pl.ds(g * 384, 384)]
            copies.append(
                pltpu.make_async_copy(columns, sent.at[g, pl.ds(512 + kind * HD, HD)], sem.at[len(copies)])
            )
    for copy in copies:
        copy.start()
    for copy in copies:
        copy.wait()


def fetch(kind, place, pieces, weight, sem):
    own, below, above, far_below, far_above, near_own, near_low, near_high = pieces
    own, below, above, far_below, far_above, near_own = (
        piece.at[:, pl.ds(kind * 96, 96)] for piece in (own, below, above, far_below, far_above, near_own)
    )
    here, there = place[0] * 4, (1 - place[0]) * 4
    parts = (
        (own, here, 4, 0),
        (below, here, 4, 3),
        (above, here, 4, 1),
        (far_below, here, 2, 2),
        (far_above, here + 2, 2, 2),
        (near_own, there, 4, 0),
        (near_low.at[0:4], there, 4, 3),
        (near_low.at[4:6], there, 2, 2),
        (near_high.at[0:4], there, 4, 1),
        (near_high.at[4:6], there + 2, 2, 2),
    )
    copies = [
        pltpu.make_async_copy(part, weight.at[pl.ds(start, count), (place[1] + ahead) % 4], sem.at[i])
        for i, (part, start, count, ahead) in enumerate(parts)
    ]
    for copy in copies:
        copy.start()
    return copies


def temporal_project_kernel(place, *refs):
    normed, out, weight, parts, sem, sems = refs[8:]
    out[...] = project(normed, weight, parts, sems, fetch(1, place, refs[:8], weight, sem))


def temporal_kernel(projected, out):
    keys, values = projected[:, 128:256], projected[:, 256:384]
    at_row = lax.broadcasted_iota(jnp.int32, (128, 512), 0) % 16
    at_column = lax.broadcasted_iota(jnp.int32, (128, 512), 1) % 16
    for step in range(4):
        rows = slice(step * 128, step * 128 + 128)
        scores = scores_of(projected[rows, 0:128], keys)
        weights = softmax(jnp.where(at_row == at_column, scores, -1e30))
        out[rows, :] = jnp.dot(weights, values, preferred_element_type=F32).astype(BF16)


def spatial_kernel(place, *refs):
    window, normed, out, weight, parts, projected, sem, sems = refs[8:]
    projected[...] = project(normed, weight, parts, sems, fetch(0, place, refs[:8], weight, sem))

    def tile_of(step, _):
        rows = pl.ds(pl.multiple_of(step * TILE, TILE), TILE)
        chosen = [pl.ds(pl.multiple_of(window[step, i] * TILE, TILE), TILE) for i in range(WIN)]
        keys = jnp.concatenate([projected[there, 128:256] for there in chosen], 0)
        values = jnp.concatenate([projected[there, 256:384] for there in chosen], 0)
        weights = softmax(scores_of(projected[rows, 0:128], keys))
        out[rows, :] = jnp.dot(weights, values, preferred_element_type=F32).astype(BF16)
        return 0

    lax.fori_loop(0, 8, tile_of, 0, unroll=True)


def mixed_kernel(core, mine, theirs, w_out, hidden, gate, out, wide):
    for side, heads in ((core[0], mine), (1 - core[0], theirs)):
        for j, ahead in enumerate((0, 3, 1, 2)):
            group = (core[1] + ahead) % 4 * 2 + side
            for kind in range(2):
                wide[:, pl.ds(pl.multiple_of(group * 256 + kind * HD, HD), HD)] = heads[j, kind]
    total = jnp.dot(wide[...], w_out[...].reshape(2048, 384), preferred_element_type=F32)
    out[...] = (hidden[...].astype(F32) + gate[...] * total).astype(BF16)


def params(flops, size):
    return dict(
        compiler_params=pltpu.CompilerParams(vmem_limit_bytes=56 * 1024 * 1024),
        cost_estimate=pl.CostEstimate(flops=flops, bytes_accessed=size, transcendentals=0),
    )


def body(hidden, shift_mod, scale_mod, gate, w_qkv, w_out, window_tiles):
    x, core, zl, yl = (lax.axis_index(name) for name in ("x", "c", "zl", "yl"))
    place = jnp.stack([yl, zl]).astype(jnp.int32)
    shift, scale = shift_mod.reshape(8, 384), scale_mod.reshape(8, 384)

    shards = jnp.concatenate([w_qkv[:, :, 0].reshape(96, 384), w_qkv[:, :, 1].reshape(96, 384)], 0)

    sent = pl.pallas_call(
        sent_kernel,
        out_shape=jax.ShapeDtypeStruct((8, 768, 384), BF16),
        in_specs=[VMEM, VMEM],
        out_specs=HBM,
        scratch_shapes=[pltpu.SemaphoreType.DMA((24,))],
        name="sent",
        **params(0, 7_000_000),
    )(hidden, w_out)
    arrived = lax.all_to_all(sent, ("x", "c"), split_axis=0, concat_axis=0, tiled=True)

    own = lax.all_gather(shards, "zh", axis=0)
    below, above = along_z(own, 1), along_z(own, -1)
    far_below, far_above = along_z(own[:2], 2), along_z(own[2:], -2)
    near_own = along_y(own, 1)
    weights = tie(own, below, above, far_below, far_above, near_own)

    def near(kind, own, below, above, far_below, far_above, near_own):
        rows = slice(kind * 96, kind * 96 + 96)
        low = along_y(jnp.concatenate([below[:, rows], far_below[:, rows]], 0), 1)
        return low, along_y(jnp.concatenate([above[:, rows], far_above[:, rows]], 0), -1)

    temporal_weights = tuple(weights) + near(1, *weights)

    normed = pl.pallas_call(
        norm_kernel,
        out_shape=jax.ShapeDtypeStruct((512, D), BF16),
        grid=(4,),
        in_specs=[
            pl.BlockSpec((8, 128, 384), lambda i: (0, i, 0)),
            pl.BlockSpec((8, 384), lambda i: (0, 0)),
            pl.BlockSpec((8, 384), lambda i: (0, 0)),
        ],
        out_specs=pl.BlockSpec((128, D), lambda i: (i, 0)),
        name="norm",
        **params(20_000_000, 6_000_000),
    )(arrived, shift, scale)

    projected = pl.pallas_call(
        temporal_project_kernel,
        out_shape=jax.ShapeDtypeStruct((512, 384), BF16),
        in_specs=[SMEM] + [HBM] * 9,
        out_specs=VMEM,
        scratch_shapes=[
            pltpu.VMEM((8, 4, 96, 384), BF16),
            pltpu.VMEM((4, 512, 768), BF16),
            pltpu.SemaphoreType.DMA((10,)),
            pltpu.SemaphoreType.DMA((4,)),
        ],
        name="temporal_project",
        **params(1_200_000_000, 6_000_000),
    )(place, *temporal_weights, normed)
    by_position = lax.all_to_all(
        projected.reshape(32, 16, 384), ("yl", "zh", "zl"), split_axis=0, concat_axis=0, tiled=True
    ).reshape(512, 384)

    *weights, _ = tie(*weights, projected)
    by_position, *near_spatial = tie(by_position, *near(0, *weights))
    spatial_weights = tuple(weights) + tuple(near_spatial)

    temporal = pl.pallas_call(
        temporal_kernel,
        out_shape=jax.ShapeDtypeStruct((512, HD), BF16),
        in_specs=[VMEM],
        out_specs=VMEM,
        name="temporal",
        **params(140_000_000, 500_000),
    )(by_position)
    temporal = lax.all_to_all(
        temporal.reshape(32, 16, HD), ("yl", "zh", "zl"), split_axis=0, concat_axis=0, tiled=True
    ).reshape(512, HD)
    spatial = pl.pallas_call(
        spatial_kernel,
        out_shape=jax.ShapeDtypeStruct((512, HD), BF16),
        in_specs=[SMEM] + [HBM] * 8 + [SMEM, HBM],
        out_specs=VMEM,
        scratch_shapes=[
            pltpu.VMEM((8, 4, 96, 384), BF16),
            pltpu.VMEM((4, 512, 768), BF16),
            pltpu.VMEM((512, 384), BF16),
            pltpu.SemaphoreType.DMA((10,)),
            pltpu.SemaphoreType.DMA((4,)),
        ],
        name="spatial",
        **params(1_300_000_000, 6_000_000),
    )(place, *spatial_weights, window_tiles, normed)

    heads = jnp.stack([spatial, temporal])
    mine = jnp.stack([heads, along_x(heads, 1), along_x(heads, -1), along_x(heads, 2)])
    theirs = other_core(mine)
    gate_here = lax.dynamic_slice_in_dim(gate, (x * 2 + core) * 384, 384).reshape(1, 384)
    return pl.pallas_call(
        mixed_kernel,
        out_shape=jax.ShapeDtypeStruct((512, 384), BF16),
        grid=(2,),
        in_specs=[SMEM, HEADS, HEADS, COLUMNS, ROWS, pl.BlockSpec((1, 384), lambda i: (0, 0))],
        out_specs=ROWS,
        scratch_shapes=[pltpu.VMEM((256, 2048), BF16)],
        name="mixed",
        **params(800_000_000, 5_000_000),
    )(jnp.stack([core, x]).astype(jnp.int32), mine, theirs, arrived, hidden, gate_here)


def solution(mesh):
    fine = Mesh(mesh.devices.reshape(2, 4, 4, 4, 2, 2), ("yl", "zh", "zl", "x", "c", "dp"))
    seq, tp = ("yl", "zh", "zl"), ("x", "c")
    in_specs = (
        P(("dp",) + seq, tp),
        P("dp"),
        P("dp"),
        P("dp"),
        P(seq, None, None, tp),
        P(None, tp, None),
        P(),
    )
    out_specs = P(("dp",) + seq, tp)
    return jax.shard_map(body, mesh=fine, in_specs=in_specs, out_specs=out_specs, check_vma=False)
```

time: 195 us -> 185 us (0.949)
  starting transfers between devices: 50.4 us -> 77.8 us
  blocking collectives: 45.9 us -> 27 us
  between operations: 13.6 us -> 0.46 us
  local copies, waits for them, and re-layouts: 9.8 us -> 6.06 us
    all_gather x4 -> x1, blocking collectives: 45.9 us -> 27 us  [body(): own = lax.all_gather(shards, 'zh', axis=0)]
    ppermute x1 -> x4, starting transfers between devices: 1.91 us -> 20.2 us  [the longest x3 11 us: along_x(): return lax.ppermute(value, 'x', [(i, (i + step) % 4) for i in range(4)])]
    ppermute x3 -> x5, waiting for transfers between devices: 0.62 us -> 8.63 us  [along_y(): lax.ppermute(value, ('yl', 'dp'), [(Y_PLACE[i], Y_PLACE[(i + step) % 4])...]
    all_to_all x1, waiting for transfers between devices: 13.1 us -> 5.23 us  [body(): lax.all_to_all(temporal.reshape(32, 16, HD), ('yl', 'zh', 'zl'), split_ax...]
    ppermute x3 -> x5, starting transfers between devices: 8.97 us -> 14.7 us  [along_y(): lax.ppermute(value, ('yl', 'dp'), [(Y_PLACE[i], Y_PLACE[(i + step) % 4])...]
    all_to_all x1, waiting for transfers between devices: 8.39 us -> 4.38 us  [body(): lax.all_to_all(projected.reshape(32, 16, 384), ('yl', 'zh', 'zl'), split_...]
    all_to_all x1, starting transfers between devices: 5.23 us -> 8.36 us  [body(): lax.all_to_all(temporal.reshape(32, 16, HD), ('yl', 'zh', 'zl'), split_ax...]
    ppermute x1 -> x4, waiting for transfers between devices: 3.76 us -> 6.25 us  [the longest x3 6 us: along_x(): return lax.ppermute(value, 'x', [(i, (i + step) % 4) for i in range(4)])]
  transfers between devices with their start and end apart: 13 -> 16, of which waited for: 8 -> 9; matrix products, arithmetic and copies ran while one was open for 2% -> 4% of each run, Pallas kernels for 14% -> 8%
where the time goes in v3:
time: 185 us; the launch traced here: 184 us
  starting transfers between devices  77.8 us (42%)
  waiting for transfers between devices  37.3 us (20%)
  Pallas kernels  31.6 us (17%)
  blocking collectives  27 us (15%)
  local copies, waits for them, and re-layouts  6.06 us (3%)
  other arithmetic  3.32 us (2%)
    all_gather x1, blocking collectives, body(): own = lax.all_gather(shards, 'zh', axis=0)  27 us
    ppermute x5, starting transfers between devices, along_y(): lax.ppermute(value, ('yl', 'dp'), [(Y_PLACE[i], Y_PLACE[(i + step) % 4])...  14.7 us
    ppermute x4, starting transfers between devices, along_z(): lax.ppermute(value, ('zh', 'zl'), [(i, (i + step) % 16) for i in range(16)])  14.1 us
    ppermute x4, waiting for transfers between devices, along_z(): lax.ppermute(value, ('zh', 'zl'), [(i, (i + step) % 16) for i in range(16)])  12.8 us
    all_to_all x1, starting transfers between devices, body(): lax.all_to_all(sent, ('x', 'c'), split_axis=0, concat_axis=0, tiled=True)  11.5 us
    ppermute x3, starting transfers between devices, along_x(): return lax.ppermute(value, 'x', [(i, (i + step) % 4) for i in range(4)])  11 us
    ppermute x1, starting transfers between devices, other_core(): return lax.ppermute(value, 'c', [(0, 1), (1, 0)])  9.19 us
    all_to_all x1, starting transfers between devices, body(): lax.all_to_all(projected.reshape(32, 16, 384), ('yl', 'zh', 'zl'), split_...  8.99 us
  transfers between devices with their start and end apart: 16, of which 9 were waited for; matrix products, arithmetic and copies ran while one was open for 4% of the time, Pallas kernels for 8%

profile of v3, /device:TPU:1, one launch (start us, length us, event | category | flops | bytes accessed | tf_op | source)
XLA Modules:
  0.0 183.6 jit_solution(17541940497135124457)
XLA Ops:
  0.0 3.9 %sent.1 = bf16[8,768,384]{2,1,0:T(8,128)(2,1)} custom-call(bf16[512,384]{1,0:T(8,128)(2,1)} %hidden.3, bf16[2,128,3072]{2,1,0:T(8,128)(2,1)} %w_out.1), custom_call_target="tpu_custom_call" | custom-call | bytes 7000000 | tf_op jit(solution)/shard_map/sent/pallas_call | solution.py:183
  3.9 11.5 %all-to-all-start = ((bf16[8,768,384]{2,1,0:T(8,128)(2,1)}), bf16[8,768,384]{2,1,0:T(8,128)(2,1)}, u32[]{:S(2)}, u32[]{:S(2)}) async-start(bf16[8,768,384]{2,1,0:T(8,128)(2,1)} %sent.1), calls=%async_computation | async-start | bytes 9437184 | tf_op jit(solution)/shard_map/all_to_all | solution.py:192
  16.4 27.0 %all-gather = bf16[768,384]{1,0:T(8,128)(2,1)S(1)} all-gather(bf16[192,384]{1,0:T(8,128)(2,1)S(1)} %pad_maximum_fusion.6), channel_id=2, replica_groups=mesh['yl'=2,'zh'=4,'zl'=4,'x'=4,'c'=2,'dp'=2] {'zh'}, dimensions={0}, use_global_device_ids=true | all-gather | bytes 737280 | tf_op jit(solution)/shard_map/all_gather | solution.py:194
  43.3 1.9 %collective-permute-start = (bf16[4,192,384]{2,1,0:T(8,128)(2,1)S(1)}, bf16[4,192,384]{2,1,0:T(8,128)(2,1)S(1)}, u32[]{:S(2)}, u32[]{:S(2)}) collective-permute-start(bf16[4,192,384]{2,1,0:T(8,128)(2,1)S(1)} %bitcast.23), channel_id=1, source_target_pairs={{0,16},{16,32},{32,48},{48,64},{64,80},{80,96},{96,112},{112,128},... | collective-permute-start | bytes 1769480 | tf_op jit(solution)/shard_map/ppermute | solution.py:27
  45.3 4.8 %collective-permute-start.1 = (bf16[4,192,384]{2,1,0:T(8,128)(2,1)S(1)}, bf16[4,192,384]{2,1,0:T(8,128)(2,1)S(1)}, u32[]{:S(2)}, u32[]{:S(2)}) collective-permute-start(bf16[4,192,384]{2,1,0:T(8,128)(2,1)S(1)} %bitcast.24), channel_id=1, source_target_pairs={{0,240},{16,0},{32,16},{48,32},{64,48},{80,64},{96,80},{112,96},{1... | collective-permute-start | bytes 1769480 | tf_op jit(solution)/shard_map/ppermute | solution.py:27
  50.0 3.2 %collective-permute-start.4 = (bf16[4,192,384]{2,1,0:T(8,128)(2,1)S(1)}, bf16[4,192,384]{2,1,0:T(8,128)(2,1)S(1)}, u32[]{:S(2)}, u32[]{:S(2)}) collective-permute-start(bf16[4,192,384]{2,1,0:T(8,128)(2,1)S(1)} %bitcast.25), channel_id=1, source_target_pairs={{0,256},{256,1},{1,257},{257,0},{2,258},{258,3},{3,259},{259,2},{4... | collective-permute-start | bytes 1769480 | tf_op jit(solution)/shard_map/ppermute | solution.py:35
  53.3 1.9 %collective-permute-start.2 = (bf16[2,192,384]{2,1,0:T(8,128)(2,1)S(1)}, bf16[2,192,384]{2,1,0:T(8,128)(2,1)S(1)}, u32[]{:S(2)}, u32[]{:S(2)}) collective-permute-start(bf16[2,192,384]{2,1,0:T(8,128)(2,1)S(1)} %bitcast.36), channel_id=1, source_target_pairs={{0,32},{16,48},{32,64},{48,80},{64,96},{80,112},{96,128},{112,144}... | collective-permute-start | bytes 884744 | tf_op jit(solution)/shard_map/ppermute | solution.py:27
  55.2 5.5 %collective-permute-start.3 = (bf16[2,192,384]{2,1,0:T(8,128)(2,1)S(1)}, bf16[2,192,384]{2,1,0:T(8,128)(2,1)S(1)}, u32[]{:S(2)}, u32[]{:S(2)}) collective-permute-start(bf16[2,192,384]{2,1,0:T(8,128)(2,1)S(1)} %bitcast.35), channel_id=1, source_target_pairs={{0,224},{16,240},{32,0},{48,16},{64,32},{80,48},{96,64},{112,80},{... | collective-permute-start | bytes 884744 | tf_op jit(solution)/shard_map/ppermute | solution.py:27
  60.7 10.2 %collective-permute-done.2.refs_3_ = bf16[2,192,384]{2,1,0:T(8,128)(2,1)S(1)} collective-permute-done((bf16[2,192,384]{2,1,0:T(8,128)(2,1)S(1)}, bf16[2,192,384]{2,1,0:T(8,128)(2,1)S(1)}, u32[]{:S(2)}, u32[]{:S(2)}) %collective-permute-start.2) | collective-permute-done | bytes 294944 | tf_op jit(solution)/shard_map/ppermute | solution.py:27
  70.9 2.7 %collective-permute-done.3.refs_4_ = bf16[2,192,384]{2,1,0:T(8,128)(2,1)S(1)} collective-permute-done((bf16[2,192,384]{2,1,0:T(8,128)(2,1)S(1)}, bf16[2,192,384]{2,1,0:T(8,128)(2,1)S(1)}, u32[]{:S(2)}, u32[]{:S(2)}) %collective-permute-start.3) | collective-permute-done | bytes 294944 | tf_op jit(solution)/shard_map/ppermute | solution.py:27
  73.7 2.1 %collective-permute-start.6 = (bf16[6,96,384]{2,1,0:T(8,128)(2,1)S(1)}, bf16[6,96,384]{2,1,0:T(8,128)(2,1)}, u32[]{:S(2)}, u32[]{:S(2)}) collective-permute-start(bf16[6,96,384]{2,1,0:T(8,128)(2,1)S(1)} %pad_maximum_fusion.2), channel_id=1, source_target_pairs={{0,257},{256,0},{1,256},{257,1},{2,259},{258,2},{3,258},{259,3},{4... | collective-permute-start | bytes 1327112 | tf_op jit(solution)/shard_map/ppermute | solution.py:35
  76.8 3.1 %collective-permute-start.5 = (bf16[6,96,384]{2,1,0:T(8,128)(2,1)}, bf16[6,96,384]{2,1,0:T(8,128)(2,1)}, u32[]{:S(2)}, u32[]{:S(2)}) collective-permute-start(bf16[6,96,384]{2,1,0:T(8,128)(2,1)} %pad_maximum_fusion.1), channel_id=1, source_target_pairs={{0,256},{256,1},{1,257},{257,0},{2,258},{258,3},{3,259},{259,2},{4... | collective-permute-start | bytes 1327112 | tf_op jit(solution)/shard_map/ppermute | solution.py:35
  81.7 5.5 %norm.1.refs_8_.refs_9_ = bf16[512,3072]{1,0:T(8,128)(2,1)} custom-call(bf16[8,768,384]{2,1,0:T(8,128)(2,1)} %all-to-all-done.blocks_ref.w_out, f32[8,384]{1,0:T(8,128)} %reshape.18.shift, f32[8,384]{1,0:T(8,128)} %reshape.19.scale), custom_call_target="tpu_custom_call" | custom-call | flops 20000000 | bytes 6000000 | tf_op jit(solution)/shard_map/norm/pallas_call | solution.py:207
  87.4 6.0 %temporal_project.1 = bf16[512,384]{1,0:T(8,128)(2,1)} custom-call(s32[2]{0:T(128)} %pad_add_fusion.1.place, bf16[4,192,384]{2,1,0:T(8,128)(2,1)} %bitcast.26, bf16[4,192,384]{2,1,0:T(8,128)(2,1)} %copy-done.1, bf16[4,192,384]{2,1,0:T(8,128)(2,1)} %copy-done.2, bf16[2,192,384]{2,1,0:T(8,128)(2,1)} %copy-done.4, bf16[2,192,384]{2,1,0:T(8,128)(2,1)} %copy-done.5, ...), custom_call_target="tpu_custom_call" | custom-call | flops 1200000000 | bytes 6000000 | tf_op jit(solution)/shard_map/temporal_project/pallas_call | solution.py:221
  93.4 9.0 %all-to-all-start.1 = ((bf16[32,16,384]{2,1,0:T(8,128)(2,1)}), bf16[32,16,384]{2,1,0:T(8,128)(2,1)S(1)}, u32[]{:S(2)}, u32[]{:S(2)}) async-start(bf16[32,16,384]{2,1,0:T(8,128)(2,1)} %bitcast.29), calls=%async_computation.1 | async-start | bytes 786432 | tf_op jit(solution)/shard_map/all_to_all | solution.py:235
  102.4 4.3 %collective-permute-start.8 = (bf16[6,96,384]{2,1,0:T(8,128)(2,1)S(1)}, bf16[6,96,384]{2,1,0:T(8,128)(2,1)S(1)}, u32[]{:S(2)}, u32[]{:S(2)}) collective-permute-start(bf16[6,96,384]{2,1,0:T(8,128)(2,1)S(1)} %pad_maximum_fusion.4), channel_id=1, source_target_pairs={{0,257},{256,0},{1,256},{257,1},{2,259},{258,2},{3,258},{259,3},{4... | collective-permute-start | bytes 1327112 | tf_op jit(solution)/shard_map/ppermute | solution.py:35
  106.9 1.9 %collective-permute-start.7 = (bf16[6,96,384]{2,1,0:T(8,128)(2,1)S(1)}, bf16[6,96,384]{2,1,0:T(8,128)(2,1)S(1)}, u32[]{:S(2)}, u32[]{:S(2)}) collective-permute-start(bf16[6,96,384]{2,1,0:T(8,128)(2,1)S(1)} %pad_maximum_fusion.3), channel_id=1, source_target_pairs={{0,256},{256,1},{1,257},{257,0},{2,258},{258,3},{3,259},{259,2},{4... | collective-permute-start | bytes 1327112 | tf_op jit(solution)/shard_map/ppermute | solution.py:35
  108.8 4.2 %collective-permute-done.8.refs_7_ = bf16[6,96,384]{2,1,0:T(8,128)(2,1)S(1)} collective-permute-done((bf16[6,96,384]{2,1,0:T(8,128)(2,1)S(1)}, bf16[6,96,384]{2,1,0:T(8,128)(2,1)S(1)}, u32[]{:S(2)}, u32[]{:S(2)}) %collective-permute-start.8) | collective-permute-done | bytes 442400 | tf_op jit(solution)/shard_map/ppermute | solution.py:35
  113.0 4.4 %collective-permute-done.7.refs_6_ = bf16[6,96,384]{2,1,0:T(8,128)(2,1)S(1)} collective-permute-done((bf16[6,96,384]{2,1,0:T(8,128)(2,1)S(1)}, bf16[6,96,384]{2,1,0:T(8,128)(2,1)S(1)}, u32[]{:S(2)}, u32[]{:S(2)}) %collective-permute-start.7) | collective-permute-done | bytes 442400 | tf_op jit(solution)/shard_map/ppermute | solution.py:35
  117.4 4.4 %all-to-all-done.1 = bf16[32,16,384]{2,1,0:T(8,128)(2,1)S(1)} async-done(((bf16[32,16,384]{2,1,0:T(8,128)(2,1)}), bf16[32,16,384]{2,1,0:T(8,128)(2,1)S(1)}, u32[]{:S(2)}, u32[]{:S(2)}) %all-to-all-start.1) | async-done | bytes 393248 | tf_op jit(solution)/shard_map/all_to_all | solution.py:235
  122.5 3.2 %temporal.1 = bf16[512,128]{1,0:T(8,128)(2,1)} custom-call(bf16[512,384]{1,0:T(8,128)(2,1)} %bitcast.28), custom_call_target="tpu_custom_call" | custom-call | flops 140000000 | bytes 500000 | tf_op jit(solution)/shard_map/temporal/pallas_call | solution.py:243
  125.7 8.4 %all-to-all-start.2 = ((bf16[32,16,128]{2,1,0:T(8,128)(2,1)}), bf16[32,16,128]{2,1,0:T(8,128)(2,1)S(1)}, u32[]{:S(2)}, u32[]{:S(2)}) async-start(bf16[32,16,128]{2,1,0:T(8,128)(2,1)} %bitcast.32), calls=%async_computation.2 | async-start | bytes 262144 | tf_op jit(solution)/shard_map/all_to_all | solution.py:251
  134.8 8.5 %spatial.1 = bf16[512,128]{1,0:T(8,128)(2,1)} custom-call(s32[2]{0:T(128)} %pad_add_fusion.1.place, bf16[4,192,384]{2,1,0:T(8,128)(2,1)} %bitcast.27, bf16[4,192,384]{2,1,0:T(8,128)(2,1)} %copy-done.1, bf16[4,192,384]{2,1,0:T(8,128)(2,1)} %copy-done.2, bf16[2,192,384]{2,1,0:T(8,128)(2,1)} %copy-done.4, bf16[2,192,384]{2,1,0:T(8,128)(2,1)} %copy-done.5, ...), custom_call_target="tpu_custom_call" | custom-call | flops 1300000000 | bytes 6000000 | tf_op jit(solution)/shard_map/spatial/pallas_call | solution.py:254
  143.3 5.2 %all-to-all-done.2 = bf16[32,16,128]{2,1,0:T(8,128)(2,1)S(1)} async-done(((bf16[32,16,128]{2,1,0:T(8,128)(2,1)}), bf16[32,16,128]{2,1,0:T(8,128)(2,1)S(1)}, u32[]{:S(2)}, u32[]{:S(2)}) %all-to-all-start.2) | async-done | bytes 131104 | tf_op jit(solution)/shard_map/all_to_all | solution.py:251
  148.5 0.9 fusion
  149.4 4.2 %collective-permute-start.9 = (bf16[2,512,128]{2,1,0:T(8,128)(2,1)S(1)}, bf16[2,512,128]{2,1,0:T(8,128)(2,1)S(1)}, u32[]{:S(2)}, u32[]{:S(2)}) collective-permute-start(bf16[2,512,128]{2,1,0:T(8,128)(2,1)S(1)} %get-tuple-element.40), channel_id=1, source_target_pairs={{0,4},{4,8},{8,12},{12,0},{1,5},{5,9},{9,13},{13,1},{2,6},{6,10},{... | collective-permute-start | bytes 786440 | tf_op jit(solution)/shard_map/ppermute | solution.py:31
  153.6 3.2 %collective-permute-start.10 = (bf16[2,512,128]{2,1,0:T(8,128)(2,1)S(1)}, bf16[2,512,128]{2,1,0:T(8,128)(2,1)S(1)}, u32[]{:S(2)}, u32[]{:S(2)}) collective-permute-start(bf16[2,512,128]{2,1,0:T(8,128)(2,1)S(1)} %get-tuple-element.40), channel_id=1, source_target_pairs={{0,12},{4,0},{8,4},{12,8},{1,13},{5,1},{9,5},{13,9},{2,14},{6,2},{... | collective-permute-start | bytes 786440 | tf_op jit(solution)/shard_map/ppermute | solution.py:31
  156.8 3.6 %collective-permute-start.11 = (bf16[2,512,128]{2,1,0:T(8,128)(2,1)S(1)}, bf16[2,512,128]{2,1,0:T(8,128)(2,1)S(1)}, u32[]{:S(2)}, u32[]{:S(2)}) collective-permute-start(bf16[2,512,128]{2,1,0:T(8,128)(2,1)S(1)} %get-tuple-element.40), channel_id=1, source_target_pairs={{0,8},{4,12},{8,0},{12,4},{1,9},{5,13},{9,1},{13,5},{2,10},{6,14},... | collective-permute-start | bytes 786440 | tf_op jit(solution)/shard_map/ppermute | solution.py:31
  160.8 5.7 %collective-permute-done.11 = bf16[2,512,128]{2,1,0:T(8,128)(2,1)S(1)} collective-permute-done((bf16[2,512,128]{2,1,0:T(8,128)(2,1)S(1)}, bf16[2,512,128]{2,1,0:T(8,128)(2,1)S(1)}, u32[]{:S(2)}, u32[]{:S(2)}) %collective-permute-start.11) | collective-permute-done | bytes 262176 | tf_op jit(solution)/shard_map/ppermute | solution.py:31
  166.6 9.2 %collective-permute-start.12 = (bf16[4,2,512,128]{3,2,1,0:T(8,128)(2,1)S(1)}, bf16[4,2,512,128]{3,2,1,0:T(8,128)(2,1)S(1)}, u32[]{:S(2)}, u32[]{:S(2)}) collective-permute-start(bf16[4,2,512,128]{3,2,1,0:T(8,128)(2,1)S(1)} %pad_maximum_fusion.mine), channel_id=1, source_target_pairs={{0,2},{2,0},{1,3},{3,1},{4,6},{6,4},{5,7},{7,5},{8,10},{10,8},{9,1... | collective-permute-start | bytes 3145736 | tf_op jit(solution)/shard_map/ppermute | solution.py:39
  178.1 1.0 copy-done.8
  179.1 4.5 %mixed.1 = bf16[512,384]{1,0:T(8,128)(2,1)} custom-call(s32[2]{0:T(128)} %pad_add_fusion.core, bf16[4,2,512,128]{3,2,1,0:T(8,128)(2,1)} %copy-done.3, bf16[4,2,512,128]{3,2,1,0:T(8,128)(2,1)} %copy-done.8, bf16[8,768,384]{2,1,0:T(8,128)(2,1)} %all-to-all-done.blocks_ref.w_out, bf16[512,384]{1,0:T(8,128)(2,1)} %hidden.3, f32[1,384]{1,0:T(1,128)} %reshape.23.gate), custom_call_target="tpu_custom_call" | custom-call | flops 800000000 | bytes 5000000 | tf_op jit(solution)/shard_map/mixed/pallas_call | solution.py:274
  (66 shorter events, 8.0 us)
Async XLA Ops:
  3.9 11.5 %copy-start.9 = (bf16[96,3,2,128]{3,2,1,0:T(2,128)(2,1)S(1)}, bf16[96,3,2,128]{3,2,1,0:T(2,128)(2,1)}, u32[]{:S(2)}) copy-start(bf16[96,3,2,128]{3,2,1,0:T(2,128)(2,1)} %param.11) | copy-start | bytes 442372
  3.9 77.8 %all-to-all-start = ((bf16[8,768,384]{2,1,0:T(8,128)(2,1)}), bf16[8,768,384]{2,1,0:T(8,128)(2,1)}, u32[]{:S(2)}, u32[]{:S(2)}) async-start(bf16[8,768,384]{2,1,0:T(8,128)(2,1)} %sent.1), calls=%async_computation | async-start | bytes 9437184 | tf_op jit(solution)/shard_map/all_to_all | solution.py:192
  15.5 64.5 %copy-start.12 = (f32[3072]{0:T(1024)S(1)}, f32[3072]{0:T(1024)}, u32[]{:S(2)}) copy-start(f32[3072]{0:T(1024)} %param.8) | copy-start | bytes 36868
  15.5 65.1 %copy-start.13 = (f32[3072]{0:T(1024)S(1)}, f32[3072]{0:T(1024)}, u32[]{:S(2)}) copy-start(f32[3072]{0:T(1024)} %param.9) | copy-start | bytes 36868
  43.3 43.9 %copy-start = (bf16[768,384]{1,0:T(8,128)(2,1)}, bf16[768,384]{1,0:T(8,128)(2,1)S(1)}, u32[]{:S(2)}) copy-start(bf16[768,384]{1,0:T(8,128)(2,1)S(1)} %all-gather) | copy-start | bytes 1769476
  43.3 30.2 %collective-permute-start = (bf16[4,192,384]{2,1,0:T(8,128)(2,1)S(1)}, bf16[4,192,384]{2,1,0:T(8,128)(2,1)S(1)}, u32[]{:S(2)}, u32[]{:S(2)}) collective-permute-start(bf16[4,192,384]{2,1,0:T(8,128)(2,1)S(1)} %bitcast.23), channel_id=1, source_target_pairs={{0,16},{16,32},{32,48},{48,64},{64,80},{80,96},{96,112},{112,128},... | collective-permute-start | bytes 1769480 | tf_op jit(solution)/shard_map/ppermute | solution.py:27
  45.3 28.3 %collective-permute-start.1 = (bf16[4,192,384]{2,1,0:T(8,128)(2,1)S(1)}, bf16[4,192,384]{2,1,0:T(8,128)(2,1)S(1)}, u32[]{:S(2)}, u32[]{:S(2)}) collective-permute-start(bf16[4,192,384]{2,1,0:T(8,128)(2,1)S(1)} %bitcast.24), channel_id=1, source_target_pairs={{0,240},{16,0},{32,16},{48,32},{64,48},{80,64},{96,80},{112,96},{1... | collective-permute-start | bytes 1769480 | tf_op jit(solution)/shard_map/ppermute | solution.py:27
  50.0 23.6 %collective-permute-start.4 = (bf16[4,192,384]{2,1,0:T(8,128)(2,1)S(1)}, bf16[4,192,384]{2,1,0:T(8,128)(2,1)S(1)}, u32[]{:S(2)}, u32[]{:S(2)}) collective-permute-start(bf16[4,192,384]{2,1,0:T(8,128)(2,1)S(1)} %bitcast.25), channel_id=1, source_target_pairs={{0,256},{256,1},{1,257},{257,0},{2,258},{258,3},{3,259},{259,2},{4... | collective-permute-start | bytes 1769480 | tf_op jit(solution)/shard_map/ppermute | solution.py:35
  53.3 17.6 %collective-permute-start.2 = (bf16[2,192,384]{2,1,0:T(8,128)(2,1)S(1)}, bf16[2,192,384]{2,1,0:T(8,128)(2,1)S(1)}, u32[]{:S(2)}, u32[]{:S(2)}) collective-permute-start(bf16[2,192,384]{2,1,0:T(8,128)(2,1)S(1)} %bitcast.36), channel_id=1, source_target_pairs={{0,32},{16,48},{32,64},{48,80},{64,96},{80,112},{96,128},{112,144}... | collective-permute-start | bytes 884744 | tf_op jit(solution)/shard_map/ppermute | solution.py:27
  55.2 18.3 %collective-permute-start.3 = (bf16[2,192,384]{2,1,0:T(8,128)(2,1)S(1)}, bf16[2,192,384]{2,1,0:T(8,128)(2,1)S(1)}, u32[]{:S(2)}, u32[]{:S(2)}) collective-permute-start(bf16[2,192,384]{2,1,0:T(8,128)(2,1)S(1)} %bitcast.35), channel_id=1, source_target_pairs={{0,224},{16,240},{32,0},{48,16},{64,32},{80,48},{96,64},{112,80},{... | collective-permute-start | bytes 884744 | tf_op jit(solution)/shard_map/ppermute | solution.py:27
  70.9 16.4 %copy-start.4 = (bf16[2,192,384]{2,1,0:T(8,128)(2,1)}, bf16[2,192,384]{2,1,0:T(8,128)(2,1)S(1)}, u32[]{:S(2)}) copy-start(bf16[2,192,384]{2,1,0:T(8,128)(2,1)S(1)} %collective-permute-done.2.refs_3_) | copy-start | bytes 884740
  73.6 13.7 %copy-start.5 = (bf16[2,192,384]{2,1,0:T(8,128)(2,1)}, bf16[2,192,384]{2,1,0:T(8,128)(2,1)S(1)}, u32[]{:S(2)}) copy-start(bf16[2,192,384]{2,1,0:T(8,128)(2,1)S(1)} %collective-permute-done.3.refs_4_) | copy-start | bytes 884740
  73.6 13.7 %copy-start.1 = (bf16[4,192,384]{2,1,0:T(8,128)(2,1)}, bf16[4,192,384]{2,1,0:T(8,128)(2,1)S(1)}, u32[]{:S(2)}) copy-start(bf16[4,192,384]{2,1,0:T(8,128)(2,1)S(1)} %collective-permute-done.refs_1_) | copy-start | bytes 1769476
  73.6 13.7 %copy-start.2 = (bf16[4,192,384]{2,1,0:T(8,128)(2,1)}, bf16[4,192,384]{2,1,0:T(8,128)(2,1)S(1)}, u32[]{:S(2)}) copy-start(bf16[4,192,384]{2,1,0:T(8,128)(2,1)S(1)} %collective-permute-done.1.refs_2_) | copy-start | bytes 1769476
  73.6 13.7 %copy-start.6 = (bf16[4,192,384]{2,1,0:T(8,128)(2,1)}, bf16[4,192,384]{2,1,0:T(8,128)(2,1)S(1)}, u32[]{:S(2)}) copy-start(bf16[4,192,384]{2,1,0:T(8,128)(2,1)S(1)} %collective-permute-done.4.refs_5_) | copy-start | bytes 1769476
  73.7 13.6 %collective-permute-start.6 = (bf16[6,96,384]{2,1,0:T(8,128)(2,1)S(1)}, bf16[6,96,384]{2,1,0:T(8,128)(2,1)}, u32[]{:S(2)}, u32[]{:S(2)}) collective-permute-start(bf16[6,96,384]{2,1,0:T(8,128)(2,1)S(1)} %pad_maximum_fusion.2), channel_id=1, source_target_pairs={{0,257},{256,0},{1,256},{257,1},{2,259},{258,2},{3,258},{259,3},{4... | collective-permute-start | bytes 1327112 | tf_op jit(solution)/shard_map/ppermute | solution.py:35
  76.8 10.6 %collective-permute-start.5 = (bf16[6,96,384]{2,1,0:T(8,128)(2,1)}, bf16[6,96,384]{2,1,0:T(8,128)(2,1)}, u32[]{:S(2)}, u32[]{:S(2)}) collective-permute-start(bf16[6,96,384]{2,1,0:T(8,128)(2,1)} %pad_maximum_fusion.1), channel_id=1, source_target_pairs={{0,256},{256,1},{1,257},{257,0},{2,258},{258,3},{3,259},{259,2},{4... | collective-permute-start | bytes 1327112 | tf_op jit(solution)/shard_map/ppermute | solution.py:35
  87.3 46.8 %copy-start.14 = (s32[8,4]{0,1:T(4,128)S(1)}, s32[8,4]{0,1:T(4,128)}, u32[]{:S(2)}) copy-start(s32[8,4]{0,1:T(4,128)} %param.13) | copy-start | bytes 388
  87.3 15.0 %slice-start.1 = ((bf16[4,192,384]{2,1,0:T(8,128)(2,1)}), bf16[4,96,384]{2,1,0:T(8,128)(2,1)S(1)}, s32[]{:S(2)}) async-start(bf16[4,192,384]{2,1,0:T(8,128)(2,1)} %copy-done.2), calls=%async_computation.4 | async-start | bytes 589824 | tf_op jit(solution)/shard_map/slice | solution.py:203
  87.3 15.0 %slice-start.3 = ((bf16[2,192,384]{2,1,0:T(8,128)(2,1)}), bf16[2,96,384]{2,1,0:T(8,128)(2,1)S(1)}, s32[]{:S(2)}) async-start(bf16[2,192,384]{2,1,0:T(8,128)(2,1)} %copy-done.5), calls=%async_computation.6 | async-start | bytes 294912 | tf_op jit(solution)/shard_map/slice | solution.py:203
  87.4 19.4 %slice-start = ((bf16[4,192,384]{2,1,0:T(8,128)(2,1)}), bf16[4,96,384]{2,1,0:T(8,128)(2,1)S(1)}, s32[]{:S(2)}) async-start(bf16[4,192,384]{2,1,0:T(8,128)(2,1)} %copy-done.1), calls=%async_computation.3 | async-start | bytes 589824 | tf_op jit(solution)/shard_map/slice | solution.py:202
  87.4 19.4 %slice-start.2 = ((bf16[2,192,384]{2,1,0:T(8,128)(2,1)}), bf16[2,96,384]{2,1,0:T(8,128)(2,1)S(1)}, s32[]{:S(2)}) async-start(bf16[2,192,384]{2,1,0:T(8,128)(2,1)} %copy-done.4), calls=%async_computation.5 | async-start | bytes 294912 | tf_op jit(solution)/shard_map/slice | solution.py:202
  93.4 28.4 %all-to-all-start.1 = ((bf16[32,16,384]{2,1,0:T(8,128)(2,1)}), bf16[32,16,384]{2,1,0:T(8,128)(2,1)S(1)}, u32[]{:S(2)}, u32[]{:S(2)}) async-start(bf16[32,16,384]{2,1,0:T(8,128)(2,1)} %bitcast.29), calls=%async_computation.1 | async-start | bytes 786432 | tf_op jit(solution)/shard_map/all_to_all | solution.py:235
  102.4 10.5 %collective-permute-start.8 = (bf16[6,96,384]{2,1,0:T(8,128)(2,1)S(1)}, bf16[6,96,384]{2,1,0:T(8,128)(2,1)S(1)}, u32[]{:S(2)}, u32[]{:S(2)}) collective-permute-start(bf16[6,96,384]{2,1,0:T(8,128)(2,1)S(1)} %pad_maximum_fusion.4), channel_id=1, source_target_pairs={{0,257},{256,0},{1,256},{257,1},{2,259},{258,2},{3,258},{259,3},{4... | collective-permute-start | bytes 1327112 | tf_op jit(solution)/shard_map/ppermute | solution.py:35
  106.9 10.6 %collective-permute-start.7 = (bf16[6,96,384]{2,1,0:T(8,128)(2,1)S(1)}, bf16[6,96,384]{2,1,0:T(8,128)(2,1)S(1)}, u32[]{:S(2)}, u32[]{:S(2)}) collective-permute-start(bf16[6,96,384]{2,1,0:T(8,128)(2,1)S(1)} %pad_maximum_fusion.3), channel_id=1, source_target_pairs={{0,256},{256,1},{1,257},{257,0},{2,258},{258,3},{3,259},{259,2},{4... | collective-permute-start | bytes 1327112 | tf_op jit(solution)/shard_map/ppermute | solution.py:35
  113.0 21.8 %copy-start.10 = (bf16[6,96,384]{2,1,0:T(8,128)(2,1)}, bf16[6,96,384]{2,1,0:T(8,128)(2,1)S(1)}, u32[]{:S(2)}) copy-start(bf16[6,96,384]{2,1,0:T(8,128)(2,1)S(1)} %collective-permute-done.8.refs_7_) | copy-start | bytes 1327108
  117.4 17.4 %copy-start.11 = (bf16[6,96,384]{2,1,0:T(8,128)(2,1)}, bf16[6,96,384]{2,1,0:T(8,128)(2,1)S(1)}, u32[]{:S(2)}) copy-start(bf16[6,96,384]{2,1,0:T(8,128)(2,1)S(1)} %collective-permute-done.7.refs_6_) | copy-start | bytes 1327108
  125.7 22.8 %all-to-all-start.2 = ((bf16[32,16,128]{2,1,0:T(8,128)(2,1)}), bf16[32,16,128]{2,1,0:T(8,128)(2,1)S(1)}, u32[]{:S(2)}, u32[]{:S(2)}) async-start(bf16[32,16,128]{2,1,0:T(8,128)(2,1)} %bitcast.32), calls=%async_computation.2 | async-start | bytes 262144 | tf_op jit(solution)/shard_map/all_to_all | solution.py:251
  149.4 11.0 %collective-permute-start.9 = (bf16[2,512,128]{2,1,0:T(8,128)(2,1)S(1)}, bf16[2,512,128]{2,1,0:T(8,128)(2,1)S(1)}, u32[]{:S(2)}, u32[]{:S(2)}) collective-permute-start(bf16[2,512,128]{2,1,0:T(8,128)(2,1)S(1)} %get-tuple-element.40), channel_id=1, source_target_pairs={{0,4},{4,8},{8,12},{12,0},{1,5},{5,9},{9,13},{13,1},{2,6},{6,10},{... | collective-permute-start | bytes 786440 | tf_op jit(solution)/shard_map/ppermute | solution.py:31
  153.6 7.1 %collective-permute-start.10 = (bf16[2,512,128]{2,1,0:T(8,128)(2,1)S(1)}, bf16[2,512,128]{2,1,0:T(8,128)(2,1)S(1)}, u32[]{:S(2)}, u32[]{:S(2)}) collective-permute-start(bf16[2,512,128]{2,1,0:T(8,128)(2,1)S(1)} %get-tuple-element.40), channel_id=1, source_target_pairs={{0,12},{4,0},{8,4},{12,8},{1,13},{5,1},{9,5},{13,9},{2,14},{6,2},{... | collective-permute-start | bytes 786440 | tf_op jit(solution)/shard_map/ppermute | solution.py:31
  156.8 9.7 %collective-permute-start.11 = (bf16[2,512,128]{2,1,0:T(8,128)(2,1)S(1)}, bf16[2,512,128]{2,1,0:T(8,128)(2,1)S(1)}, u32[]{:S(2)}, u32[]{:S(2)}) collective-permute-start(bf16[2,512,128]{2,1,0:T(8,128)(2,1)S(1)} %get-tuple-element.40), channel_id=1, source_target_pairs={{0,8},{4,12},{8,0},{12,4},{1,9},{5,13},{9,1},{13,5},{2,10},{6,14},... | collective-permute-start | bytes 786440 | tf_op jit(solution)/shard_map/ppermute | solution.py:31
  166.6 11.5 %collective-permute-start.12 = (bf16[4,2,512,128]{3,2,1,0:T(8,128)(2,1)S(1)}, bf16[4,2,512,128]{3,2,1,0:T(8,128)(2,1)S(1)}, u32[]{:S(2)}, u32[]{:S(2)}) collective-permute-start(bf16[4,2,512,128]{3,2,1,0:T(8,128)(2,1)S(1)} %pad_maximum_fusion.mine), channel_id=1, source_target_pairs={{0,2},{2,0},{1,3},{3,1},{4,6},{6,4},{5,7},{7,5},{8,10},{10,8},{9,1... | collective-permute-start | bytes 3145736 | tf_op jit(solution)/shard_map/ppermute | solution.py:39
  (3 other events, 13.2 us)

commit v4 on v3

--- a/solution.py
+++ b/solution.py
@@ -51,9 +51,10 @@
         blocks = [block - middle for block in blocks]
         spread = jnp.sum(sum(block * block for block in blocks), -1, keepdims=True) * (1.0 / D)
         inverse = lax.rsqrt(spread + 1e-06)
-        for j in range(8):
-            value = blocks[j] * inverse * (1.0 + scale[pl.ds(j, 1), :]) + shift[pl.ds(j, 1), :]
-            normed[rows, j * 384 : (j + 1) * 384] = value.astype(BF16)
+        for j in range(24):
+            block = blocks[j // 3][:, j % 3 * 128 : j % 3 * 128 + 128]
+            value = block * inverse * (1.0 + scale[j : j + 1, :]) + shift[j : j + 1, :]
+            normed[rows, j * 128 : j * 128 + 128] = value.astype(BF16)
         return 0
 
     lax.fori_loop(0, normed.shape[0] // 16, rows_of, 0, unroll=4)
@@ -156,27 +157,37 @@
     lax.fori_loop(0, 8, tile_of, 0, unroll=True)
 
 
-def mixed_kernel(core, mine, theirs, w_out, hidden, gate, out, wide):
-    for side, heads in ((core[0], mine), (1 - core[0], theirs)):
-        for j, ahead in enumerate((0, 3, 1, 2)):
-            group = (core[1] + ahead) % 4 * 2 + side
-            for kind in range(2):
-                wide[:, pl.ds(pl.multiple_of(group * 256 + kind * HD, HD), HD)] = heads[j, kind]
-    total = jnp.dot(wide[...], w_out[...].reshape(2048, 384), preferred_element_type=F32)
-    out[...] = (hidden[...].astype(F32) + gate[...] * total).astype(BF16)
-
-
-def params(flops, size):
+def heads_times(heads, w_out, wide, x, side):
+    for j, ahead in enumerate((0, 3, 1, 2)):
+        for kind in range(2):
+            wide[:, (j * 2 + kind) * HD : (j * 2 + kind + 1) * HD] = heads[j, kind]
+    rows = jnp.concatenate([w_out[(x + ahead) % 4 * 2 + side] for ahead in (0, 3, 1, 2)], 0)
+    return jnp.dot(wide[...], rows, preferred_element_type=F32)
+
+
+def share_kernel(place, heads, w_out, share, wide):
+    share[...] = heads_times(heads, w_out, wide, place[2], place[3])
+
+
+def mixed_kernel(place, heads, w_out, share, hidden, gate, out, wide):
+    total = share[...] + heads_times(heads, w_out, wide, place[2], 1 - place[3])
+    for k in range(3):
+        columns = slice(k * 128, k * 128 + 128)
+        scale = gate[pl.ds((place[2] * 2 + place[3]) * 3 + k, 1), :]
+        out[:, columns] = (hidden[:, columns].astype(F32) + scale * total[:, columns]).astype(BF16)
+
+
+def params(flops, size, limit=56):
     return dict(
-        compiler_params=pltpu.CompilerParams(vmem_limit_bytes=56 * 1024 * 1024),
+        compiler_params=pltpu.CompilerParams(vmem_limit_bytes=limit * 1024 * 1024),
         cost_estimate=pl.CostEstimate(flops=flops, bytes_accessed=size, transcendentals=0),
     )
 
 
 def body(hidden, shift_mod, scale_mod, gate, w_qkv, w_out, window_tiles):
     x, core, zl, yl = (lax.axis_index(name) for name in ("x", "c", "zl", "yl"))
-    place = jnp.stack([yl, zl]).astype(jnp.int32)
-    shift, scale = shift_mod.reshape(8, 384), scale_mod.reshape(8, 384)
+    place = jnp.stack([yl, zl, x, core]).astype(jnp.int32)
+    shift, scale, gate = (value.reshape(24, 128) for value in (shift_mod, scale_mod, gate))
 
     shards = jnp.concatenate([w_qkv[:, :, 0].reshape(96, 384), w_qkv[:, :, 1].reshape(96, 384)], 0)
 
@@ -195,7 +206,7 @@
     below, above = along_z(own, 1), along_z(own, -1)
     far_below, far_above = along_z(own[:2], 2), along_z(own[2:], -2)
     near_own = along_y(own, 1)
-    weights = tie(own, below, above, far_below, far_above, near_own)
+    place, window_tiles, *weights = tie(place, window_tiles, own, below, above, far_below, far_above, near_own)
 
     def near(kind, own, below, above, far_below, far_above, near_own):
         rows = slice(kind * 96, kind * 96 + 96)
@@ -210,8 +221,8 @@
         grid=(4,),
         in_specs=[
             pl.BlockSpec((8, 128, 384), lambda i: (0, i, 0)),
-            pl.BlockSpec((8, 384), lambda i: (0, 0)),
-            pl.BlockSpec((8, 384), lambda i: (0, 0)),
+            pl.BlockSpec((24, 128), lambda i: (0, 0)),
+            pl.BlockSpec((24, 128), lambda i: (0, 0)),
         ],
         out_specs=pl.BlockSpec((128, D), lambda i: (i, 0)),
         name="norm",
@@ -270,17 +281,26 @@
     heads = jnp.stack([spatial, temporal])
     mine = jnp.stack([heads, along_x(heads, 1), along_x(heads, -1), along_x(heads, 2)])
     theirs = other_core(mine)
-    gate_here = lax.dynamic_slice_in_dim(gate, (x * 2 + core) * 384, 384).reshape(1, 384)
+    share = pl.pallas_call(
+        share_kernel,
+        out_shape=jax.ShapeDtypeStruct((512, 384), F32),
+        grid=(2,),
+        in_specs=[SMEM, HEADS, COLUMNS],
+        out_specs=ROWS,
+        scratch_shapes=[pltpu.VMEM((256, 1024), BF16)],
+        name="share",
+        **params(400_000_000, 4_000_000, 24),
+    )(place, mine, arrived)
     return pl.pallas_call(
         mixed_kernel,
         out_shape=jax.ShapeDtypeStruct((512, 384), BF16),
         grid=(2,),
-        in_specs=[SMEM, HEADS, HEADS, COLUMNS, ROWS, pl.BlockSpec((1, 384), lambda i: (0, 0))],
+        in_specs=[SMEM, HEADS, COLUMNS, ROWS, ROWS, pl.BlockSpec((24, 128), lambda i: (0, 0))],
         out_specs=ROWS,
-        scratch_shapes=[pltpu.VMEM((256, 2048), BF16)],
+        scratch_shapes=[pltpu.VMEM((256, 1024), BF16)],
         name="mixed",
-        **params(800_000_000, 5_000_000),
-    )(jnp.stack([core, x]).astype(jnp.int32), mine, theirs, arrived, hidden, gate_here)
+        **params(400_000_000, 5_000_000, 24),
+    )(place, theirs, arrived, share, hidden, gate)
 
 
 def solution(mesh):

time: 185 us -> 182 us (0.984)
  local copies, waits for them, and re-layouts: 6.06 us -> 2.51 us
    pallas_call x0 -> x1, Pallas kernels: none -> 2.43 us  [body(): pl.pallas_call(share_kernel, out_shape=jax.ShapeDtypeStruct((512, 384), F...]
  transfers between devices with their start and end apart: 16 -> 16, of which waited for: 9 -> 9; matrix products, arithmetic and copies ran while one was open for 4% -> 2% of each run, Pallas kernels for 8% -> 9%
where the time goes in v4:
time: 182 us; the launch traced here: 181 us
  starting transfers between devices  78.4 us (43%)
  waiting for transfers between devices  37.1 us (20%)
  Pallas kernels  32.7 us (18%)
  blocking collectives  27 us (15%)
  other arithmetic  2.75 us (2%)
  local copies, waits for them, and re-layouts  2.51 us (1%)
    all_gather x1, blocking collectives, body(): own = lax.all_gather(shards, 'zh', axis=0)  27 us
    ppermute x5, starting transfers between devices, along_y(): lax.ppermute(value, ('yl', 'dp'), [(Y_PLACE[i], Y_PLACE[(i + step) % 4])...  15.1 us
    ppermute x4, starting transfers between devices, along_z(): lax.ppermute(value, ('zh', 'zl'), [(i, (i + step) % 16) for i in range(16)])  14.1 us
    ppermute x4, waiting for transfers between devices, along_z(): lax.ppermute(value, ('zh', 'zl'), [(i, (i + step) % 16) for i in range(16)])  12.2 us
    all_to_all x1, starting transfers between devices, body(): lax.all_to_all(sent, ('x', 'c'), split_axis=0, concat_axis=0, tiled=True)  11.5 us
    ppermute x3, starting transfers between devices, along_x(): return lax.ppermute(value, 'x', [(i, (i + step) % 4) for i in range(4)])  10.9 us
    ppermute x5, waiting for transfers between devices, along_y(): lax.ppermute(value, ('yl', 'dp'), [(Y_PLACE[i], Y_PLACE[(i + step) % 4])...  10.3 us
    ppermute x1, starting transfers between devices, other_core(): return lax.ppermute(value, 'c', [(0, 1), (1, 0)])  9.21 us
  transfers between devices with their start and end apart: 16, of which 9 were waited for; matrix products, arithmetic and copies ran while one was open for 2% of the time, Pallas kernels for 9%

profile of v4, /device:TPU:1, one launch (start us, length us, event | category | flops | bytes accessed | tf_op | source)
XLA Modules:
  0.0 180.9 jit_solution(7103611561375805191)
XLA Ops:
  0.0 3.9 %sent.1 = bf16[8,768,384]{2,1,0:T(8,128)(2,1)} custom-call(bf16[512,384]{1,0:T(8,128)(2,1)} %hidden.3, bf16[2,128,3072]{2,1,0:T(8,128)(2,1)} %w_out.1), custom_call_target="tpu_custom_call" | custom-call | bytes 7000000 | tf_op jit(solution)/shard_map/sent/pallas_call | solution.py:194
  3.9 11.5 %all-to-all-start = ((bf16[8,768,384]{2,1,0:T(8,128)(2,1)}), bf16[8,768,384]{2,1,0:T(8,128)(2,1)}, u32[]{:S(2)}, u32[]{:S(2)}) async-start(bf16[8,768,384]{2,1,0:T(8,128)(2,1)} %sent.1), calls=%async_computation | async-start | bytes 9437184 | tf_op jit(solution)/shard_map/all_to_all | solution.py:203
  16.4 27.0 %all-gather = bf16[768,384]{1,0:T(8,128)(2,1)S(1)} all-gather(bf16[192,384]{1,0:T(8,128)(2,1)S(1)} %pad_maximum_fusion.6), channel_id=2, replica_groups=mesh['yl'=2,'zh'=4,'zl'=4,'x'=4,'c'=2,'dp'=2] {'zh'}, dimensions={0}, use_global_device_ids=true | all-gather | bytes 737280 | tf_op jit(solution)/shard_map/all_gather | solution.py:205
  43.3 1.9 %collective-permute-start = (bf16[4,192,384]{2,1,0:T(8,128)(2,1)S(1)}, bf16[4,192,384]{2,1,0:T(8,128)(2,1)S(1)}, u32[]{:S(2)}, u32[]{:S(2)}) collective-permute-start(bf16[4,192,384]{2,1,0:T(8,128)(2,1)S(1)} %bitcast.27), channel_id=1, source_target_pairs={{0,16},{16,32},{32,48},{48,64},{64,80},{80,96},{96,112},{112,128},... | collective-permute-start | bytes 1769480 | tf_op jit(solution)/shard_map/ppermute | solution.py:27
  45.2 4.8 %collective-permute-start.1 = (bf16[4,192,384]{2,1,0:T(8,128)(2,1)S(1)}, bf16[4,192,384]{2,1,0:T(8,128)(2,1)S(1)}, u32[]{:S(2)}, u32[]{:S(2)}) collective-permute-start(bf16[4,192,384]{2,1,0:T(8,128)(2,1)S(1)} %bitcast.28), channel_id=1, source_target_pairs={{0,240},{16,0},{32,16},{48,32},{64,48},{80,64},{96,80},{112,96},{1... | collective-permute-start | bytes 1769480 | tf_op jit(solution)/shard_map/ppermute | solution.py:27
  50.0 3.2 %collective-permute-start.4 = (bf16[4,192,384]{2,1,0:T(8,128)(2,1)S(1)}, bf16[4,192,384]{2,1,0:T(8,128)(2,1)S(1)}, u32[]{:S(2)}, u32[]{:S(2)}) collective-permute-start(bf16[4,192,384]{2,1,0:T(8,128)(2,1)S(1)} %bitcast.29), channel_id=1, source_target_pairs={{0,256},{256,1},{1,257},{257,0},{2,258},{258,3},{3,259},{259,2},{4... | collective-permute-start | bytes 1769480 | tf_op jit(solution)/shard_map/ppermute | solution.py:35
  53.3 1.9 %collective-permute-start.2 = (bf16[2,192,384]{2,1,0:T(8,128)(2,1)S(1)}, bf16[2,192,384]{2,1,0:T(8,128)(2,1)S(1)}, u32[]{:S(2)}, u32[]{:S(2)}) collective-permute-start(bf16[2,192,384]{2,1,0:T(8,128)(2,1)S(1)} %bitcast.40), channel_id=1, source_target_pairs={{0,32},{16,48},{32,64},{48,80},{64,96},{80,112},{96,128},{112,144}... | collective-permute-start | bytes 884744 | tf_op jit(solution)/shard_map/ppermute | solution.py:27
  55.2 5.5 %collective-permute-start.3 = (bf16[2,192,384]{2,1,0:T(8,128)(2,1)S(1)}, bf16[2,192,384]{2,1,0:T(8,128)(2,1)S(1)}, u32[]{:S(2)}, u32[]{:S(2)}) collective-permute-start(bf16[2,192,384]{2,1,0:T(8,128)(2,1)S(1)} %bitcast.39), channel_id=1, source_target_pairs={{0,224},{16,240},{32,0},{48,16},{64,32},{80,48},{96,64},{112,80},{... | collective-permute-start | bytes 884744 | tf_op jit(solution)/shard_map/ppermute | solution.py:27
  61.3 9.5 %collective-permute-done.2.refs_3_ = bf16[2,192,384]{2,1,0:T(8,128)(2,1)S(1)} collective-permute-done((bf16[2,192,384]{2,1,0:T(8,128)(2,1)S(1)}, bf16[2,192,384]{2,1,0:T(8,128)(2,1)S(1)}, u32[]{:S(2)}, u32[]{:S(2)}) %collective-permute-start.2) | collective-permute-done | bytes 294944 | tf_op jit(solution)/shard_map/ppermute | solution.py:27
  70.9 2.7 %collective-permute-done.3.refs_4_ = bf16[2,192,384]{2,1,0:T(8,128)(2,1)S(1)} collective-permute-done((bf16[2,192,384]{2,1,0:T(8,128)(2,1)S(1)}, bf16[2,192,384]{2,1,0:T(8,128)(2,1)S(1)}, u32[]{:S(2)}, u32[]{:S(2)}) %collective-permute-start.3) | collective-permute-done | bytes 294944 | tf_op jit(solution)/shard_map/ppermute | solution.py:27
  73.7 2.1 %collective-permute-start.6 = (bf16[6,96,384]{2,1,0:T(8,128)(2,1)S(1)}, bf16[6,96,384]{2,1,0:T(8,128)(2,1)}, u32[]{:S(2)}, u32[]{:S(2)}) collective-permute-start(bf16[6,96,384]{2,1,0:T(8,128)(2,1)S(1)} %pad_maximum_fusion.2), channel_id=1, source_target_pairs={{0,257},{256,0},{1,256},{257,1},{2,259},{258,2},{3,258},{259,3},{4... | collective-permute-start | bytes 1327112 | tf_op jit(solution)/shard_map/ppermute | solution.py:35
  76.7 3.1 %collective-permute-start.5 = (bf16[6,96,384]{2,1,0:T(8,128)(2,1)}, bf16[6,96,384]{2,1,0:T(8,128)(2,1)}, u32[]{:S(2)}, u32[]{:S(2)}) collective-permute-start(bf16[6,96,384]{2,1,0:T(8,128)(2,1)} %pad_maximum_fusion.1), channel_id=1, source_target_pairs={{0,256},{256,1},{1,257},{257,0},{2,258},{258,3},{3,259},{259,2},{4... | collective-permute-start | bytes 1327112 | tf_op jit(solution)/shard_map/ppermute | solution.py:35
  79.9 5.6 %norm.1.refs_8_.refs_9_ = bf16[512,3072]{1,0:T(8,128)(2,1)} custom-call(bf16[8,768,384]{2,1,0:T(8,128)(2,1)} %all-to-all-done.blocks_ref.w_out, f32[24,128]{1,0:T(8,128)} %bitcast.44, f32[24,128]{1,0:T(8,128)} %bitcast.45), custom_call_target="tpu_custom_call" | custom-call | flops 20000000 | bytes 6000000 | tf_op jit(solution)/shard_map/norm/pallas_call | solution.py:218
  85.6 1.7 collective-permute-done.5.refs_6_
  87.3 5.8 %temporal_project.1 = bf16[512,384]{1,0:T(8,128)(2,1)} custom-call(s32[4]{0:T(128)} %pad_add_fusion.place, bf16[4,192,384]{2,1,0:T(8,128)(2,1)} %bitcast.30, bf16[4,192,384]{2,1,0:T(8,128)(2,1)} %copy-done.4, bf16[4,192,384]{2,1,0:T(8,128)(2,1)} %copy-done.5, bf16[2,192,384]{2,1,0:T(8,128)(2,1)} %copy-done.6, bf16[2,192,384]{2,1,0:T(8,128)(2,1)} %copy-done.7, ...), custom_call_target="tpu_custom_call" | custom-call | flops 1200000000 | bytes 6000000 | tf_op jit(solution)/shard_map/temporal_project/pallas_call | solution.py:232
  93.2 8.8 %all-to-all-start.1 = ((bf16[32,16,384]{2,1,0:T(8,128)(2,1)}), bf16[32,16,384]{2,1,0:T(8,128)(2,1)S(1)}, u32[]{:S(2)}, u32[]{:S(2)}) async-start(bf16[32,16,384]{2,1,0:T(8,128)(2,1)} %bitcast.33), calls=%async_computation.1 | async-start | bytes 786432 | tf_op jit(solution)/shard_map/all_to_all | solution.py:246
  102.0 4.7 %collective-permute-start.8 = (bf16[6,96,384]{2,1,0:T(8,128)(2,1)S(1)}, bf16[6,96,384]{2,1,0:T(8,128)(2,1)S(1)}, u32[]{:S(2)}, u32[]{:S(2)}) collective-permute-start(bf16[6,96,384]{2,1,0:T(8,128)(2,1)S(1)} %pad_maximum_fusion.4), channel_id=1, source_target_pairs={{0,257},{256,0},{1,256},{257,1},{2,259},{258,2},{3,258},{259,3},{4... | collective-permute-start | bytes 1327112 | tf_op jit(solution)/shard_map/ppermute | solution.py:35
  106.8 1.9 %collective-permute-start.7 = (bf16[6,96,384]{2,1,0:T(8,128)(2,1)S(1)}, bf16[6,96,384]{2,1,0:T(8,128)(2,1)S(1)}, u32[]{:S(2)}, u32[]{:S(2)}) collective-permute-start(bf16[6,96,384]{2,1,0:T(8,128)(2,1)S(1)} %pad_maximum_fusion.3), channel_id=1, source_target_pairs={{0,256},{256,1},{1,257},{257,0},{2,258},{258,3},{3,259},{259,2},{4... | collective-permute-start | bytes 1327112 | tf_op jit(solution)/shard_map/ppermute | solution.py:35
  108.8 3.5 %collective-permute-done.8.refs_7_ = bf16[6,96,384]{2,1,0:T(8,128)(2,1)S(1)} collective-permute-done((bf16[6,96,384]{2,1,0:T(8,128)(2,1)S(1)}, bf16[6,96,384]{2,1,0:T(8,128)(2,1)S(1)}, u32[]{:S(2)}, u32[]{:S(2)}) %collective-permute-start.8) | collective-permute-done | bytes 442400 | tf_op jit(solution)/shard_map/ppermute | solution.py:35
  112.2 5.1 %collective-permute-done.7.refs_6_ = bf16[6,96,384]{2,1,0:T(8,128)(2,1)S(1)} collective-permute-done((bf16[6,96,384]{2,1,0:T(8,128)(2,1)S(1)}, bf16[6,96,384]{2,1,0:T(8,128)(2,1)S(1)}, u32[]{:S(2)}, u32[]{:S(2)}) %collective-permute-start.7) | collective-permute-done | bytes 442400 | tf_op jit(solution)/shard_map/ppermute | solution.py:35
  117.4 3.4 %all-to-all-done.1 = bf16[32,16,384]{2,1,0:T(8,128)(2,1)S(1)} async-done(((bf16[32,16,384]{2,1,0:T(8,128)(2,1)}), bf16[32,16,384]{2,1,0:T(8,128)(2,1)S(1)}, u32[]{:S(2)}, u32[]{:S(2)}) %all-to-all-start.1) | async-done | bytes 393248 | tf_op jit(solution)/shard_map/all_to_all | solution.py:246
  121.6 3.2 %temporal.1 = bf16[512,128]{1,0:T(8,128)(2,1)} custom-call(bf16[512,384]{1,0:T(8,128)(2,1)} %bitcast.32), custom_call_target="tpu_custom_call" | custom-call | flops 140000000 | bytes 500000 | tf_op jit(solution)/shard_map/temporal/pallas_call | solution.py:254
  124.7 8.9 %all-to-all-start.2 = ((bf16[32,16,128]{2,1,0:T(8,128)(2,1)}), bf16[32,16,128]{2,1,0:T(8,128)(2,1)S(1)}, u32[]{:S(2)}, u32[]{:S(2)}) async-start(bf16[32,16,128]{2,1,0:T(8,128)(2,1)} %bitcast.36), calls=%async_computation.2 | async-start | bytes 262144 | tf_op jit(solution)/shard_map/all_to_all | solution.py:262
  134.3 8.5 %spatial.1 = bf16[512,128]{1,0:T(8,128)(2,1)} custom-call(s32[4]{0:T(128)} %pad_add_fusion.place, bf16[4,192,384]{2,1,0:T(8,128)(2,1)} %bitcast.31, bf16[4,192,384]{2,1,0:T(8,128)(2,1)} %copy-done.4, bf16[4,192,384]{2,1,0:T(8,128)(2,1)} %copy-done.5, bf16[2,192,384]{2,1,0:T(8,128)(2,1)} %copy-done.6, bf16[2,192,384]{2,1,0:T(8,128)(2,1)} %copy-done.7, ...), custom_call_target="tpu_custom_call" | custom-call | flops 1300000000 | bytes 6000000 | tf_op jit(solution)/shard_map/spatial/pallas_call | solution.py:265
  142.8 5.2 %all-to-all-done.2 = bf16[32,16,128]{2,1,0:T(8,128)(2,1)S(1)} async-done(((bf16[32,16,128]{2,1,0:T(8,128)(2,1)}), bf16[32,16,128]{2,1,0:T(8,128)(2,1)S(1)}, u32[]{:S(2)}, u32[]{:S(2)}) %all-to-all-start.2) | async-done | bytes 131104 | tf_op jit(solution)/shard_map/all_to_all | solution.py:262
  149.0 4.1 %collective-permute-start.9 = (bf16[2,512,128]{2,1,0:T(8,128)(2,1)S(1)}, bf16[2,512,128]{2,1,0:T(8,128)(2,1)S(1)}, u32[]{:S(2)}, u32[]{:S(2)}) collective-permute-start(bf16[2,512,128]{2,1,0:T(8,128)(2,1)S(1)} %get-tuple-element.44), channel_id=1, source_target_pairs={{0,4},{4,8},{8,12},{12,0},{1,5},{5,9},{9,13},{13,1},{2,6},{6,10},{... | collective-permute-start | bytes 786440 | tf_op jit(solution)/shard_map/ppermute | solution.py:31
  153.1 3.2 %collective-permute-start.10 = (bf16[2,512,128]{2,1,0:T(8,128)(2,1)S(1)}, bf16[2,512,128]{2,1,0:T(8,128)(2,1)S(1)}, u32[]{:S(2)}, u32[]{:S(2)}) collective-permute-start(bf16[2,512,128]{2,1,0:T(8,128)(2,1)S(1)} %get-tuple-element.44), channel_id=1, source_target_pairs={{0,12},{4,0},{8,4},{12,8},{1,13},{5,1},{9,5},{13,9},{2,14},{6,2},{... | collective-permute-start | bytes 786440 | tf_op jit(solution)/shard_map/ppermute | solution.py:31
  156.3 3.6 %collective-permute-start.11 = (bf16[2,512,128]{2,1,0:T(8,128)(2,1)S(1)}, bf16[2,512,128]{2,1,0:T(8,128)(2,1)S(1)}, u32[]{:S(2)}, u32[]{:S(2)}) collective-permute-start(bf16[2,512,128]{2,1,0:T(8,128)(2,1)S(1)} %get-tuple-element.44), channel_id=1, source_target_pairs={{0,8},{4,12},{8,0},{12,4},{1,9},{5,13},{9,1},{13,5},{2,10},{6,14},... | collective-permute-start | bytes 786440 | tf_op jit(solution)/shard_map/ppermute | solution.py:31
  160.2 5.7 %collective-permute-done.11 = bf16[2,512,128]{2,1,0:T(8,128)(2,1)S(1)} collective-permute-done((bf16[2,512,128]{2,1,0:T(8,128)(2,1)S(1)}, bf16[2,512,128]{2,1,0:T(8,128)(2,1)S(1)}, u32[]{:S(2)}, u32[]{:S(2)}) %collective-permute-start.11) | collective-permute-done | bytes 262176 | tf_op jit(solution)/shard_map/ppermute | solution.py:31
  166.1 9.2 %collective-permute-start.12 = (bf16[4,2,512,128]{3,2,1,0:T(8,128)(2,1)S(1)}, bf16[4,2,512,128]{3,2,1,0:T(8,128)(2,1)S(1)}, u32[]{:S(2)}, u32[]{:S(2)}) collective-permute-start(bf16[4,2,512,128]{3,2,1,0:T(8,128)(2,1)S(1)} %pad_maximum_fusion.heads), channel_id=1, source_target_pairs={{0,2},{2,0},{1,3},{3,1},{4,6},{6,4},{5,7},{7,5},{8,10},{10,8},{9,1... | collective-permute-start | bytes 3145736 | tf_op jit(solution)/shard_map/ppermute | solution.py:39
  175.3 2.4 %share.1 = f32[512,384]{1,0:T(8,128)S(1)} custom-call(s32[4]{0:T(128)S(1)} %copy-done.1, bf16[4,2,512,128]{3,2,1,0:T(8,128)(2,1)S(1)} %pad_maximum_fusion.heads, bf16[8,768,384]{2,1,0:T(8,128)(2,1)} %all-to-all-done.blocks_ref.w_out), custom_call_target="tpu_custom_call" | custom-call | flops 400000000 | bytes 4000000 | tf_op jit(solution)/shard_map/share/pallas_call | solution.py:284
  177.8 3.1 %mixed.1 = bf16[512,384]{1,0:T(8,128)(2,1)} custom-call(s32[4]{0:T(128)S(1)} %copy-done.1, bf16[4,2,512,128]{3,2,1,0:T(8,128)(2,1)S(1)} %collective-permute-done.12.heads, bf16[8,768,384]{2,1,0:T(8,128)(2,1)} %all-to-all-done.blocks_ref.w_out, f32[512,384]{1,0:T(8,128)S(1)} %share.1, bf16[512,384]{1,0:T(8,128)(2,1)S(1)} %copy-done, f32[24,128]{1,0:T(8,128)S(1)} %bitcast.26), custom_call_target="tpu_custom_call" | custom-call | flops 400000000 | bytes 5000000 | tf_op jit(solution)/shard_map/mixed/pallas_call | solution.py:294
  (60 shorter events, 5.6 us)
Async XLA Ops:
  3.9 75.9 %all-to-all-start = ((bf16[8,768,384]{2,1,0:T(8,128)(2,1)}), bf16[8,768,384]{2,1,0:T(8,128)(2,1)}, u32[]{:S(2)}, u32[]{:S(2)}) async-start(bf16[8,768,384]{2,1,0:T(8,128)(2,1)} %sent.1), calls=%async_computation | async-start | bytes 9437184 | tf_op jit(solution)/shard_map/all_to_all | solution.py:203
  43.3 42.2 %copy-start.3 = (bf16[768,384]{1,0:T(8,128)(2,1)}, bf16[768,384]{1,0:T(8,128)(2,1)S(1)}, u32[]{:S(2)}) copy-start(bf16[768,384]{1,0:T(8,128)(2,1)S(1)} %all-gather) | copy-start | bytes 1769476
  43.3 30.2 %collective-permute-start = (bf16[4,192,384]{2,1,0:T(8,128)(2,1)S(1)}, bf16[4,192,384]{2,1,0:T(8,128)(2,1)S(1)}, u32[]{:S(2)}, u32[]{:S(2)}) collective-permute-start(bf16[4,192,384]{2,1,0:T(8,128)(2,1)S(1)} %bitcast.27), channel_id=1, source_target_pairs={{0,16},{16,32},{32,48},{48,64},{64,80},{80,96},{96,112},{112,128},... | collective-permute-start | bytes 1769480 | tf_op jit(solution)/shard_map/ppermute | solution.py:27
  45.2 28.3 %collective-permute-start.1 = (bf16[4,192,384]{2,1,0:T(8,128)(2,1)S(1)}, bf16[4,192,384]{2,1,0:T(8,128)(2,1)S(1)}, u32[]{:S(2)}, u32[]{:S(2)}) collective-permute-start(bf16[4,192,384]{2,1,0:T(8,128)(2,1)S(1)} %bitcast.28), channel_id=1, source_target_pairs={{0,240},{16,0},{32,16},{48,32},{64,48},{80,64},{96,80},{112,96},{1... | collective-permute-start | bytes 1769480 | tf_op jit(solution)/shard_map/ppermute | solution.py:27
  50.0 23.6 %collective-permute-start.4 = (bf16[4,192,384]{2,1,0:T(8,128)(2,1)S(1)}, bf16[4,192,384]{2,1,0:T(8,128)(2,1)S(1)}, u32[]{:S(2)}, u32[]{:S(2)}) collective-permute-start(bf16[4,192,384]{2,1,0:T(8,128)(2,1)S(1)} %bitcast.29), channel_id=1, source_target_pairs={{0,256},{256,1},{1,257},{257,0},{2,258},{258,3},{3,259},{259,2},{4... | collective-permute-start | bytes 1769480 | tf_op jit(solution)/shard_map/ppermute | solution.py:35
  53.3 17.6 %collective-permute-start.2 = (bf16[2,192,384]{2,1,0:T(8,128)(2,1)S(1)}, bf16[2,192,384]{2,1,0:T(8,128)(2,1)S(1)}, u32[]{:S(2)}, u32[]{:S(2)}) collective-permute-start(bf16[2,192,384]{2,1,0:T(8,128)(2,1)S(1)} %bitcast.40), channel_id=1, source_target_pairs={{0,32},{16,48},{32,64},{48,80},{64,96},{80,112},{96,128},{112,144}... | collective-permute-start | bytes 884744 | tf_op jit(solution)/shard_map/ppermute | solution.py:27
  55.2 18.3 %collective-permute-start.3 = (bf16[2,192,384]{2,1,0:T(8,128)(2,1)S(1)}, bf16[2,192,384]{2,1,0:T(8,128)(2,1)S(1)}, u32[]{:S(2)}, u32[]{:S(2)}) collective-permute-start(bf16[2,192,384]{2,1,0:T(8,128)(2,1)S(1)} %bitcast.39), channel_id=1, source_target_pairs={{0,224},{16,240},{32,0},{48,16},{64,32},{80,48},{96,64},{112,80},{... | collective-permute-start | bytes 884744 | tf_op jit(solution)/shard_map/ppermute | solution.py:27
  70.9 14.7 %copy-start.6 = (bf16[2,192,384]{2,1,0:T(8,128)(2,1)}, bf16[2,192,384]{2,1,0:T(8,128)(2,1)S(1)}, u32[]{:S(2)}) copy-start(bf16[2,192,384]{2,1,0:T(8,128)(2,1)S(1)} %collective-permute-done.2.refs_3_) | copy-start | bytes 884740
  73.5 12.0 %copy-start.7 = (bf16[2,192,384]{2,1,0:T(8,128)(2,1)}, bf16[2,192,384]{2,1,0:T(8,128)(2,1)S(1)}, u32[]{:S(2)}) copy-start(bf16[2,192,384]{2,1,0:T(8,128)(2,1)S(1)} %collective-permute-done.3.refs_4_) | copy-start | bytes 884740
  73.5 12.0 %copy-start.4 = (bf16[4,192,384]{2,1,0:T(8,128)(2,1)}, bf16[4,192,384]{2,1,0:T(8,128)(2,1)S(1)}, u32[]{:S(2)}) copy-start(bf16[4,192,384]{2,1,0:T(8,128)(2,1)S(1)} %collective-permute-done.refs_1_) | copy-start | bytes 1769476
  73.5 12.0 %copy-start.5 = (bf16[4,192,384]{2,1,0:T(8,128)(2,1)}, bf16[4,192,384]{2,1,0:T(8,128)(2,1)S(1)}, u32[]{:S(2)}) copy-start(bf16[4,192,384]{2,1,0:T(8,128)(2,1)S(1)} %collective-permute-done.1.refs_2_) | copy-start | bytes 1769476
  73.6 12.0 %copy-start.8 = (bf16[4,192,384]{2,1,0:T(8,128)(2,1)}, bf16[4,192,384]{2,1,0:T(8,128)(2,1)S(1)}, u32[]{:S(2)}) copy-start(bf16[4,192,384]{2,1,0:T(8,128)(2,1)S(1)} %collective-permute-done.4.refs_5_) | copy-start | bytes 1769476
  73.7 11.9 %collective-permute-start.6 = (bf16[6,96,384]{2,1,0:T(8,128)(2,1)S(1)}, bf16[6,96,384]{2,1,0:T(8,128)(2,1)}, u32[]{:S(2)}, u32[]{:S(2)}) collective-permute-start(bf16[6,96,384]{2,1,0:T(8,128)(2,1)S(1)} %pad_maximum_fusion.2), channel_id=1, source_target_pairs={{0,257},{256,0},{1,256},{257,1},{2,259},{258,2},{3,258},{259,3},{4... | collective-permute-start | bytes 1327112 | tf_op jit(solution)/shard_map/ppermute | solution.py:35
  76.7 10.6 %collective-permute-start.5 = (bf16[6,96,384]{2,1,0:T(8,128)(2,1)}, bf16[6,96,384]{2,1,0:T(8,128)(2,1)}, u32[]{:S(2)}, u32[]{:S(2)}) collective-permute-start(bf16[6,96,384]{2,1,0:T(8,128)(2,1)} %pad_maximum_fusion.1), channel_id=1, source_target_pairs={{0,256},{256,1},{1,257},{257,0},{2,258},{258,3},{3,259},{259,2},{4... | collective-permute-start | bytes 1327112 | tf_op jit(solution)/shard_map/ppermute | solution.py:35
  85.6 48.0 %copy-start.13 = (s32[8,4]{0,1:T(4,128)S(1)}, s32[8,4]{0,1:T(4,128)}, u32[]{:S(2)}) copy-start(s32[8,4]{0,1:T(4,128)} %param.13) | copy-start | bytes 388
  85.6 16.3 %slice-start.1 = ((bf16[4,192,384]{2,1,0:T(8,128)(2,1)}), bf16[4,96,384]{2,1,0:T(8,128)(2,1)S(1)}, s32[]{:S(2)}) async-start(bf16[4,192,384]{2,1,0:T(8,128)(2,1)} %copy-done.5), calls=%async_computation.4 | async-start | bytes 589824 | tf_op jit(solution)/shard_map/slice | solution.py:214
  85.6 16.3 %slice-start.3 = ((bf16[2,192,384]{2,1,0:T(8,128)(2,1)}), bf16[2,96,384]{2,1,0:T(8,128)(2,1)S(1)}, s32[]{:S(2)}) async-start(bf16[2,192,384]{2,1,0:T(8,128)(2,1)} %copy-done.7), calls=%async_computation.6 | async-start | bytes 294912 | tf_op jit(solution)/shard_map/slice | solution.py:214
  85.6 21.1 %slice-start = ((bf16[4,192,384]{2,1,0:T(8,128)(2,1)}), bf16[4,96,384]{2,1,0:T(8,128)(2,1)S(1)}, s32[]{:S(2)}) async-start(bf16[4,192,384]{2,1,0:T(8,128)(2,1)} %copy-done.4), calls=%async_computation.3 | async-start | bytes 589824 | tf_op jit(solution)/shard_map/slice | solution.py:213
  85.6 21.1 %slice-start.2 = ((bf16[2,192,384]{2,1,0:T(8,128)(2,1)}), bf16[2,96,384]{2,1,0:T(8,128)(2,1)S(1)}, s32[]{:S(2)}) async-start(bf16[2,192,384]{2,1,0:T(8,128)(2,1)} %copy-done.6), calls=%async_computation.5 | async-start | bytes 294912 | tf_op jit(solution)/shard_map/slice | solution.py:213
  93.2 27.6 %all-to-all-start.1 = ((bf16[32,16,384]{2,1,0:T(8,128)(2,1)}), bf16[32,16,384]{2,1,0:T(8,128)(2,1)S(1)}, u32[]{:S(2)}, u32[]{:S(2)}) async-start(bf16[32,16,384]{2,1,0:T(8,128)(2,1)} %bitcast.33), calls=%async_computation.1 | async-start | bytes 786432 | tf_op jit(solution)/shard_map/all_to_all | solution.py:246
  102.0 10.2 %collective-permute-start.8 = (bf16[6,96,384]{2,1,0:T(8,128)(2,1)S(1)}, bf16[6,96,384]{2,1,0:T(8,128)(2,1)S(1)}, u32[]{:S(2)}, u32[]{:S(2)}) collective-permute-start(bf16[6,96,384]{2,1,0:T(8,128)(2,1)S(1)} %pad_maximum_fusion.4), channel_id=1, source_target_pairs={{0,257},{256,0},{1,256},{257,1},{2,259},{258,2},{3,258},{259,3},{4... | collective-permute-start | bytes 1327112 | tf_op jit(solution)/shard_map/ppermute | solution.py:35
  106.8 10.6 %collective-permute-start.7 = (bf16[6,96,384]{2,1,0:T(8,128)(2,1)S(1)}, bf16[6,96,384]{2,1,0:T(8,128)(2,1)S(1)}, u32[]{:S(2)}, u32[]{:S(2)}) collective-permute-start(bf16[6,96,384]{2,1,0:T(8,128)(2,1)S(1)} %pad_maximum_fusion.3), channel_id=1, source_target_pairs={{0,256},{256,1},{1,257},{257,0},{2,258},{258,3},{3,259},{259,2},{4... | collective-permute-start | bytes 1327112 | tf_op jit(solution)/shard_map/ppermute | solution.py:35
  112.2 22.0 %copy-start.11 = (bf16[6,96,384]{2,1,0:T(8,128)(2,1)}, bf16[6,96,384]{2,1,0:T(8,128)(2,1)S(1)}, u32[]{:S(2)}) copy-start(bf16[6,96,384]{2,1,0:T(8,128)(2,1)S(1)} %collective-permute-done.8.refs_7_) | copy-start | bytes 1327108
  117.4 16.9 %copy-start.12 = (bf16[6,96,384]{2,1,0:T(8,128)(2,1)}, bf16[6,96,384]{2,1,0:T(8,128)(2,1)S(1)}, u32[]{:S(2)}) copy-start(bf16[6,96,384]{2,1,0:T(8,128)(2,1)S(1)} %collective-permute-done.7.refs_6_) | copy-start | bytes 1327108
  124.7 23.3 %all-to-all-start.2 = ((bf16[32,16,128]{2,1,0:T(8,128)(2,1)}), bf16[32,16,128]{2,1,0:T(8,128)(2,1)S(1)}, u32[]{:S(2)}, u32[]{:S(2)}) async-start(bf16[32,16,128]{2,1,0:T(8,128)(2,1)} %bitcast.36), calls=%async_computation.2 | async-start | bytes 262144 | tf_op jit(solution)/shard_map/all_to_all | solution.py:262
  134.3 41.0 %copy-start.1 = (s32[4]{0:T(128)S(1)}, s32[4]{0:T(128)}, u32[]{:S(2)}) copy-start(s32[4]{0:T(128)} %pad_add_fusion.place) | copy-start | bytes 52
  148.0 29.8 %copy-start = (bf16[512,384]{1,0:T(8,128)(2,1)S(1)}, bf16[512,384]{1,0:T(8,128)(2,1)}, u32[]{:S(2)}) copy-start(bf16[512,384]{1,0:T(8,128)(2,1)} %hidden.3) | copy-start | bytes 1179652
  148.0 29.8 %copy-start.2 = (f32[3072]{0:T(1024)S(1)}, f32[3072]{0:T(1024)}, u32[]{:S(2)}) copy-start(f32[3072]{0:T(1024)} %param.10) | copy-start | bytes 36868
  149.0 10.9 %collective-permute-start.9 = (bf16[2,512,128]{2,1,0:T(8,128)(2,1)S(1)}, bf16[2,512,128]{2,1,0:T(8,128)(2,1)S(1)}, u32[]{:S(2)}, u32[]{:S(2)}) collective-permute-start(bf16[2,512,128]{2,1,0:T(8,128)(2,1)S(1)} %get-tuple-element.44), channel_id=1, source_target_pairs={{0,4},{4,8},{8,12},{12,0},{1,5},{5,9},{9,13},{13,1},{2,6},{6,10},{... | collective-permute-start | bytes 786440 | tf_op jit(solution)/shard_map/ppermute | solution.py:31
  153.1 7.1 %collective-permute-start.10 = (bf16[2,512,128]{2,1,0:T(8,128)(2,1)S(1)}, bf16[2,512,128]{2,1,0:T(8,128)(2,1)S(1)}, u32[]{:S(2)}, u32[]{:S(2)}) collective-permute-start(bf16[2,512,128]{2,1,0:T(8,128)(2,1)S(1)} %get-tuple-element.44), channel_id=1, source_target_pairs={{0,12},{4,0},{8,4},{12,8},{1,13},{5,1},{9,5},{13,9},{2,14},{6,2},{... | collective-permute-start | bytes 786440 | tf_op jit(solution)/shard_map/ppermute | solution.py:31
  156.3 9.6 %collective-permute-start.11 = (bf16[2,512,128]{2,1,0:T(8,128)(2,1)S(1)}, bf16[2,512,128]{2,1,0:T(8,128)(2,1)S(1)}, u32[]{:S(2)}, u32[]{:S(2)}) collective-permute-start(bf16[2,512,128]{2,1,0:T(8,128)(2,1)S(1)} %get-tuple-element.44), channel_id=1, source_target_pairs={{0,8},{4,12},{8,0},{12,4},{1,9},{5,13},{9,1},{13,5},{2,10},{6,14},... | collective-permute-start | bytes 786440 | tf_op jit(solution)/shard_map/ppermute | solution.py:31
  166.1 11.7 %collective-permute-start.12 = (bf16[4,2,512,128]{3,2,1,0:T(8,128)(2,1)S(1)}, bf16[4,2,512,128]{3,2,1,0:T(8,128)(2,1)S(1)}, u32[]{:S(2)}, u32[]{:S(2)}) collective-permute-start(bf16[4,2,512,128]{3,2,1,0:T(8,128)(2,1)S(1)} %pad_maximum_fusion.heads), channel_id=1, source_target_pairs={{0,2},{2,0},{1,3},{3,1},{4,6},{6,4},{5,7},{7,5},{8,10},{10,8},{9,1... | collective-permute-start | bytes 3145736 | tf_op jit(solution)/shard_map/ppermute | solution.py:39
  (2 other events, 12.3 us)

commit v5 on v4

--- a/solution.py
+++ b/solution.py
@@ -99,22 +99,20 @@
 
 
 def fetch(kind, place, pieces, weight, sem):
-    own, below, above, far_below, far_above, near_own, near_low, near_high = pieces
-    own, below, above, far_below, far_above, near_own = (
-        piece.at[:, pl.ds(kind * 96, 96)] for piece in (own, below, above, far_below, far_above, near_own)
-    )
+    own, below, above, far_first, far_second, near_own, near_low, near_high = pieces
+    own, below, above, near_own = (piece.at[:, pl.ds(kind * 96, 96)] for piece in (own, below, above, near_own))
     here, there = place[0] * 4, (1 - place[0]) * 4
     parts = (
         (own, here, 4, 0),
         (below, here, 4, 3),
         (above, here, 4, 1),
-        (far_below, here, 2, 2),
-        (far_above, here + 2, 2, 2),
+        (far_first, here, 2, 2),
+        (far_second, here + 2, 2, 2),
         (near_own, there, 4, 0),
         (near_low.at[0:4], there, 4, 3),
-        (near_low.at[4:6], there, 2, 2),
+        (near_low.at[4:6], there + 2, 2, 2),
         (near_high.at[0:4], there, 4, 1),
-        (near_high.at[4:6], there + 2, 2, 2),
+        (near_high.at[4:6], there, 2, 2),
     )
     copies = [
         pltpu.make_async_copy(part, weight.at[pl.ds(start, count), (place[1] + ahead) % 4], sem.at[i])
@@ -147,7 +145,7 @@
 
     def tile_of(step, _):
         rows = pl.ds(pl.multiple_of(step * TILE, TILE), TILE)
-        chosen = [pl.ds(pl.multiple_of(window[step, i] * TILE, TILE), TILE) for i in range(WIN)]
+        chosen = [pl.ds(pl.multiple_of(window[i, step] * TILE, TILE), TILE) for i in range(WIN)]
         keys = jnp.concatenate([projected[there, 128:256] for there in chosen], 0)
         values = jnp.concatenate([projected[there, 256:384] for there in chosen], 0)
         weights = softmax(scores_of(projected[rows, 0:128], keys))
@@ -204,16 +202,18 @@
 
     own = lax.all_gather(shards, "zh", axis=0)
     below, above = along_z(own, 1), along_z(own, -1)
-    far_below, far_above = along_z(own[:2], 2), along_z(own[2:], -2)
+    spatial_rows, temporal_rows = slice(0, 96), slice(96, 192)
+    far_below, far_above = along_z(own[:2, temporal_rows], 2), along_z(own[2:, temporal_rows], -2)
     near_own = along_y(own, 1)
-    place, window_tiles, *weights = tie(place, window_tiles, own, below, above, far_below, far_above, near_own)
-
-    def near(kind, own, below, above, far_below, far_above, near_own):
-        rows = slice(kind * 96, kind * 96 + 96)
-        low = along_y(jnp.concatenate([below[:, rows], far_below[:, rows]], 0), 1)
-        return low, along_y(jnp.concatenate([above[:, rows], far_above[:, rows]], 0), -1)
-
-    temporal_weights = tuple(weights) + near(1, *weights)
+    place, own, below, above, far_below, near_own = tie(place, own, below, above, far_below, near_own)
+    far_spatial = along_z(own[:, spatial_rows], 2)
+
+    def near(rows, first, second):
+        high = along_y(jnp.concatenate([above[:, rows], first], 0), -1)
+        return along_y(jnp.concatenate([below[:, rows], second], 0), 1), high
+
+    near_temporal = near(temporal_rows, far_below, far_above)
+    temporal_weights = (own, below, above, far_below, far_above, near_own, *near_temporal)
 
     normed = pl.pallas_call(
         norm_kernel,
@@ -243,13 +243,14 @@
         name="temporal_project",
         **params(1_200_000_000, 6_000_000),
     )(place, *temporal_weights, normed)
+    projected, far_spatial = tie(projected, far_spatial)
     by_position = lax.all_to_all(
         projected.reshape(32, 16, 384), ("yl", "zh", "zl"), split_axis=0, concat_axis=0, tiled=True
     ).reshape(512, 384)
 
-    *weights, _ = tie(*weights, projected)
-    by_position, *near_spatial = tie(by_position, *near(0, *weights))
-    spatial_weights = tuple(weights) + tuple(near_spatial)
+    below, above, far_spatial, _ = tie(below, above, far_spatial, projected)
+    by_position, *near_spatial = tie(by_position, *near(spatial_rows, far_spatial[:2], far_spatial[2:]))
+    spatial_weights = (own, below, above, far_spatial[:2], far_spatial[2:], near_own, *near_spatial)
 
     temporal = pl.pallas_call(
         temporal_kernel,
@@ -276,7 +277,7 @@
         ],
         name="spatial",
         **params(1_300_000_000, 6_000_000),
-    )(place, *spatial_weights, window_tiles, normed)
+    )(place, *spatial_weights, window_tiles.T, normed)
 
     heads = jnp.stack([spatial, temporal])
     mine = jnp.stack([heads, along_x(heads, 1), along_x(heads, -1), along_x(heads, 2)])

time: 182 us -> 180 us (0.989)
  waiting for transfers between devices: 37.1 us -> 26 us
  starting transfers between devices: 78.4 us -> 84.5 us
  local copies, waits for them, and re-layouts: 2.51 us -> 4.98 us
    ppermute x4 -> x5, waiting for transfers between devices: 12.2 us -> 3.62 us  [along_z(): lax.ppermute(value, ('zh', 'zl'), [(i, (i + step) % 16) for i in range(16)])]
    ppermute x1, starting transfers between devices: 9.21 us -> 12.9 us  [other_core(): return lax.ppermute(value, 'c', [(0, 1), (1, 0)])]
    ppermute x4 -> x5, starting transfers between devices: 14.1 us -> 16 us  [along_z(): lax.ppermute(value, ('zh', 'zl'), [(i, (i + step) % 16) for i in range(16)])]
  transfers between devices with their start and end apart: 16 -> 17, of which waited for: 9 -> 8; matrix products, arithmetic and copies ran while one was open for 2% -> 3% of each run, Pallas kernels for 9% -> 13%
where the time goes in v5:
time: 180 us; the launch traced here: 179 us
  starting transfers between devices  84.5 us (47%)
  Pallas kernels  32.8 us (18%)
  blocking collectives  27 us (15%)
  waiting for transfers between devices  26 us (14%)
  local copies, waits for them, and re-layouts  4.98 us (3%)
  other arithmetic  3.64 us (2%)
    all_gather x1, blocking collectives, body(): own = lax.all_gather(shards, 'zh', axis=0)  27 us
    ppermute x5, starting transfers between devices, along_y(): lax.ppermute(value, ('yl', 'dp'), [(Y_PLACE[i], Y_PLACE[(i + step) % 4])...  16.3 us
    ppermute x5, starting transfers between devices, along_z(): lax.ppermute(value, ('zh', 'zl'), [(i, (i + step) % 16) for i in range(16)])  16 us
    ppermute x1, starting transfers between devices, other_core(): return lax.ppermute(value, 'c', [(0, 1), (1, 0)])  12.9 us
    all_to_all x1, starting transfers between devices, body(): lax.all_to_all(sent, ('x', 'c'), split_axis=0, concat_axis=0, tiled=True)  11.5 us
    ppermute x3, starting transfers between devices, along_x(): return lax.ppermute(value, 'x', [(i, (i + step) % 4) for i in range(4)])  11.3 us
    all_to_all x1, starting transfers between devices, body(): lax.all_to_all(temporal.reshape(32, 16, HD), ('yl', 'zh', 'zl'), split_ax...  9.45 us
    ppermute x5, waiting for transfers between devices, along_y(): lax.ppermute(value, ('yl', 'dp'), [(Y_PLACE[i], Y_PLACE[(i + step) % 4])...  8.78 us
  transfers between devices with their start and end apart: 17, of which 8 were waited for; matrix products, arithmetic and copies ran while one was open for 3% of the time, Pallas kernels for 13%

profile of v5, /device:TPU:1, one launch (start us, length us, event | category | flops | bytes accessed | tf_op | source)
XLA Modules:
  0.0 179.3 jit_solution(10301686762195876214)
XLA Ops:
  0.0 3.9 %sent.1 = bf16[8,768,384]{2,1,0:T(8,128)(2,1)} custom-call(bf16[512,384]{1,0:T(8,128)(2,1)} %hidden.3, bf16[2,128,3072]{2,1,0:T(8,128)(2,1)} %w_out.1), custom_call_target="tpu_custom_call" | custom-call | bytes 7000000 | tf_op jit(solution)/shard_map/sent/pallas_call | solution.py:192
  3.9 11.5 %all-to-all-start = ((bf16[8,768,384]{2,1,0:T(8,128)(2,1)}), bf16[8,768,384]{2,1,0:T(8,128)(2,1)}, u32[]{:S(2)}, u32[]{:S(2)}) async-start(bf16[8,768,384]{2,1,0:T(8,128)(2,1)} %sent.1), calls=%async_computation | async-start | bytes 9437184 | tf_op jit(solution)/shard_map/all_to_all | solution.py:201
  16.4 27.0 %all-gather = bf16[768,384]{1,0:T(8,128)(2,1)S(1)} all-gather(bf16[192,384]{1,0:T(8,128)(2,1)S(1)} %pad_maximum_fusion.6), channel_id=2, replica_groups=mesh['yl'=2,'zh'=4,'zl'=4,'x'=4,'c'=2,'dp'=2] {'zh'}, dimensions={0}, use_global_device_ids=true | all-gather | bytes 737280 | tf_op jit(solution)/shard_map/all_gather | solution.py:203
  43.3 1.9 %collective-permute-start = (bf16[4,192,384]{2,1,0:T(8,128)(2,1)S(1)}, bf16[4,192,384]{2,1,0:T(8,128)(2,1)S(1)}, u32[]{:S(2)}, u32[]{:S(2)}) collective-permute-start(bf16[4,192,384]{2,1,0:T(8,128)(2,1)S(1)} %bitcast.26), channel_id=1, source_target_pairs={{0,16},{16,32},{32,48},{48,64},{64,80},{80,96},{96,112},{112,128},... | collective-permute-start | bytes 1769480 | tf_op jit(solution)/shard_map/ppermute | solution.py:27
  45.2 4.8 %collective-permute-start.1 = (bf16[4,192,384]{2,1,0:T(8,128)(2,1)S(1)}, bf16[4,192,384]{2,1,0:T(8,128)(2,1)S(1)}, u32[]{:S(2)}, u32[]{:S(2)}) collective-permute-start(bf16[4,192,384]{2,1,0:T(8,128)(2,1)S(1)} %bitcast.27), channel_id=1, source_target_pairs={{0,240},{16,0},{32,16},{48,32},{64,48},{80,64},{96,80},{112,96},{1... | collective-permute-start | bytes 1769480 | tf_op jit(solution)/shard_map/ppermute | solution.py:27
  50.0 3.2 %collective-permute-start.3 = (bf16[4,192,384]{2,1,0:T(8,128)(2,1)S(1)}, bf16[4,192,384]{2,1,0:T(8,128)(2,1)S(1)}, u32[]{:S(2)}, u32[]{:S(2)}) collective-permute-start(bf16[4,192,384]{2,1,0:T(8,128)(2,1)S(1)} %bitcast.28), channel_id=1, source_target_pairs={{0,256},{256,1},{1,257},{257,0},{2,258},{258,3},{3,259},{259,2},{4... | collective-permute-start | bytes 1769480 | tf_op jit(solution)/shard_map/ppermute | solution.py:35
  53.3 1.9 %collective-permute-start.2 = (bf16[2,96,384]{2,1,0:T(8,128)(2,1)S(1)}, bf16[2,96,384]{2,1,0:T(8,128)(2,1)S(1)}, u32[]{:S(2)}, u32[]{:S(2)}) collective-permute-start(bf16[2,96,384]{2,1,0:T(8,128)(2,1)S(1)} %get-tuple-element.36), channel_id=1, source_target_pairs={{0,32},{16,48},{32,64},{48,80},{64,96},{80,112},{96,128},{112,144}... | collective-permute-start | bytes 442376 | tf_op jit(solution)/shard_map/ppermute | solution.py:27
  55.2 5.5 %collective-permute-start.4 = (bf16[2,96,384]{2,1,0:T(8,128)(2,1)S(1)}, bf16[2,96,384]{2,1,0:T(8,128)(2,1)S(1)}, u32[]{:S(2)}, u32[]{:S(2)}) collective-permute-start(bf16[2,96,384]{2,1,0:T(8,128)(2,1)S(1)} %get-tuple-element.35), channel_id=1, source_target_pairs={{0,224},{16,240},{32,0},{48,16},{64,32},{80,48},{96,64},{112,80},{... | collective-permute-start | bytes 442376 | tf_op jit(solution)/shard_map/ppermute | solution.py:27
  61.3 3.6 %collective-permute-done.2.refs_3_ = bf16[2,96,384]{2,1,0:T(8,128)(2,1)S(1)} collective-permute-done((bf16[2,96,384]{2,1,0:T(8,128)(2,1)S(1)}, bf16[2,96,384]{2,1,0:T(8,128)(2,1)S(1)}, u32[]{:S(2)}, u32[]{:S(2)}) %collective-permute-start.2) | collective-permute-done | bytes 147488 | tf_op jit(solution)/shard_map/ppermute | solution.py:27
  65.9 4.3 %collective-permute-start.6 = (bf16[6,96,384]{2,1,0:T(8,128)(2,1)}, bf16[6,96,384]{2,1,0:T(8,128)(2,1)S(1)}, u32[]{:S(2)}, u32[]{:S(2)}) collective-permute-start(bf16[6,96,384]{2,1,0:T(8,128)(2,1)} %pad_maximum_fusion.2), channel_id=1, source_target_pairs={{0,257},{256,0},{1,256},{257,1},{2,259},{258,2},{3,258},{259,3},{4... | collective-permute-start | bytes 1327112 | tf_op jit(solution)/shard_map/ppermute | solution.py:35
  71.1 1.9 %collective-permute-start.5 = (bf16[6,96,384]{2,1,0:T(8,128)(2,1)}, bf16[6,96,384]{2,1,0:T(8,128)(2,1)S(1)}, u32[]{:S(2)}, u32[]{:S(2)}) collective-permute-start(bf16[6,96,384]{2,1,0:T(8,128)(2,1)} %pad_maximum_fusion.1), channel_id=1, source_target_pairs={{0,256},{256,1},{1,257},{257,0},{2,258},{258,3},{3,259},{259,2},{4... | collective-permute-start | bytes 1327112 | tf_op jit(solution)/shard_map/ppermute | solution.py:35
  73.8 1.9 %collective-permute-start.7 = (bf16[4,96,384]{2,1,0:T(8,128)(2,1)}, bf16[4,96,384]{2,1,0:T(8,128)(2,1)}, u32[]{:S(2)}, u32[]{:S(2)}) collective-permute-start(bf16[4,96,384]{2,1,0:T(8,128)(2,1)} %slice.41), channel_id=1, source_target_pairs={{0,32},{16,48},{32,64},{48,80},{64,96},{80,112},{96,128},{112,144}... | collective-permute-start | bytes 884744 | tf_op jit(solution)/shard_map/ppermute | solution.py:27
  75.7 5.6 %norm.1.refs_8_.refs_9_ = bf16[512,3072]{1,0:T(8,128)(2,1)} custom-call(bf16[8,768,384]{2,1,0:T(8,128)(2,1)} %all-to-all-done.blocks_ref.w_out, f32[24,128]{1,0:T(8,128)} %bitcast.43, f32[24,128]{1,0:T(8,128)} %bitcast.44), custom_call_target="tpu_custom_call" | custom-call | flops 20000000 | bytes 6000000 | tf_op jit(solution)/shard_map/norm/pallas_call | solution.py:218
  83.0 6.1 %temporal_project.1 = bf16[512,384]{1,0:T(8,128)(2,1)} custom-call(s32[4]{0:T(128)} %pad_add_fusion.place, bf16[4,192,384]{2,1,0:T(8,128)(2,1)} %bitcast.31, bf16[4,192,384]{2,1,0:T(8,128)(2,1)} %copy-done.4, bf16[4,192,384]{2,1,0:T(8,128)(2,1)} %copy-done.5, bf16[2,96,384]{2,1,0:T(8,128)(2,1)} %copy-done.10, bf16[2,96,384]{2,1,0:T(8,128)(2,1)} %copy-done.11, ...), custom_call_target="tpu_custom_call" | custom-call | flops 1200000000 | bytes 6000000 | tf_op jit(solution)/shard_map/temporal_project/pallas_call | solution.py:232
  89.1 7.1 %all-to-all-start.1 = ((bf16[32,16,384]{2,1,0:T(8,128)(2,1)}), bf16[32,16,384]{2,1,0:T(8,128)(2,1)S(1)}, u32[]{:S(2)}, u32[]{:S(2)}) async-start(bf16[32,16,384]{2,1,0:T(8,128)(2,1)} %bitcast.33), calls=%async_computation.1 | async-start | bytes 786432 | tf_op jit(solution)/shard_map/all_to_all | solution.py:247
  96.2 1.0 fusion.2
  97.3 4.9 %collective-permute-start.9 = (bf16[6,96,384]{2,1,0:T(8,128)(2,1)S(1)}, bf16[6,96,384]{2,1,0:T(8,128)(2,1)S(1)}, u32[]{:S(2)}, u32[]{:S(2)}) collective-permute-start(bf16[6,96,384]{2,1,0:T(8,128)(2,1)S(1)} %pad_maximum_fusion.4), channel_id=1, source_target_pairs={{0,257},{256,0},{1,256},{257,1},{2,259},{258,2},{3,258},{259,3},{4... | collective-permute-start | bytes 1327112 | tf_op jit(solution)/shard_map/ppermute | solution.py:35
  102.3 1.9 %collective-permute-start.8 = (bf16[6,96,384]{2,1,0:T(8,128)(2,1)S(1)}, bf16[6,96,384]{2,1,0:T(8,128)(2,1)S(1)}, u32[]{:S(2)}, u32[]{:S(2)}) collective-permute-start(bf16[6,96,384]{2,1,0:T(8,128)(2,1)S(1)} %pad_maximum_fusion.3), channel_id=1, source_target_pairs={{0,256},{256,1},{1,257},{257,0},{2,258},{258,3},{3,259},{259,2},{4... | collective-permute-start | bytes 1327112 | tf_op jit(solution)/shard_map/ppermute | solution.py:35
  104.3 3.6 %collective-permute-done.9.refs_7_ = bf16[6,96,384]{2,1,0:T(8,128)(2,1)S(1)} collective-permute-done((bf16[6,96,384]{2,1,0:T(8,128)(2,1)S(1)}, bf16[6,96,384]{2,1,0:T(8,128)(2,1)S(1)}, u32[]{:S(2)}, u32[]{:S(2)}) %collective-permute-start.9) | collective-permute-done | bytes 442400 | tf_op jit(solution)/shard_map/ppermute | solution.py:35
  107.9 5.0 %collective-permute-done.8.refs_6_ = bf16[6,96,384]{2,1,0:T(8,128)(2,1)S(1)} collective-permute-done((bf16[6,96,384]{2,1,0:T(8,128)(2,1)S(1)}, bf16[6,96,384]{2,1,0:T(8,128)(2,1)S(1)}, u32[]{:S(2)}, u32[]{:S(2)}) %collective-permute-start.8) | collective-permute-done | bytes 442400 | tf_op jit(solution)/shard_map/ppermute | solution.py:35
  112.9 2.2 %all-to-all-done.1 = bf16[32,16,384]{2,1,0:T(8,128)(2,1)S(1)} async-done(((bf16[32,16,384]{2,1,0:T(8,128)(2,1)}), bf16[32,16,384]{2,1,0:T(8,128)(2,1)S(1)}, u32[]{:S(2)}, u32[]{:S(2)}) %all-to-all-start.1) | async-done | bytes 393248 | tf_op jit(solution)/shard_map/all_to_all | solution.py:247
  115.8 3.2 %temporal.1 = bf16[512,128]{1,0:T(8,128)(2,1)} custom-call(bf16[512,384]{1,0:T(8,128)(2,1)} %bitcast.34), custom_call_target="tpu_custom_call" | custom-call | flops 140000000 | bytes 500000 | tf_op jit(solution)/shard_map/temporal/pallas_call | solution.py:255
  119.0 9.4 %all-to-all-start.2 = ((bf16[32,16,128]{2,1,0:T(8,128)(2,1)}), bf16[32,16,128]{2,1,0:T(8,128)(2,1)S(1)}, u32[]{:S(2)}, u32[]{:S(2)}) async-start(bf16[32,16,128]{2,1,0:T(8,128)(2,1)} %bitcast.37), calls=%async_computation.2 | async-start | bytes 262144 | tf_op jit(solution)/shard_map/all_to_all | solution.py:263
  128.5 8.5 %spatial.1 = bf16[512,128]{1,0:T(8,128)(2,1)} custom-call(s32[4]{0:T(128)} %pad_add_fusion.place, bf16[4,192,384]{2,1,0:T(8,128)(2,1)} %bitcast.32, bf16[4,192,384]{2,1,0:T(8,128)(2,1)} %copy-done.4, bf16[4,192,384]{2,1,0:T(8,128)(2,1)} %copy-done.5, bf16[2,96,384]{2,1,0:T(8,128)(2,1)} %copy-done.8, bf16[2,96,384]{2,1,0:T(8,128)(2,1)} %copy-done.9, ...), custom_call_target="tpu_custom_call" | custom-call | flops 1300000000 | bytes 6000000 | tf_op jit(solution)/shard_map/spatial/pallas_call | solution.py:266
  137.0 5.9 %all-to-all-done.2 = bf16[32,16,128]{2,1,0:T(8,128)(2,1)S(1)} async-done(((bf16[32,16,128]{2,1,0:T(8,128)(2,1)}), bf16[32,16,128]{2,1,0:T(8,128)(2,1)S(1)}, u32[]{:S(2)}, u32[]{:S(2)}) %all-to-all-start.2) | async-done | bytes 131104 | tf_op jit(solution)/shard_map/all_to_all | solution.py:263
  143.8 3.9 %collective-permute-start.10 = (bf16[2,512,128]{2,1,0:T(8,128)(2,1)S(1)}, bf16[2,512,128]{2,1,0:T(8,128)(2,1)S(1)}, u32[]{:S(2)}, u32[]{:S(2)}) collective-permute-start(bf16[2,512,128]{2,1,0:T(8,128)(2,1)S(1)} %get-tuple-element.40), channel_id=1, source_target_pairs={{0,4},{4,8},{8,12},{12,0},{1,5},{5,9},{9,13},{13,1},{2,6},{6,10},{... | collective-permute-start | bytes 786440 | tf_op jit(solution)/shard_map/ppermute | solution.py:31
  147.7 4.4 %collective-permute-start.11 = (bf16[2,512,128]{2,1,0:T(8,128)(2,1)S(1)}, bf16[2,512,128]{2,1,0:T(8,128)(2,1)S(1)}, u32[]{:S(2)}, u32[]{:S(2)}) collective-permute-start(bf16[2,512,128]{2,1,0:T(8,128)(2,1)S(1)} %get-tuple-element.40), channel_id=1, source_target_pairs={{0,12},{4,0},{8,4},{12,8},{1,13},{5,1},{9,5},{13,9},{2,14},{6,2},{... | collective-permute-start | bytes 786440 | tf_op jit(solution)/shard_map/ppermute | solution.py:31
  152.1 3.1 %collective-permute-start.12 = (bf16[2,512,128]{2,1,0:T(8,128)(2,1)S(1)}, bf16[2,512,128]{2,1,0:T(8,128)(2,1)S(1)}, u32[]{:S(2)}, u32[]{:S(2)}) collective-permute-start(bf16[2,512,128]{2,1,0:T(8,128)(2,1)S(1)} %get-tuple-element.40), channel_id=1, source_target_pairs={{0,8},{4,12},{8,0},{12,4},{1,9},{5,13},{9,1},{13,5},{2,10},{6,14},... | collective-permute-start | bytes 786440 | tf_op jit(solution)/shard_map/ppermute | solution.py:31
  155.4 5.3 %collective-permute-done.12 = bf16[2,512,128]{2,1,0:T(8,128)(2,1)S(1)} collective-permute-done((bf16[2,512,128]{2,1,0:T(8,128)(2,1)S(1)}, bf16[2,512,128]{2,1,0:T(8,128)(2,1)S(1)}, u32[]{:S(2)}, u32[]{:S(2)}) %collective-permute-start.12) | collective-permute-done | bytes 262176 | tf_op jit(solution)/shard_map/ppermute | solution.py:31
  160.9 12.9 %collective-permute-start.13 = (bf16[4,2,512,128]{3,2,1,0:T(8,128)(2,1)S(1)}, bf16[4,2,512,128]{3,2,1,0:T(8,128)(2,1)S(1)}, u32[]{:S(2)}, u32[]{:S(2)}) collective-permute-start(bf16[4,2,512,128]{3,2,1,0:T(8,128)(2,1)S(1)} %pad_maximum_fusion.heads), channel_id=1, source_target_pairs={{0,2},{2,0},{1,3},{3,1},{4,6},{6,4},{5,7},{7,5},{8,10},{10,8},{9,1... | collective-permute-start | bytes 3145736 | tf_op jit(solution)/shard_map/ppermute | solution.py:39
  173.7 2.4 %share.1 = f32[512,384]{1,0:T(8,128)S(1)} custom-call(s32[4]{0:T(128)S(1)} %copy-done.1, bf16[4,2,512,128]{3,2,1,0:T(8,128)(2,1)S(1)} %pad_maximum_fusion.heads, bf16[8,768,384]{2,1,0:T(8,128)(2,1)} %all-to-all-done.blocks_ref.w_out), custom_call_target="tpu_custom_call" | custom-call | flops 400000000 | bytes 4000000 | tf_op jit(solution)/shard_map/share/pallas_call | solution.py:285
  176.2 3.1 %mixed.1 = bf16[512,384]{1,0:T(8,128)(2,1)} custom-call(s32[4]{0:T(128)S(1)} %copy-done.1, bf16[4,2,512,128]{3,2,1,0:T(8,128)(2,1)S(1)} %collective-permute-done.13.heads, bf16[8,768,384]{2,1,0:T(8,128)(2,1)} %all-to-all-done.blocks_ref.w_out, f32[512,384]{1,0:T(8,128)S(1)} %share.1, bf16[512,384]{1,0:T(8,128)(2,1)S(1)} %copy-done, f32[24,128]{1,0:T(8,128)S(1)} %bitcast.25), custom_call_target="tpu_custom_call" | custom-call | flops 400000000 | bytes 5000000 | tf_op jit(solution)/shard_map/mixed/pallas_call | solution.py:295
  (63 shorter events, 8.0 us)
Async XLA Ops:
  3.9 11.5 %copy-start.12 = (bf16[96,3,2,128]{3,2,1,0:T(2,128)(2,1)S(1)}, bf16[96,3,2,128]{3,2,1,0:T(2,128)(2,1)}, u32[]{:S(2)}) copy-start(bf16[96,3,2,128]{3,2,1,0:T(2,128)(2,1)} %param.11) | copy-start | bytes 442372
  3.9 71.8 %all-to-all-start = ((bf16[8,768,384]{2,1,0:T(8,128)(2,1)}), bf16[8,768,384]{2,1,0:T(8,128)(2,1)}, u32[]{:S(2)}, u32[]{:S(2)}) async-start(bf16[8,768,384]{2,1,0:T(8,128)(2,1)} %sent.1), calls=%async_computation | async-start | bytes 9437184 | tf_op jit(solution)/shard_map/all_to_all | solution.py:201
  43.3 38.0 %copy-start.3 = (bf16[768,384]{1,0:T(8,128)(2,1)}, bf16[768,384]{1,0:T(8,128)(2,1)S(1)}, u32[]{:S(2)}) copy-start(bf16[768,384]{1,0:T(8,128)(2,1)S(1)} %all-gather) | copy-start | bytes 1769476
  43.3 21.6 %collective-permute-start = (bf16[4,192,384]{2,1,0:T(8,128)(2,1)S(1)}, bf16[4,192,384]{2,1,0:T(8,128)(2,1)S(1)}, u32[]{:S(2)}, u32[]{:S(2)}) collective-permute-start(bf16[4,192,384]{2,1,0:T(8,128)(2,1)S(1)} %bitcast.26), channel_id=1, source_target_pairs={{0,16},{16,32},{32,48},{48,64},{64,80},{80,96},{96,112},{112,128},... | collective-permute-start | bytes 1769480 | tf_op jit(solution)/shard_map/ppermute | solution.py:27
  45.2 19.7 %collective-permute-start.1 = (bf16[4,192,384]{2,1,0:T(8,128)(2,1)S(1)}, bf16[4,192,384]{2,1,0:T(8,128)(2,1)S(1)}, u32[]{:S(2)}, u32[]{:S(2)}) collective-permute-start(bf16[4,192,384]{2,1,0:T(8,128)(2,1)S(1)} %bitcast.27), channel_id=1, source_target_pairs={{0,240},{16,0},{32,16},{48,32},{64,48},{80,64},{96,80},{112,96},{1... | collective-permute-start | bytes 1769480 | tf_op jit(solution)/shard_map/ppermute | solution.py:27
  50.0 14.9 %collective-permute-start.3 = (bf16[4,192,384]{2,1,0:T(8,128)(2,1)S(1)}, bf16[4,192,384]{2,1,0:T(8,128)(2,1)S(1)}, u32[]{:S(2)}, u32[]{:S(2)}) collective-permute-start(bf16[4,192,384]{2,1,0:T(8,128)(2,1)S(1)} %bitcast.28), channel_id=1, source_target_pairs={{0,256},{256,1},{1,257},{257,0},{2,258},{258,3},{3,259},{259,2},{4... | collective-permute-start | bytes 1769480 | tf_op jit(solution)/shard_map/ppermute | solution.py:35
  53.3 11.6 %collective-permute-start.2 = (bf16[2,96,384]{2,1,0:T(8,128)(2,1)S(1)}, bf16[2,96,384]{2,1,0:T(8,128)(2,1)S(1)}, u32[]{:S(2)}, u32[]{:S(2)}) collective-permute-start(bf16[2,96,384]{2,1,0:T(8,128)(2,1)S(1)} %get-tuple-element.36), channel_id=1, source_target_pairs={{0,32},{16,48},{32,64},{48,80},{64,96},{80,112},{96,128},{112,144}... | collective-permute-start | bytes 442376 | tf_op jit(solution)/shard_map/ppermute | solution.py:27
  55.2 15.1 %collective-permute-start.4 = (bf16[2,96,384]{2,1,0:T(8,128)(2,1)S(1)}, bf16[2,96,384]{2,1,0:T(8,128)(2,1)S(1)}, u32[]{:S(2)}, u32[]{:S(2)}) collective-permute-start(bf16[2,96,384]{2,1,0:T(8,128)(2,1)S(1)} %get-tuple-element.35), channel_id=1, source_target_pairs={{0,224},{16,240},{32,0},{48,16},{64,32},{80,48},{96,64},{112,80},{... | collective-permute-start | bytes 442376 | tf_op jit(solution)/shard_map/ppermute | solution.py:27
  64.9 16.5 %copy-start.10 = (bf16[2,96,384]{2,1,0:T(8,128)(2,1)}, bf16[2,96,384]{2,1,0:T(8,128)(2,1)S(1)}, u32[]{:S(2)}) copy-start(bf16[2,96,384]{2,1,0:T(8,128)(2,1)S(1)} %collective-permute-done.2.refs_3_) | copy-start | bytes 442372
  64.9 16.5 %copy-start.4 = (bf16[4,192,384]{2,1,0:T(8,128)(2,1)}, bf16[4,192,384]{2,1,0:T(8,128)(2,1)S(1)}, u32[]{:S(2)}) copy-start(bf16[4,192,384]{2,1,0:T(8,128)(2,1)S(1)} %collective-permute-done.refs_1_) | copy-start | bytes 1769476
  64.9 16.5 %copy-start.5 = (bf16[4,192,384]{2,1,0:T(8,128)(2,1)}, bf16[4,192,384]{2,1,0:T(8,128)(2,1)S(1)}, u32[]{:S(2)}) copy-start(bf16[4,192,384]{2,1,0:T(8,128)(2,1)S(1)} %collective-permute-done.1.refs_2_) | copy-start | bytes 1769476
  64.9 16.5 %copy-start.6 = (bf16[4,192,384]{2,1,0:T(8,128)(2,1)}, bf16[4,192,384]{2,1,0:T(8,128)(2,1)S(1)}, u32[]{:S(2)}) copy-start(bf16[4,192,384]{2,1,0:T(8,128)(2,1)S(1)} %collective-permute-done.3.refs_5_) | copy-start | bytes 1769476
  65.9 15.5 %collective-permute-start.6 = (bf16[6,96,384]{2,1,0:T(8,128)(2,1)}, bf16[6,96,384]{2,1,0:T(8,128)(2,1)S(1)}, u32[]{:S(2)}, u32[]{:S(2)}) collective-permute-start(bf16[6,96,384]{2,1,0:T(8,128)(2,1)} %pad_maximum_fusion.2), channel_id=1, source_target_pairs={{0,257},{256,0},{1,256},{257,1},{2,259},{258,2},{3,258},{259,3},{4... | collective-permute-start | bytes 1327112 | tf_op jit(solution)/shard_map/ppermute | solution.py:35
  71.1 10.5 %collective-permute-start.5 = (bf16[6,96,384]{2,1,0:T(8,128)(2,1)}, bf16[6,96,384]{2,1,0:T(8,128)(2,1)S(1)}, u32[]{:S(2)}, u32[]{:S(2)}) collective-permute-start(bf16[6,96,384]{2,1,0:T(8,128)(2,1)} %pad_maximum_fusion.1), channel_id=1, source_target_pairs={{0,256},{256,1},{1,257},{257,0},{2,258},{258,3},{3,259},{259,2},{4... | collective-permute-start | bytes 1327112 | tf_op jit(solution)/shard_map/ppermute | solution.py:35
  73.8 15.3 %collective-permute-start.7 = (bf16[4,96,384]{2,1,0:T(8,128)(2,1)}, bf16[4,96,384]{2,1,0:T(8,128)(2,1)}, u32[]{:S(2)}, u32[]{:S(2)}) collective-permute-start(bf16[4,96,384]{2,1,0:T(8,128)(2,1)} %slice.41), channel_id=1, source_target_pairs={{0,32},{16,48},{32,64},{48,80},{64,96},{80,112},{96,128},{112,144}... | collective-permute-start | bytes 884744 | tf_op jit(solution)/shard_map/ppermute | solution.py:27
  81.4 15.8 %slice-start.1 = ((bf16[4,192,384]{2,1,0:T(8,128)(2,1)}), bf16[4,96,384]{2,1,0:T(8,128)(2,1)S(1)}, s32[]{:S(2)}) async-start(bf16[4,192,384]{2,1,0:T(8,128)(2,1)} %copy-done.5), calls=%async_computation.4 | async-start | bytes 589824 | tf_op jit(solution)/shard_map/slice | solution.py:212
  81.4 20.8 %slice-start = ((bf16[4,192,384]{2,1,0:T(8,128)(2,1)}), bf16[4,96,384]{2,1,0:T(8,128)(2,1)S(1)}, s32[]{:S(2)}) async-start(bf16[4,192,384]{2,1,0:T(8,128)(2,1)} %copy-done.4), calls=%async_computation.3 | async-start | bytes 589824 | tf_op jit(solution)/shard_map/slice | solution.py:213
  89.1 25.9 %all-to-all-start.1 = ((bf16[32,16,384]{2,1,0:T(8,128)(2,1)}), bf16[32,16,384]{2,1,0:T(8,128)(2,1)S(1)}, u32[]{:S(2)}, u32[]{:S(2)}) async-start(bf16[32,16,384]{2,1,0:T(8,128)(2,1)} %bitcast.33), calls=%async_computation.1 | async-start | bytes 786432 | tf_op jit(solution)/shard_map/all_to_all | solution.py:247
  97.2 31.2 %copy-start.8 = (bf16[2,96,384]{2,1,0:T(8,128)(2,1)}, bf16[2,96,384]{2,1,0:T(8,128)(2,1)S(1)}, u32[]{:S(2)}) copy-start(bf16[2,96,384]{2,1,0:T(8,128)(2,1)S(1)} %get-tuple-element.37.refs_3_) | copy-start | bytes 442372
  97.3 31.2 %copy-start.9 = (bf16[2,96,384]{2,1,0:T(8,128)(2,1)}, bf16[2,96,384]{2,1,0:T(8,128)(2,1)S(1)}, u32[]{:S(2)}) copy-start(bf16[2,96,384]{2,1,0:T(8,128)(2,1)S(1)} %get-tuple-element.38.refs_4_) | copy-start | bytes 442372
  97.3 10.5 %collective-permute-start.9 = (bf16[6,96,384]{2,1,0:T(8,128)(2,1)S(1)}, bf16[6,96,384]{2,1,0:T(8,128)(2,1)S(1)}, u32[]{:S(2)}, u32[]{:S(2)}) collective-permute-start(bf16[6,96,384]{2,1,0:T(8,128)(2,1)S(1)} %pad_maximum_fusion.4), channel_id=1, source_target_pairs={{0,257},{256,0},{1,256},{257,1},{2,259},{258,2},{3,258},{259,3},{4... | collective-permute-start | bytes 1327112 | tf_op jit(solution)/shard_map/ppermute | solution.py:35
  102.3 10.6 %collective-permute-start.8 = (bf16[6,96,384]{2,1,0:T(8,128)(2,1)S(1)}, bf16[6,96,384]{2,1,0:T(8,128)(2,1)S(1)}, u32[]{:S(2)}, u32[]{:S(2)}) collective-permute-start(bf16[6,96,384]{2,1,0:T(8,128)(2,1)S(1)} %pad_maximum_fusion.3), channel_id=1, source_target_pairs={{0,256},{256,1},{1,257},{257,0},{2,258},{258,3},{3,259},{259,2},{4... | collective-permute-start | bytes 1327112 | tf_op jit(solution)/shard_map/ppermute | solution.py:35
  107.9 20.6 %copy-start.15 = (bf16[6,96,384]{2,1,0:T(8,128)(2,1)}, bf16[6,96,384]{2,1,0:T(8,128)(2,1)S(1)}, u32[]{:S(2)}) copy-start(bf16[6,96,384]{2,1,0:T(8,128)(2,1)S(1)} %collective-permute-done.9.refs_7_) | copy-start | bytes 1327108
  112.9 15.6 %copy-start.16 = (bf16[6,96,384]{2,1,0:T(8,128)(2,1)}, bf16[6,96,384]{2,1,0:T(8,128)(2,1)S(1)}, u32[]{:S(2)}) copy-start(bf16[6,96,384]{2,1,0:T(8,128)(2,1)S(1)} %collective-permute-done.8.refs_6_) | copy-start | bytes 1327108
  119.0 23.9 %all-to-all-start.2 = ((bf16[32,16,128]{2,1,0:T(8,128)(2,1)}), bf16[32,16,128]{2,1,0:T(8,128)(2,1)S(1)}, u32[]{:S(2)}, u32[]{:S(2)}) async-start(bf16[32,16,128]{2,1,0:T(8,128)(2,1)} %bitcast.37), calls=%async_computation.2 | async-start | bytes 262144 | tf_op jit(solution)/shard_map/all_to_all | solution.py:263
  128.5 45.2 %copy-start.1 = (s32[4]{0:T(128)S(1)}, s32[4]{0:T(128)}, u32[]{:S(2)}) copy-start(s32[4]{0:T(128)} %pad_add_fusion.place) | copy-start | bytes 52
  142.8 33.3 %copy-start = (bf16[512,384]{1,0:T(8,128)(2,1)S(1)}, bf16[512,384]{1,0:T(8,128)(2,1)}, u32[]{:S(2)}) copy-start(bf16[512,384]{1,0:T(8,128)(2,1)} %hidden.3) | copy-start | bytes 1179652
  142.8 33.4 %copy-start.2 = (f32[3072]{0:T(1024)S(1)}, f32[3072]{0:T(1024)}, u32[]{:S(2)}) copy-start(f32[3072]{0:T(1024)} %param.10) | copy-start | bytes 36868
  143.8 11.4 %collective-permute-start.10 = (bf16[2,512,128]{2,1,0:T(8,128)(2,1)S(1)}, bf16[2,512,128]{2,1,0:T(8,128)(2,1)S(1)}, u32[]{:S(2)}, u32[]{:S(2)}) collective-permute-start(bf16[2,512,128]{2,1,0:T(8,128)(2,1)S(1)} %get-tuple-element.40), channel_id=1, source_target_pairs={{0,4},{4,8},{8,12},{12,0},{1,5},{5,9},{9,13},{13,1},{2,6},{6,10},{... | collective-permute-start | bytes 786440 | tf_op jit(solution)/shard_map/ppermute | solution.py:31
  147.7 7.7 %collective-permute-start.11 = (bf16[2,512,128]{2,1,0:T(8,128)(2,1)S(1)}, bf16[2,512,128]{2,1,0:T(8,128)(2,1)S(1)}, u32[]{:S(2)}, u32[]{:S(2)}) collective-permute-start(bf16[2,512,128]{2,1,0:T(8,128)(2,1)S(1)} %get-tuple-element.40), channel_id=1, source_target_pairs={{0,12},{4,0},{8,4},{12,8},{1,13},{5,1},{9,5},{13,9},{2,14},{6,2},{... | collective-permute-start | bytes 786440 | tf_op jit(solution)/shard_map/ppermute | solution.py:31
  152.1 8.6 %collective-permute-start.12 = (bf16[2,512,128]{2,1,0:T(8,128)(2,1)S(1)}, bf16[2,512,128]{2,1,0:T(8,128)(2,1)S(1)}, u32[]{:S(2)}, u32[]{:S(2)}) collective-permute-start(bf16[2,512,128]{2,1,0:T(8,128)(2,1)S(1)} %get-tuple-element.40), channel_id=1, source_target_pairs={{0,8},{4,12},{8,0},{12,4},{1,9},{5,13},{9,1},{13,5},{2,10},{6,14},... | collective-permute-start | bytes 786440 | tf_op jit(solution)/shard_map/ppermute | solution.py:31
  160.9 15.3 %collective-permute-start.13 = (bf16[4,2,512,128]{3,2,1,0:T(8,128)(2,1)S(1)}, bf16[4,2,512,128]{3,2,1,0:T(8,128)(2,1)S(1)}, u32[]{:S(2)}, u32[]{:S(2)}) collective-permute-start(bf16[4,2,512,128]{3,2,1,0:T(8,128)(2,1)S(1)} %pad_maximum_fusion.heads), channel_id=1, source_target_pairs={{0,2},{2,0},{1,3},{3,1},{4,6},{6,4},{5,7},{7,5},{8,10},{10,8},{9,1... | collective-permute-start | bytes 3145736 | tf_op jit(solution)/shard_map/ppermute | solution.py:39
  (4 other events, 13.7 us)

commit v6 on v5

--- a/solution.py
+++ b/solution.py
@@ -83,16 +83,21 @@
     return lax.dot_general(queries, keys, (((1,), (1,)), ((), ())), preferred_element_type=F32) * float(HD) ** (-0.5)
 
 
-def sent_kernel(hidden, w_out, sent, sem):
-    copies = []
+def sent_kernel(hidden, w_out, sent, hidden_here, w_out_here, sem, sems):
+    loads = [pltpu.make_async_copy(hidden, hidden_here, sem.at[0]), pltpu.make_async_copy(w_out, w_out_here, sem.at[1])]
+    for load in loads:
+        load.start()
+    copies = [pltpu.make_async_copy(hidden_here, sent.at[g, pl.ds(0, 512)], sems.at[g]) for g in range(8)]
     for g in range(8):
-        copies.append(pltpu.make_async_copy(hidden, sent.at[g, pl.ds(0, 512)], sem.at[len(copies)]))
         for kind in range(2):
-            columns = w_out.at[kind, :, pl.ds(g * 384, 384)]
-            copies.append(
-                pltpu.make_async_copy(columns, sent.at[g, pl.ds(512 + kind * HD, HD)], sem.at[len(copies)])
-            )
-    for copy in copies:
+            columns = w_out_here.at[kind, :, pl.ds(g * 384, 384)]
+            there = sent.at[g, pl.ds(512 + kind * HD, HD)]
+            copies.append(pltpu.make_async_copy(columns, there, sems.at[len(copies)]))
+    loads[0].wait()
+    for copy in copies[:8]:
+        copy.start()
+    loads[1].wait()
+    for copy in copies[8:]:
         copy.start()
     for copy in copies:
         copy.wait()
@@ -192,9 +197,14 @@
     sent = pl.pallas_call(
         sent_kernel,
         out_shape=jax.ShapeDtypeStruct((8, 768, 384), BF16),
-        in_specs=[VMEM, VMEM],
+        in_specs=[HBM, HBM],
         out_specs=HBM,
-        scratch_shapes=[pltpu.SemaphoreType.DMA((24,))],
+        scratch_shapes=[
+            pltpu.VMEM((512, 384), BF16),
+            pltpu.VMEM((2, HD, D), BF16),
+            pltpu.SemaphoreType.DMA((2,)),
+            pltpu.SemaphoreType.DMA((24,)),
+        ],
         name="sent",
         **params(0, 7_000_000),
     )(hidden, w_out)
@@ -258,7 +268,7 @@
         in_specs=[VMEM],
         out_specs=VMEM,
         name="temporal",
-        **params(140_000_000, 500_000),
+        **params(140_000_000, 500_000, 24),
     )(by_position)
     temporal = lax.all_to_all(
         temporal.reshape(32, 16, HD), ("yl", "zh", "zl"), split_axis=0, concat_axis=0, tiled=True

time: 180 us -> 176 us (0.978)
  local copies, waits for them, and re-layouts: 4.98 us -> 2.32 us
  transfers between devices with their start and end apart: 17 -> 17, of which waited for: 8 -> 8; matrix products, arithmetic and copies ran while one was open for 3% -> 2% of each run, Pallas kernels for 13% -> 13%
where the time goes in v6:
time: 176 us; the launch traced here: 175 us
  starting transfers between devices  83.4 us (47%)
  Pallas kernels  31.3 us (18%)
  waiting for transfers between devices  27.2 us (15%)
  blocking collectives  27 us (15%)
  other arithmetic  3.66 us (2%)
  local copies, waits for them, and re-layouts  2.32 us (1%)
    all_gather x1, blocking collectives, body(): own = lax.all_gather(shards, 'zh', axis=0)  27 us
    ppermute x5, starting transfers between devices, along_y(): lax.ppermute(value, ('yl', 'dp'), [(Y_PLACE[i], Y_PLACE[(i + step) % 4])...  16.3 us
    ppermute x5, starting transfers between devices, along_z(): lax.ppermute(value, ('zh', 'zl'), [(i, (i + step) % 16) for i in range(16)])  16 us
    ppermute x3, starting transfers between devices, along_x(): return lax.ppermute(value, 'x', [(i, (i + step) % 4) for i in range(4)])  12.3 us
    ppermute x1, starting transfers between devices, other_core(): return lax.ppermute(value, 'c', [(0, 1), (1, 0)])  11.8 us
    all_to_all x1, starting transfers between devices, body(): lax.all_to_all(sent, ('x', 'c'), split_axis=0, concat_axis=0, tiled=True)  11.5 us
    ppermute x5, waiting for transfers between devices, along_y(): lax.ppermute(value, ('yl', 'dp'), [(Y_PLACE[i], Y_PLACE[(i + step) % 4])...  8.9 us
    all_to_all x1, starting transfers between devices, body(): lax.all_to_all(temporal.reshape(32, 16, HD), ('yl', 'zh', 'zl'), split_ax...  8.47 us
  transfers between devices with their start and end apart: 17, of which 8 were waited for; matrix products, arithmetic and copies ran while one was open for 2% of the time, Pallas kernels for 13%

profile of v6, /device:TPU:1, one launch (start us, length us, event | category | flops | bytes accessed | tf_op | source)
XLA Modules:
  0.0 175.3 jit_solution(13985166123940547656)
XLA Ops:
  0.0 3.4 %sent.1 = bf16[8,768,384]{2,1,0:T(8,128)(2,1)} custom-call(bf16[512,384]{1,0:T(8,128)(2,1)} %hidden.3, bf16[2,128,3072]{2,1,0:T(8,128)(2,1)} %w_out.1), custom_call_target="tpu_custom_call" | custom-call | bytes 7000000 | tf_op jit(solution)/shard_map/sent/pallas_call | solution.py:197
  3.5 11.5 %all-to-all-start = ((bf16[8,768,384]{2,1,0:T(8,128)(2,1)}), bf16[8,768,384]{2,1,0:T(8,128)(2,1)}, u32[]{:S(2)}, u32[]{:S(2)}) async-start(bf16[8,768,384]{2,1,0:T(8,128)(2,1)} %sent.1), calls=%async_computation | async-start | bytes 9437184 | tf_op jit(solution)/shard_map/all_to_all | solution.py:211
  15.8 27.0 %all-gather = bf16[768,384]{1,0:T(8,128)(2,1)S(1)} all-gather(bf16[192,384]{1,0:T(8,128)(2,1)S(1)} %pad_maximum_fusion.6), channel_id=2, replica_groups=mesh['yl'=2,'zh'=4,'zl'=4,'x'=4,'c'=2,'dp'=2] {'zh'}, dimensions={0}, use_global_device_ids=true | all-gather | bytes 737280 | tf_op jit(solution)/shard_map/all_gather | solution.py:213
  42.8 1.9 %collective-permute-start = (bf16[4,192,384]{2,1,0:T(8,128)(2,1)S(1)}, bf16[4,192,384]{2,1,0:T(8,128)(2,1)S(1)}, u32[]{:S(2)}, u32[]{:S(2)}) collective-permute-start(bf16[4,192,384]{2,1,0:T(8,128)(2,1)S(1)} %bitcast.27), channel_id=1, source_target_pairs={{0,16},{16,32},{32,48},{48,64},{64,80},{80,96},{96,112},{112,128},... | collective-permute-start | bytes 1769480 | tf_op jit(solution)/shard_map/ppermute | solution.py:27
  44.7 4.8 %collective-permute-start.1 = (bf16[4,192,384]{2,1,0:T(8,128)(2,1)S(1)}, bf16[4,192,384]{2,1,0:T(8,128)(2,1)S(1)}, u32[]{:S(2)}, u32[]{:S(2)}) collective-permute-start(bf16[4,192,384]{2,1,0:T(8,128)(2,1)S(1)} %bitcast.28), channel_id=1, source_target_pairs={{0,240},{16,0},{32,16},{48,32},{64,48},{80,64},{96,80},{112,96},{1... | collective-permute-start | bytes 1769480 | tf_op jit(solution)/shard_map/ppermute | solution.py:27
  49.5 3.2 %collective-permute-start.3 = (bf16[4,192,384]{2,1,0:T(8,128)(2,1)S(1)}, bf16[4,192,384]{2,1,0:T(8,128)(2,1)S(1)}, u32[]{:S(2)}, u32[]{:S(2)}) collective-permute-start(bf16[4,192,384]{2,1,0:T(8,128)(2,1)S(1)} %bitcast.29), channel_id=1, source_target_pairs={{0,256},{256,1},{1,257},{257,0},{2,258},{258,3},{3,259},{259,2},{4... | collective-permute-start | bytes 1769480 | tf_op jit(solution)/shard_map/ppermute | solution.py:35
  52.8 1.9 %collective-permute-start.2 = (bf16[2,96,384]{2,1,0:T(8,128)(2,1)S(1)}, bf16[2,96,384]{2,1,0:T(8,128)(2,1)S(1)}, u32[]{:S(2)}, u32[]{:S(2)}) collective-permute-start(bf16[2,96,384]{2,1,0:T(8,128)(2,1)S(1)} %get-tuple-element.36), channel_id=1, source_target_pairs={{0,32},{16,48},{32,64},{48,80},{64,96},{80,112},{96,128},{112,144}... | collective-permute-start | bytes 442376 | tf_op jit(solution)/shard_map/ppermute | solution.py:27
  54.7 5.5 %collective-permute-start.4 = (bf16[2,96,384]{2,1,0:T(8,128)(2,1)S(1)}, bf16[2,96,384]{2,1,0:T(8,128)(2,1)S(1)}, u32[]{:S(2)}, u32[]{:S(2)}) collective-permute-start(bf16[2,96,384]{2,1,0:T(8,128)(2,1)S(1)} %get-tuple-element.35), channel_id=1, source_target_pairs={{0,224},{16,240},{32,0},{48,16},{64,32},{80,48},{96,64},{112,80},{... | collective-permute-start | bytes 442376 | tf_op jit(solution)/shard_map/ppermute | solution.py:27
  60.8 3.6 %collective-permute-done.2.refs_3_ = bf16[2,96,384]{2,1,0:T(8,128)(2,1)S(1)} collective-permute-done((bf16[2,96,384]{2,1,0:T(8,128)(2,1)S(1)}, bf16[2,96,384]{2,1,0:T(8,128)(2,1)S(1)}, u32[]{:S(2)}, u32[]{:S(2)}) %collective-permute-start.2) | collective-permute-done | bytes 147488 | tf_op jit(solution)/shard_map/ppermute | solution.py:27
  65.4 4.3 %collective-permute-start.6 = (bf16[6,96,384]{2,1,0:T(8,128)(2,1)}, bf16[6,96,384]{2,1,0:T(8,128)(2,1)S(1)}, u32[]{:S(2)}, u32[]{:S(2)}) collective-permute-start(bf16[6,96,384]{2,1,0:T(8,128)(2,1)} %pad_maximum_fusion.2), channel_id=1, source_target_pairs={{0,257},{256,0},{1,256},{257,1},{2,259},{258,2},{3,258},{259,3},{4... | collective-permute-start | bytes 1327112 | tf_op jit(solution)/shard_map/ppermute | solution.py:35
  70.7 1.9 %collective-permute-start.5 = (bf16[6,96,384]{2,1,0:T(8,128)(2,1)}, bf16[6,96,384]{2,1,0:T(8,128)(2,1)}, u32[]{:S(2)}, u32[]{:S(2)}) collective-permute-start(bf16[6,96,384]{2,1,0:T(8,128)(2,1)} %pad_maximum_fusion.1), channel_id=1, source_target_pairs={{0,256},{256,1},{1,257},{257,0},{2,258},{258,3},{3,259},{259,2},{4... | collective-permute-start | bytes 1327112 | tf_op jit(solution)/shard_map/ppermute | solution.py:35
  73.3 1.9 %collective-permute-start.7 = (bf16[4,96,384]{2,1,0:T(8,128)(2,1)}, bf16[4,96,384]{2,1,0:T(8,128)(2,1)S(1)}, u32[]{:S(2)}, u32[]{:S(2)}) collective-permute-start(bf16[4,96,384]{2,1,0:T(8,128)(2,1)} %slice.41), channel_id=1, source_target_pairs={{0,32},{16,48},{32,64},{48,80},{64,96},{80,112},{96,128},{112,144}... | collective-permute-start | bytes 884744 | tf_op jit(solution)/shard_map/ppermute | solution.py:27
  75.2 5.6 %norm.1.refs_8_.refs_9_ = bf16[512,3072]{1,0:T(8,128)(2,1)} custom-call(bf16[8,768,384]{2,1,0:T(8,128)(2,1)} %all-to-all-done.blocks_ref.w_out, f32[24,128]{1,0:T(8,128)} %bitcast.42, f32[24,128]{1,0:T(8,128)} %bitcast.43), custom_call_target="tpu_custom_call" | custom-call | flops 20000000 | bytes 6000000 | tf_op jit(solution)/shard_map/norm/pallas_call | solution.py:228
  81.7 6.1 %temporal_project.1 = bf16[512,384]{1,0:T(8,128)(2,1)} custom-call(s32[4]{0:T(128)} %pad_add_fusion.place, bf16[4,192,384]{2,1,0:T(8,128)(2,1)} %bitcast.32, bf16[4,192,384]{2,1,0:T(8,128)(2,1)} %copy-done.4, bf16[4,192,384]{2,1,0:T(8,128)(2,1)} %copy-done.5, bf16[2,96,384]{2,1,0:T(8,128)(2,1)} %copy-done.9, bf16[2,96,384]{2,1,0:T(8,128)(2,1)} %copy-done.10, ...), custom_call_target="tpu_custom_call" | custom-call | flops 1200000000 | bytes 6000000 | tf_op jit(solution)/shard_map/temporal_project/pallas_call | solution.py:242
  87.8 7.1 %all-to-all-start.1 = ((bf16[32,16,384]{2,1,0:T(8,128)(2,1)}), bf16[32,16,384]{2,1,0:T(8,128)(2,1)S(1)}, u32[]{:S(2)}, u32[]{:S(2)}) async-start(bf16[32,16,384]{2,1,0:T(8,128)(2,1)} %bitcast.34), calls=%async_computation.1 | async-start | bytes 786432 | tf_op jit(solution)/shard_map/all_to_all | solution.py:257
  95.0 4.9 %collective-permute-start.9 = (bf16[6,96,384]{2,1,0:T(8,128)(2,1)S(1)}, bf16[6,96,384]{2,1,0:T(8,128)(2,1)S(1)}, u32[]{:S(2)}, u32[]{:S(2)}) collective-permute-start(bf16[6,96,384]{2,1,0:T(8,128)(2,1)S(1)} %pad_maximum_fusion.4), channel_id=1, source_target_pairs={{0,257},{256,0},{1,256},{257,1},{2,259},{258,2},{3,258},{259,3},{4... | collective-permute-start | bytes 1327112 | tf_op jit(solution)/shard_map/ppermute | solution.py:35
  100.0 1.9 %collective-permute-start.8 = (bf16[6,96,384]{2,1,0:T(8,128)(2,1)S(1)}, bf16[6,96,384]{2,1,0:T(8,128)(2,1)S(1)}, u32[]{:S(2)}, u32[]{:S(2)}) collective-permute-start(bf16[6,96,384]{2,1,0:T(8,128)(2,1)S(1)} %pad_maximum_fusion.3), channel_id=1, source_target_pairs={{0,256},{256,1},{1,257},{257,0},{2,258},{258,3},{3,259},{259,2},{4... | collective-permute-start | bytes 1327112 | tf_op jit(solution)/shard_map/ppermute | solution.py:35
  102.0 3.6 %collective-permute-done.9.refs_7_ = bf16[6,96,384]{2,1,0:T(8,128)(2,1)S(1)} collective-permute-done((bf16[6,96,384]{2,1,0:T(8,128)(2,1)S(1)}, bf16[6,96,384]{2,1,0:T(8,128)(2,1)S(1)}, u32[]{:S(2)}, u32[]{:S(2)}) %collective-permute-start.9) | collective-permute-done | bytes 442400 | tf_op jit(solution)/shard_map/ppermute | solution.py:35
  105.6 5.0 %collective-permute-done.8.refs_6_ = bf16[6,96,384]{2,1,0:T(8,128)(2,1)S(1)} collective-permute-done((bf16[6,96,384]{2,1,0:T(8,128)(2,1)S(1)}, bf16[6,96,384]{2,1,0:T(8,128)(2,1)S(1)}, u32[]{:S(2)}, u32[]{:S(2)}) %collective-permute-start.8) | collective-permute-done | bytes 442400 | tf_op jit(solution)/shard_map/ppermute | solution.py:35
  110.6 3.1 %all-to-all-done.1 = bf16[32,16,384]{2,1,0:T(8,128)(2,1)S(1)} async-done(((bf16[32,16,384]{2,1,0:T(8,128)(2,1)}), bf16[32,16,384]{2,1,0:T(8,128)(2,1)S(1)}, u32[]{:S(2)}, u32[]{:S(2)}) %all-to-all-start.1) | async-done | bytes 393248 | tf_op jit(solution)/shard_map/all_to_all | solution.py:257
  113.7 2.2 %temporal.1 = bf16[512,128]{1,0:T(8,128)(2,1)} custom-call(bf16[512,384]{1,0:T(8,128)(2,1)S(1)} %bitcast.25), custom_call_target="tpu_custom_call" | custom-call | flops 140000000 | bytes 500000 | tf_op jit(solution)/shard_map/temporal/pallas_call | solution.py:265
  115.9 8.5 %all-to-all-start.2 = ((bf16[32,16,128]{2,1,0:T(8,128)(2,1)}), bf16[32,16,128]{2,1,0:T(8,128)(2,1)S(1)}, u32[]{:S(2)}, u32[]{:S(2)}) async-start(bf16[32,16,128]{2,1,0:T(8,128)(2,1)} %bitcast.11), calls=%async_computation.2 | async-start | bytes 262144 | tf_op jit(solution)/shard_map/all_to_all | solution.py:273
  124.5 8.5 %spatial.1 = bf16[512,128]{1,0:T(8,128)(2,1)} custom-call(s32[4]{0:T(128)} %pad_add_fusion.place, bf16[4,192,384]{2,1,0:T(8,128)(2,1)} %bitcast.33, bf16[4,192,384]{2,1,0:T(8,128)(2,1)} %copy-done.4, bf16[4,192,384]{2,1,0:T(8,128)(2,1)} %copy-done.5, bf16[2,96,384]{2,1,0:T(8,128)(2,1)} %copy-done.7, bf16[2,96,384]{2,1,0:T(8,128)(2,1)} %copy-done.8, ...), custom_call_target="tpu_custom_call" | custom-call | flops 1300000000 | bytes 6000000 | tf_op jit(solution)/shard_map/spatial/pallas_call | solution.py:276
  132.9 5.9 %all-to-all-done.2 = bf16[32,16,128]{2,1,0:T(8,128)(2,1)S(1)} async-done(((bf16[32,16,128]{2,1,0:T(8,128)(2,1)}), bf16[32,16,128]{2,1,0:T(8,128)(2,1)S(1)}, u32[]{:S(2)}, u32[]{:S(2)}) %all-to-all-start.2) | async-done | bytes 131104 | tf_op jit(solution)/shard_map/all_to_all | solution.py:273
  138.8 1.0 fusion
  139.8 4.3 %collective-permute-start.10 = (bf16[2,512,128]{2,1,0:T(8,128)(2,1)S(1)}, bf16[2,512,128]{2,1,0:T(8,128)(2,1)S(1)}, u32[]{:S(2)}, u32[]{:S(2)}) collective-permute-start(bf16[2,512,128]{2,1,0:T(8,128)(2,1)S(1)} %get-tuple-element.40), channel_id=1, source_target_pairs={{0,4},{4,8},{8,12},{12,0},{1,5},{5,9},{9,13},{13,1},{2,6},{6,10},{... | collective-permute-start | bytes 786440 | tf_op jit(solution)/shard_map/ppermute | solution.py:31
  144.1 4.9 %collective-permute-start.11 = (bf16[2,512,128]{2,1,0:T(8,128)(2,1)S(1)}, bf16[2,512,128]{2,1,0:T(8,128)(2,1)S(1)}, u32[]{:S(2)}, u32[]{:S(2)}) collective-permute-start(bf16[2,512,128]{2,1,0:T(8,128)(2,1)S(1)} %get-tuple-element.40), channel_id=1, source_target_pairs={{0,12},{4,0},{8,4},{12,8},{1,13},{5,1},{9,5},{13,9},{2,14},{6,2},{... | collective-permute-start | bytes 786440 | tf_op jit(solution)/shard_map/ppermute | solution.py:31
  149.1 3.1 %collective-permute-start.12 = (bf16[2,512,128]{2,1,0:T(8,128)(2,1)S(1)}, bf16[2,512,128]{2,1,0:T(8,128)(2,1)S(1)}, u32[]{:S(2)}, u32[]{:S(2)}) collective-permute-start(bf16[2,512,128]{2,1,0:T(8,128)(2,1)S(1)} %get-tuple-element.40), channel_id=1, source_target_pairs={{0,8},{4,12},{8,0},{12,4},{1,9},{5,13},{9,1},{13,5},{2,10},{6,14},... | collective-permute-start | bytes 786440 | tf_op jit(solution)/shard_map/ppermute | solution.py:31
  152.4 5.4 %collective-permute-done.12 = bf16[2,512,128]{2,1,0:T(8,128)(2,1)S(1)} collective-permute-done((bf16[2,512,128]{2,1,0:T(8,128)(2,1)S(1)}, bf16[2,512,128]{2,1,0:T(8,128)(2,1)S(1)}, u32[]{:S(2)}, u32[]{:S(2)}) %collective-permute-start.12) | collective-permute-done | bytes 262176 | tf_op jit(solution)/shard_map/ppermute | solution.py:31
  157.9 11.8 %collective-permute-start.13 = (bf16[4,2,512,128]{3,2,1,0:T(8,128)(2,1)S(1)}, bf16[4,2,512,128]{3,2,1,0:T(8,128)(2,1)S(1)}, u32[]{:S(2)}, u32[]{:S(2)}) collective-permute-start(bf16[4,2,512,128]{3,2,1,0:T(8,128)(2,1)S(1)} %pad_maximum_fusion.heads), channel_id=1, source_target_pairs={{0,2},{2,0},{1,3},{3,1},{4,6},{6,4},{5,7},{7,5},{8,10},{10,8},{9,1... | collective-permute-start | bytes 3145736 | tf_op jit(solution)/shard_map/ppermute | solution.py:39
  169.7 2.4 %share.1 = f32[512,384]{1,0:T(8,128)S(1)} custom-call(s32[4]{0:T(128)S(1)} %copy-done.1, bf16[4,2,512,128]{3,2,1,0:T(8,128)(2,1)S(1)} %pad_maximum_fusion.heads, bf16[8,768,384]{2,1,0:T(8,128)(2,1)} %all-to-all-done.blocks_ref.w_out), custom_call_target="tpu_custom_call" | custom-call | flops 400000000 | bytes 4000000 | tf_op jit(solution)/shard_map/share/pallas_call | solution.py:295
  172.2 3.1 %mixed.1 = bf16[512,384]{1,0:T(8,128)(2,1)} custom-call(s32[4]{0:T(128)S(1)} %copy-done.1, bf16[4,2,512,128]{3,2,1,0:T(8,128)(2,1)S(1)} %collective-permute-done.13.heads, bf16[8,768,384]{2,1,0:T(8,128)(2,1)} %all-to-all-done.blocks_ref.w_out, f32[512,384]{1,0:T(8,128)S(1)} %share.1, bf16[512,384]{1,0:T(8,128)(2,1)S(1)} %copy-done, f32[24,128]{1,0:T(8,128)S(1)} %bitcast.26), custom_call_target="tpu_custom_call" | custom-call | flops 400000000 | bytes 5000000 | tf_op jit(solution)/shard_map/mixed/pallas_call | solution.py:305
  (59 shorter events, 5.5 us)
Async XLA Ops:
  3.4 11.5 %copy-start.11 = (bf16[96,3,2,128]{3,2,1,0:T(2,128)(2,1)S(1)}, bf16[96,3,2,128]{3,2,1,0:T(2,128)(2,1)}, u32[]{:S(2)}) copy-start(bf16[96,3,2,128]{3,2,1,0:T(2,128)(2,1)} %param.11) | copy-start | bytes 442372
  3.5 71.8 %all-to-all-start = ((bf16[8,768,384]{2,1,0:T(8,128)(2,1)}), bf16[8,768,384]{2,1,0:T(8,128)(2,1)}, u32[]{:S(2)}, u32[]{:S(2)}) async-start(bf16[8,768,384]{2,1,0:T(8,128)(2,1)} %sent.1), calls=%async_computation | async-start | bytes 9437184 | tf_op jit(solution)/shard_map/all_to_all | solution.py:211
  42.8 38.1 %copy-start.3 = (bf16[768,384]{1,0:T(8,128)(2,1)}, bf16[768,384]{1,0:T(8,128)(2,1)S(1)}, u32[]{:S(2)}) copy-start(bf16[768,384]{1,0:T(8,128)(2,1)S(1)} %all-gather) | copy-start | bytes 1769476
  42.8 21.6 %collective-permute-start = (bf16[4,192,384]{2,1,0:T(8,128)(2,1)S(1)}, bf16[4,192,384]{2,1,0:T(8,128)(2,1)S(1)}, u32[]{:S(2)}, u32[]{:S(2)}) collective-permute-start(bf16[4,192,384]{2,1,0:T(8,128)(2,1)S(1)} %bitcast.27), channel_id=1, source_target_pairs={{0,16},{16,32},{32,48},{48,64},{64,80},{80,96},{96,112},{112,128},... | collective-permute-start | bytes 1769480 | tf_op jit(solution)/shard_map/ppermute | solution.py:27
  44.7 19.7 %collective-permute-start.1 = (bf16[4,192,384]{2,1,0:T(8,128)(2,1)S(1)}, bf16[4,192,384]{2,1,0:T(8,128)(2,1)S(1)}, u32[]{:S(2)}, u32[]{:S(2)}) collective-permute-start(bf16[4,192,384]{2,1,0:T(8,128)(2,1)S(1)} %bitcast.28), channel_id=1, source_target_pairs={{0,240},{16,0},{32,16},{48,32},{64,48},{80,64},{96,80},{112,96},{1... | collective-permute-start | bytes 1769480 | tf_op jit(solution)/shard_map/ppermute | solution.py:27
  49.5 14.9 %collective-permute-start.3 = (bf16[4,192,384]{2,1,0:T(8,128)(2,1)S(1)}, bf16[4,192,384]{2,1,0:T(8,128)(2,1)S(1)}, u32[]{:S(2)}, u32[]{:S(2)}) collective-permute-start(bf16[4,192,384]{2,1,0:T(8,128)(2,1)S(1)} %bitcast.29), channel_id=1, source_target_pairs={{0,256},{256,1},{1,257},{257,0},{2,258},{258,3},{3,259},{259,2},{4... | collective-permute-start | bytes 1769480 | tf_op jit(solution)/shard_map/ppermute | solution.py:35
  52.8 11.6 %collective-permute-start.2 = (bf16[2,96,384]{2,1,0:T(8,128)(2,1)S(1)}, bf16[2,96,384]{2,1,0:T(8,128)(2,1)S(1)}, u32[]{:S(2)}, u32[]{:S(2)}) collective-permute-start(bf16[2,96,384]{2,1,0:T(8,128)(2,1)S(1)} %get-tuple-element.36), channel_id=1, source_target_pairs={{0,32},{16,48},{32,64},{48,80},{64,96},{80,112},{96,128},{112,144}... | collective-permute-start | bytes 442376 | tf_op jit(solution)/shard_map/ppermute | solution.py:27
  54.7 15.1 %collective-permute-start.4 = (bf16[2,96,384]{2,1,0:T(8,128)(2,1)S(1)}, bf16[2,96,384]{2,1,0:T(8,128)(2,1)S(1)}, u32[]{:S(2)}, u32[]{:S(2)}) collective-permute-start(bf16[2,96,384]{2,1,0:T(8,128)(2,1)S(1)} %get-tuple-element.35), channel_id=1, source_target_pairs={{0,224},{16,240},{32,0},{48,16},{64,32},{80,48},{96,64},{112,80},{... | collective-permute-start | bytes 442376 | tf_op jit(solution)/shard_map/ppermute | solution.py:27
  64.4 16.5 %copy-start.9 = (bf16[2,96,384]{2,1,0:T(8,128)(2,1)}, bf16[2,96,384]{2,1,0:T(8,128)(2,1)S(1)}, u32[]{:S(2)}) copy-start(bf16[2,96,384]{2,1,0:T(8,128)(2,1)S(1)} %collective-permute-done.2.refs_3_) | copy-start | bytes 442372
  64.4 16.5 %copy-start.4 = (bf16[4,192,384]{2,1,0:T(8,128)(2,1)}, bf16[4,192,384]{2,1,0:T(8,128)(2,1)S(1)}, u32[]{:S(2)}) copy-start(bf16[4,192,384]{2,1,0:T(8,128)(2,1)S(1)} %collective-permute-done.refs_1_) | copy-start | bytes 1769476
  64.4 16.5 %copy-start.5 = (bf16[4,192,384]{2,1,0:T(8,128)(2,1)}, bf16[4,192,384]{2,1,0:T(8,128)(2,1)S(1)}, u32[]{:S(2)}) copy-start(bf16[4,192,384]{2,1,0:T(8,128)(2,1)S(1)} %collective-permute-done.1.refs_2_) | copy-start | bytes 1769476
  64.4 16.5 %copy-start.6 = (bf16[4,192,384]{2,1,0:T(8,128)(2,1)}, bf16[4,192,384]{2,1,0:T(8,128)(2,1)S(1)}, u32[]{:S(2)}) copy-start(bf16[4,192,384]{2,1,0:T(8,128)(2,1)S(1)} %collective-permute-done.3.refs_5_) | copy-start | bytes 1769476
  65.4 15.5 %collective-permute-start.6 = (bf16[6,96,384]{2,1,0:T(8,128)(2,1)}, bf16[6,96,384]{2,1,0:T(8,128)(2,1)S(1)}, u32[]{:S(2)}, u32[]{:S(2)}) collective-permute-start(bf16[6,96,384]{2,1,0:T(8,128)(2,1)} %pad_maximum_fusion.2), channel_id=1, source_target_pairs={{0,257},{256,0},{1,256},{257,1},{2,259},{258,2},{3,258},{259,3},{4... | collective-permute-start | bytes 1327112 | tf_op jit(solution)/shard_map/ppermute | solution.py:35
  70.7 10.6 %collective-permute-start.5 = (bf16[6,96,384]{2,1,0:T(8,128)(2,1)}, bf16[6,96,384]{2,1,0:T(8,128)(2,1)}, u32[]{:S(2)}, u32[]{:S(2)}) collective-permute-start(bf16[6,96,384]{2,1,0:T(8,128)(2,1)} %pad_maximum_fusion.1), channel_id=1, source_target_pairs={{0,256},{256,1},{1,257},{257,0},{2,258},{258,3},{3,259},{259,2},{4... | collective-permute-start | bytes 1327112 | tf_op jit(solution)/shard_map/ppermute | solution.py:35
  73.3 14.5 %collective-permute-start.7 = (bf16[4,96,384]{2,1,0:T(8,128)(2,1)}, bf16[4,96,384]{2,1,0:T(8,128)(2,1)S(1)}, u32[]{:S(2)}, u32[]{:S(2)}) collective-permute-start(bf16[4,96,384]{2,1,0:T(8,128)(2,1)} %slice.41), channel_id=1, source_target_pairs={{0,32},{16,48},{32,64},{48,80},{64,96},{80,112},{96,128},{112,144}... | collective-permute-start | bytes 884744 | tf_op jit(solution)/shard_map/ppermute | solution.py:27
  80.9 14.1 %slice-start.1 = ((bf16[4,192,384]{2,1,0:T(8,128)(2,1)}), bf16[4,96,384]{2,1,0:T(8,128)(2,1)S(1)}, s32[]{:S(2)}) async-start(bf16[4,192,384]{2,1,0:T(8,128)(2,1)} %copy-done.5), calls=%async_computation.4 | async-start | bytes 589824 | tf_op jit(solution)/shard_map/slice | solution.py:222
  80.9 19.0 %slice-start = ((bf16[4,192,384]{2,1,0:T(8,128)(2,1)}), bf16[4,96,384]{2,1,0:T(8,128)(2,1)S(1)}, s32[]{:S(2)}) async-start(bf16[4,192,384]{2,1,0:T(8,128)(2,1)} %copy-done.4), calls=%async_computation.3 | async-start | bytes 589824 | tf_op jit(solution)/shard_map/slice | solution.py:223
  87.8 25.9 %all-to-all-start.1 = ((bf16[32,16,384]{2,1,0:T(8,128)(2,1)}), bf16[32,16,384]{2,1,0:T(8,128)(2,1)S(1)}, u32[]{:S(2)}, u32[]{:S(2)}) async-start(bf16[32,16,384]{2,1,0:T(8,128)(2,1)} %bitcast.34), calls=%async_computation.1 | async-start | bytes 786432 | tf_op jit(solution)/shard_map/all_to_all | solution.py:257
  95.0 29.5 %copy-start.7 = (bf16[2,96,384]{2,1,0:T(8,128)(2,1)}, bf16[2,96,384]{2,1,0:T(8,128)(2,1)S(1)}, u32[]{:S(2)}) copy-start(bf16[2,96,384]{2,1,0:T(8,128)(2,1)S(1)} %get-tuple-element.37.refs_3_) | copy-start | bytes 442372
  95.0 29.5 %copy-start.8 = (bf16[2,96,384]{2,1,0:T(8,128)(2,1)}, bf16[2,96,384]{2,1,0:T(8,128)(2,1)S(1)}, u32[]{:S(2)}) copy-start(bf16[2,96,384]{2,1,0:T(8,128)(2,1)S(1)} %get-tuple-element.38.refs_4_) | copy-start | bytes 442372
  95.0 10.5 %collective-permute-start.9 = (bf16[6,96,384]{2,1,0:T(8,128)(2,1)S(1)}, bf16[6,96,384]{2,1,0:T(8,128)(2,1)S(1)}, u32[]{:S(2)}, u32[]{:S(2)}) collective-permute-start(bf16[6,96,384]{2,1,0:T(8,128)(2,1)S(1)} %pad_maximum_fusion.4), channel_id=1, source_target_pairs={{0,257},{256,0},{1,256},{257,1},{2,259},{258,2},{3,258},{259,3},{4... | collective-permute-start | bytes 1327112 | tf_op jit(solution)/shard_map/ppermute | solution.py:35
  100.0 10.6 %collective-permute-start.8 = (bf16[6,96,384]{2,1,0:T(8,128)(2,1)S(1)}, bf16[6,96,384]{2,1,0:T(8,128)(2,1)S(1)}, u32[]{:S(2)}, u32[]{:S(2)}) collective-permute-start(bf16[6,96,384]{2,1,0:T(8,128)(2,1)S(1)} %pad_maximum_fusion.3), channel_id=1, source_target_pairs={{0,256},{256,1},{1,257},{257,0},{2,258},{258,3},{3,259},{259,2},{4... | collective-permute-start | bytes 1327112 | tf_op jit(solution)/shard_map/ppermute | solution.py:35
  105.6 18.9 %copy-start.13 = (bf16[6,96,384]{2,1,0:T(8,128)(2,1)}, bf16[6,96,384]{2,1,0:T(8,128)(2,1)S(1)}, u32[]{:S(2)}) copy-start(bf16[6,96,384]{2,1,0:T(8,128)(2,1)S(1)} %collective-permute-done.9.refs_7_) | copy-start | bytes 1327108
  110.6 13.8 %copy-start.14 = (bf16[6,96,384]{2,1,0:T(8,128)(2,1)}, bf16[6,96,384]{2,1,0:T(8,128)(2,1)S(1)}, u32[]{:S(2)}) copy-start(bf16[6,96,384]{2,1,0:T(8,128)(2,1)S(1)} %collective-permute-done.8.refs_6_) | copy-start | bytes 1327108
  115.9 22.9 %all-to-all-start.2 = ((bf16[32,16,128]{2,1,0:T(8,128)(2,1)}), bf16[32,16,128]{2,1,0:T(8,128)(2,1)S(1)}, u32[]{:S(2)}, u32[]{:S(2)}) async-start(bf16[32,16,128]{2,1,0:T(8,128)(2,1)} %bitcast.11), calls=%async_computation.2 | async-start | bytes 262144 | tf_op jit(solution)/shard_map/all_to_all | solution.py:273
  124.4 45.2 %copy-start.1 = (s32[4]{0:T(128)S(1)}, s32[4]{0:T(128)}, u32[]{:S(2)}) copy-start(s32[4]{0:T(128)} %pad_add_fusion.place) | copy-start | bytes 52
  138.8 33.3 %copy-start = (bf16[512,384]{1,0:T(8,128)(2,1)S(1)}, bf16[512,384]{1,0:T(8,128)(2,1)}, u32[]{:S(2)}) copy-start(bf16[512,384]{1,0:T(8,128)(2,1)} %hidden.3) | copy-start | bytes 1179652
  138.8 33.4 %copy-start.2 = (f32[3072]{0:T(1024)S(1)}, f32[3072]{0:T(1024)}, u32[]{:S(2)}) copy-start(f32[3072]{0:T(1024)} %param.10) | copy-start | bytes 36868
  139.8 12.4 %collective-permute-start.10 = (bf16[2,512,128]{2,1,0:T(8,128)(2,1)S(1)}, bf16[2,512,128]{2,1,0:T(8,128)(2,1)S(1)}, u32[]{:S(2)}, u32[]{:S(2)}) collective-permute-start(bf16[2,512,128]{2,1,0:T(8,128)(2,1)S(1)} %get-tuple-element.40), channel_id=1, source_target_pairs={{0,4},{4,8},{8,12},{12,0},{1,5},{5,9},{9,13},{13,1},{2,6},{6,10},{... | collective-permute-start | bytes 786440 | tf_op jit(solution)/shard_map/ppermute | solution.py:31
  144.1 8.2 %collective-permute-start.11 = (bf16[2,512,128]{2,1,0:T(8,128)(2,1)S(1)}, bf16[2,512,128]{2,1,0:T(8,128)(2,1)S(1)}, u32[]{:S(2)}, u32[]{:S(2)}) collective-permute-start(bf16[2,512,128]{2,1,0:T(8,128)(2,1)S(1)} %get-tuple-element.40), channel_id=1, source_target_pairs={{0,12},{4,0},{8,4},{12,8},{1,13},{5,1},{9,5},{13,9},{2,14},{6,2},{... | collective-permute-start | bytes 786440 | tf_op jit(solution)/shard_map/ppermute | solution.py:31
  149.1 8.7 %collective-permute-start.12 = (bf16[2,512,128]{2,1,0:T(8,128)(2,1)S(1)}, bf16[2,512,128]{2,1,0:T(8,128)(2,1)S(1)}, u32[]{:S(2)}, u32[]{:S(2)}) collective-permute-start(bf16[2,512,128]{2,1,0:T(8,128)(2,1)S(1)} %get-tuple-element.40), channel_id=1, source_target_pairs={{0,8},{4,12},{8,0},{12,4},{1,9},{5,13},{9,1},{13,5},{2,10},{6,14},... | collective-permute-start | bytes 786440 | tf_op jit(solution)/shard_map/ppermute | solution.py:31
  157.9 14.2 %collective-permute-start.13 = (bf16[4,2,512,128]{3,2,1,0:T(8,128)(2,1)S(1)}, bf16[4,2,512,128]{3,2,1,0:T(8,128)(2,1)S(1)}, u32[]{:S(2)}, u32[]{:S(2)}) collective-permute-start(bf16[4,2,512,128]{3,2,1,0:T(8,128)(2,1)S(1)} %pad_maximum_fusion.heads), channel_id=1, source_target_pairs={{0,2},{2,0},{1,3},{3,1},{4,6},{6,4},{5,7},{7,5},{8,10},{10,8},{9,1... | collective-permute-start | bytes 3145736 | tf_op jit(solution)/shard_map/ppermute | solution.py:39
  (2 other events, 12.2 us)

commit v7 on v6

--- a/solution.py
+++ b/solution.py
@@ -17,8 +17,8 @@
 SMEM = pl.BlockSpec(memory_space=pltpu.SMEM)
 HBM = pl.BlockSpec(memory_space=pl.ANY)
 COLUMNS = pl.BlockSpec((8, 256, 384), lambda i: (0, 2, 0))
-ROWS = pl.BlockSpec((256, 384), lambda i: (i, 0))
-HEADS = pl.BlockSpec((4, 2, 256, HD), lambda i: (0, 0, i, 0))
+ROWS = pl.BlockSpec((512, 384), lambda i: (i, 0))
+HEADS = pl.BlockSpec((4, 2, 512, HD), lambda i: (0, 0, i, 0))
 
 Y_PLACE = (0, 2, 1, 3)
 
@@ -228,13 +228,13 @@
     normed = pl.pallas_call(
         norm_kernel,
         out_shape=jax.ShapeDtypeStruct((512, D), BF16),
-        grid=(4,),
+        grid=(2,),
         in_specs=[
-            pl.BlockSpec((8, 128, 384), lambda i: (0, i, 0)),
+            pl.BlockSpec((8, 256, 384), lambda i: (0, i, 0)),
             pl.BlockSpec((24, 128), lambda i: (0, 0)),
             pl.BlockSpec((24, 128), lambda i: (0, 0)),
         ],
-        out_specs=pl.BlockSpec((128, D), lambda i: (i, 0)),
+        out_specs=pl.BlockSpec((256, D), lambda i: (i, 0)),
         name="norm",
         **params(20_000_000, 6_000_000),
     )(arrived, shift, scale)
@@ -295,20 +295,20 @@
     share = pl.pallas_call(
         share_kernel,
         out_shape=jax.ShapeDtypeStruct((512, 384), F32),
-        grid=(2,),
+        grid=(1,),
         in_specs=[SMEM, HEADS, COLUMNS],
         out_specs=ROWS,
-        scratch_shapes=[pltpu.VMEM((256, 1024), BF16)],
+        scratch_shapes=[pltpu.VMEM((512, 1024), BF16)],
         name="share",
         **params(400_000_000, 4_000_000, 24),
     )(place, mine, arrived)
     return pl.pallas_call(
         mixed_kernel,
         out_shape=jax.ShapeDtypeStruct((512, 384), BF16),
-        grid=(2,),
+        grid=(1,),
         in_specs=[SMEM, HEADS, COLUMNS, ROWS, ROWS, pl.BlockSpec((24, 128), lambda i: (0, 0))],
         out_specs=ROWS,
-        scratch_shapes=[pltpu.VMEM((256, 1024), BF16)],
+        scratch_shapes=[pltpu.VMEM((512, 1024), BF16)],
         name="mixed",
         **params(400_000_000, 5_000_000, 24),
     )(place, theirs, arrived, share, hidden, gate)

time: 176 us -> 175 us (level)
  transfers between devices with their start and end apart: 17 -> 17, of which waited for: 8 -> 9; matrix products, arithmetic and copies ran while one was open for 2% -> 2% of each run, Pallas kernels for 13% -> 13%
where the time goes in v7:
time: 175 us
  starting transfers between devices  83.5 us (48%)
  Pallas kernels  30.6 us (17%)
  waiting for transfers between devices  27.4 us (16%)
  blocking collectives  27 us (15%)
  other arithmetic  3.66 us (2%)
  local copies, waits for them, and re-layouts  2.04 us (1%)
    all_gather x1, blocking collectives, body(): own = lax.all_gather(shards, 'zh', axis=0)  27 us
    ppermute x5, starting transfers between devices, along_y(): lax.ppermute(value, ('yl', 'dp'), [(Y_PLACE[i], Y_PLACE[(i + step) % 4])...  16.5 us
    ppermute x5, starting transfers between devices, along_z(): lax.ppermute(value, ('zh', 'zl'), [(i, (i + step) % 16) for i in range(16)])  16 us
    ppermute x3, starting transfers between devices, along_x(): return lax.ppermute(value, 'x', [(i, (i + step) % 4) for i in range(4)])  12 us
    ppermute x1, starting transfers between devices, other_core(): return lax.ppermute(value, 'c', [(0, 1), (1, 0)])  11.8 us
    all_to_all x1, starting transfers between devices, body(): lax.all_to_all(sent, ('x', 'c'), split_axis=0, concat_axis=0, tiled=True)  11.5 us
    ppermute x5, waiting for transfers between devices, along_y(): lax.ppermute(value, ('yl', 'dp'), [(Y_PLACE[i], Y_PLACE[(i + step) % 4])...  9.18 us
    all_to_all x1, starting transfers between devices, body(): lax.all_to_all(temporal.reshape(32, 16, HD), ('yl', 'zh', 'zl'), split_ax...  8.66 us
  transfers between devices with their start and end apart: 17, of which 9 were waited for; matrix products, arithmetic and copies ran while one was open for 2% of the time, Pallas kernels for 13%

profile of v7, /device:TPU:1, one launch (start us, length us, event | category | flops | bytes accessed | tf_op | source)
XLA Modules:
  0.0 174.6 jit_solution(197985619337429479)
XLA Ops:
  0.0 3.4 %sent.1 = bf16[8,768,384]{2,1,0:T(8,128)(2,1)} custom-call(bf16[512,384]{1,0:T(8,128)(2,1)} %hidden.3, bf16[2,128,3072]{2,1,0:T(8,128)(2,1)} %w_out.1), custom_call_target="tpu_custom_call" | custom-call | bytes 7000000 | tf_op jit(solution)/shard_map/sent/pallas_call | solution.py:197
  3.5 11.5 %all-to-all-start = ((bf16[8,768,384]{2,1,0:T(8,128)(2,1)}), bf16[8,768,384]{2,1,0:T(8,128)(2,1)}, u32[]{:S(2)}, u32[]{:S(2)}) async-start(bf16[8,768,384]{2,1,0:T(8,128)(2,1)} %sent.1), calls=%async_computation | async-start | bytes 9437184 | tf_op jit(solution)/shard_map/all_to_all | solution.py:211
  15.8 27.0 %all-gather = bf16[768,384]{1,0:T(8,128)(2,1)S(1)} all-gather(bf16[192,384]{1,0:T(8,128)(2,1)S(1)} %pad_maximum_fusion.6), channel_id=2, replica_groups=mesh['yl'=2,'zh'=4,'zl'=4,'x'=4,'c'=2,'dp'=2] {'zh'}, dimensions={0}, use_global_device_ids=true | all-gather | bytes 737280 | tf_op jit(solution)/shard_map/all_gather | solution.py:213
  42.8 1.9 %collective-permute-start = (bf16[4,192,384]{2,1,0:T(8,128)(2,1)S(1)}, bf16[4,192,384]{2,1,0:T(8,128)(2,1)S(1)}, u32[]{:S(2)}, u32[]{:S(2)}) collective-permute-start(bf16[4,192,384]{2,1,0:T(8,128)(2,1)S(1)} %bitcast.27), channel_id=1, source_target_pairs={{0,16},{16,32},{32,48},{48,64},{64,80},{80,96},{96,112},{112,128},... | collective-permute-start | bytes 1769480 | tf_op jit(solution)/shard_map/ppermute | solution.py:27
  44.7 4.8 %collective-permute-start.1 = (bf16[4,192,384]{2,1,0:T(8,128)(2,1)S(1)}, bf16[4,192,384]{2,1,0:T(8,128)(2,1)S(1)}, u32[]{:S(2)}, u32[]{:S(2)}) collective-permute-start(bf16[4,192,384]{2,1,0:T(8,128)(2,1)S(1)} %bitcast.28), channel_id=1, source_target_pairs={{0,240},{16,0},{32,16},{48,32},{64,48},{80,64},{96,80},{112,96},{1... | collective-permute-start | bytes 1769480 | tf_op jit(solution)/shard_map/ppermute | solution.py:27
  49.5 3.2 %collective-permute-start.3 = (bf16[4,192,384]{2,1,0:T(8,128)(2,1)S(1)}, bf16[4,192,384]{2,1,0:T(8,128)(2,1)S(1)}, u32[]{:S(2)}, u32[]{:S(2)}) collective-permute-start(bf16[4,192,384]{2,1,0:T(8,128)(2,1)S(1)} %bitcast.29), channel_id=1, source_target_pairs={{0,256},{256,1},{1,257},{257,0},{2,258},{258,3},{3,259},{259,2},{4... | collective-permute-start | bytes 1769480 | tf_op jit(solution)/shard_map/ppermute | solution.py:35
  52.8 1.9 %collective-permute-start.2 = (bf16[2,96,384]{2,1,0:T(8,128)(2,1)S(1)}, bf16[2,96,384]{2,1,0:T(8,128)(2,1)S(1)}, u32[]{:S(2)}, u32[]{:S(2)}) collective-permute-start(bf16[2,96,384]{2,1,0:T(8,128)(2,1)S(1)} %get-tuple-element.36), channel_id=1, source_target_pairs={{0,32},{16,48},{32,64},{48,80},{64,96},{80,112},{96,128},{112,144}... | collective-permute-start | bytes 442376 | tf_op jit(solution)/shard_map/ppermute | solution.py:27
  54.7 5.5 %collective-permute-start.4 = (bf16[2,96,384]{2,1,0:T(8,128)(2,1)S(1)}, bf16[2,96,384]{2,1,0:T(8,128)(2,1)S(1)}, u32[]{:S(2)}, u32[]{:S(2)}) collective-permute-start(bf16[2,96,384]{2,1,0:T(8,128)(2,1)S(1)} %get-tuple-element.35), channel_id=1, source_target_pairs={{0,224},{16,240},{32,0},{48,16},{64,32},{80,48},{96,64},{112,80},{... | collective-permute-start | bytes 442376 | tf_op jit(solution)/shard_map/ppermute | solution.py:27
  60.8 3.6 %collective-permute-done.2.refs_3_ = bf16[2,96,384]{2,1,0:T(8,128)(2,1)S(1)} collective-permute-done((bf16[2,96,384]{2,1,0:T(8,128)(2,1)S(1)}, bf16[2,96,384]{2,1,0:T(8,128)(2,1)S(1)}, u32[]{:S(2)}, u32[]{:S(2)}) %collective-permute-start.2) | collective-permute-done | bytes 147488 | tf_op jit(solution)/shard_map/ppermute | solution.py:27
  65.4 4.3 %collective-permute-start.6 = (bf16[6,96,384]{2,1,0:T(8,128)(2,1)}, bf16[6,96,384]{2,1,0:T(8,128)(2,1)S(1)}, u32[]{:S(2)}, u32[]{:S(2)}) collective-permute-start(bf16[6,96,384]{2,1,0:T(8,128)(2,1)} %pad_maximum_fusion.2), channel_id=1, source_target_pairs={{0,257},{256,0},{1,256},{257,1},{2,259},{258,2},{3,258},{259,3},{4... | collective-permute-start | bytes 1327112 | tf_op jit(solution)/shard_map/ppermute | solution.py:35
  70.7 1.9 %collective-permute-start.5 = (bf16[6,96,384]{2,1,0:T(8,128)(2,1)}, bf16[6,96,384]{2,1,0:T(8,128)(2,1)}, u32[]{:S(2)}, u32[]{:S(2)}) collective-permute-start(bf16[6,96,384]{2,1,0:T(8,128)(2,1)} %pad_maximum_fusion.1), channel_id=1, source_target_pairs={{0,256},{256,1},{1,257},{257,0},{2,258},{258,3},{3,259},{259,2},{4... | collective-permute-start | bytes 1327112 | tf_op jit(solution)/shard_map/ppermute | solution.py:35
  73.3 1.9 %collective-permute-start.7 = (bf16[4,96,384]{2,1,0:T(8,128)(2,1)}, bf16[4,96,384]{2,1,0:T(8,128)(2,1)S(1)}, u32[]{:S(2)}, u32[]{:S(2)}) collective-permute-start(bf16[4,96,384]{2,1,0:T(8,128)(2,1)} %slice.41), channel_id=1, source_target_pairs={{0,32},{16,48},{32,64},{48,80},{64,96},{80,112},{96,128},{112,144}... | collective-permute-start | bytes 884744 | tf_op jit(solution)/shard_map/ppermute | solution.py:27
  75.2 5.3 %norm.1.refs_8_.refs_9_ = bf16[512,3072]{1,0:T(8,128)(2,1)} custom-call(bf16[8,768,384]{2,1,0:T(8,128)(2,1)} %all-to-all-done.blocks_ref.w_out, f32[24,128]{1,0:T(8,128)} %bitcast.42, f32[24,128]{1,0:T(8,128)} %bitcast.43), custom_call_target="tpu_custom_call" | custom-call | flops 20000000 | bytes 6000000 | tf_op jit(solution)/shard_map/norm/pallas_call | solution.py:228
  81.4 6.1 %temporal_project.1 = bf16[512,384]{1,0:T(8,128)(2,1)} custom-call(s32[4]{0:T(128)} %pad_add_fusion.place, bf16[4,192,384]{2,1,0:T(8,128)(2,1)} %bitcast.32, bf16[4,192,384]{2,1,0:T(8,128)(2,1)} %copy-done.4, bf16[4,192,384]{2,1,0:T(8,128)(2,1)} %copy-done.5, bf16[2,96,384]{2,1,0:T(8,128)(2,1)} %copy-done.9, bf16[2,96,384]{2,1,0:T(8,128)(2,1)} %copy-done.10, ...), custom_call_target="tpu_custom_call" | custom-call | flops 1200000000 | bytes 6000000 | tf_op jit(solution)/shard_map/temporal_project/pallas_call | solution.py:242
  87.5 7.1 %all-to-all-start.1 = ((bf16[32,16,384]{2,1,0:T(8,128)(2,1)}), bf16[32,16,384]{2,1,0:T(8,128)(2,1)S(1)}, u32[]{:S(2)}, u32[]{:S(2)}) async-start(bf16[32,16,384]{2,1,0:T(8,128)(2,1)} %bitcast.34), calls=%async_computation.1 | async-start | bytes 786432 | tf_op jit(solution)/shard_map/all_to_all | solution.py:257
  94.8 5.1 %collective-permute-start.9 = (bf16[6,96,384]{2,1,0:T(8,128)(2,1)S(1)}, bf16[6,96,384]{2,1,0:T(8,128)(2,1)S(1)}, u32[]{:S(2)}, u32[]{:S(2)}) collective-permute-start(bf16[6,96,384]{2,1,0:T(8,128)(2,1)S(1)} %pad_maximum_fusion.4), channel_id=1, source_target_pairs={{0,257},{256,0},{1,256},{257,1},{2,259},{258,2},{3,258},{259,3},{4... | collective-permute-start | bytes 1327112 | tf_op jit(solution)/shard_map/ppermute | solution.py:35
  100.0 1.9 %collective-permute-start.8 = (bf16[6,96,384]{2,1,0:T(8,128)(2,1)S(1)}, bf16[6,96,384]{2,1,0:T(8,128)(2,1)S(1)}, u32[]{:S(2)}, u32[]{:S(2)}) collective-permute-start(bf16[6,96,384]{2,1,0:T(8,128)(2,1)S(1)} %pad_maximum_fusion.3), channel_id=1, source_target_pairs={{0,256},{256,1},{1,257},{257,0},{2,258},{258,3},{3,259},{259,2},{4... | collective-permute-start | bytes 1327112 | tf_op jit(solution)/shard_map/ppermute | solution.py:35
  101.9 3.4 %collective-permute-done.9.refs_7_ = bf16[6,96,384]{2,1,0:T(8,128)(2,1)S(1)} collective-permute-done((bf16[6,96,384]{2,1,0:T(8,128)(2,1)S(1)}, bf16[6,96,384]{2,1,0:T(8,128)(2,1)S(1)}, u32[]{:S(2)}, u32[]{:S(2)}) %collective-permute-start.9) | collective-permute-done | bytes 442400 | tf_op jit(solution)/shard_map/ppermute | solution.py:35
  105.3 5.2 %collective-permute-done.8.refs_6_ = bf16[6,96,384]{2,1,0:T(8,128)(2,1)S(1)} collective-permute-done((bf16[6,96,384]{2,1,0:T(8,128)(2,1)S(1)}, bf16[6,96,384]{2,1,0:T(8,128)(2,1)S(1)}, u32[]{:S(2)}, u32[]{:S(2)}) %collective-permute-start.8) | collective-permute-done | bytes 442400 | tf_op jit(solution)/shard_map/ppermute | solution.py:35
  110.6 2.9 %all-to-all-done.1 = bf16[32,16,384]{2,1,0:T(8,128)(2,1)S(1)} async-done(((bf16[32,16,384]{2,1,0:T(8,128)(2,1)}), bf16[32,16,384]{2,1,0:T(8,128)(2,1)S(1)}, u32[]{:S(2)}, u32[]{:S(2)}) %all-to-all-start.1) | async-done | bytes 393248 | tf_op jit(solution)/shard_map/all_to_all | solution.py:257
  113.5 2.2 %temporal.1 = bf16[512,128]{1,0:T(8,128)(2,1)} custom-call(bf16[512,384]{1,0:T(8,128)(2,1)S(1)} %bitcast.25), custom_call_target="tpu_custom_call" | custom-call | flops 140000000 | bytes 500000 | tf_op jit(solution)/shard_map/temporal/pallas_call | solution.py:265
  115.7 8.7 %all-to-all-start.2 = ((bf16[32,16,128]{2,1,0:T(8,128)(2,1)}), bf16[32,16,128]{2,1,0:T(8,128)(2,1)S(1)}, u32[]{:S(2)}, u32[]{:S(2)}) async-start(bf16[32,16,128]{2,1,0:T(8,128)(2,1)} %bitcast.11), calls=%async_computation.2 | async-start | bytes 262144 | tf_op jit(solution)/shard_map/all_to_all | solution.py:273
  124.4 8.5 %spatial.1 = bf16[512,128]{1,0:T(8,128)(2,1)} custom-call(s32[4]{0:T(128)} %pad_add_fusion.place, bf16[4,192,384]{2,1,0:T(8,128)(2,1)} %bitcast.33, bf16[4,192,384]{2,1,0:T(8,128)(2,1)} %copy-done.4, bf16[4,192,384]{2,1,0:T(8,128)(2,1)} %copy-done.5, bf16[2,96,384]{2,1,0:T(8,128)(2,1)} %copy-done.7, bf16[2,96,384]{2,1,0:T(8,128)(2,1)} %copy-done.8, ...), custom_call_target="tpu_custom_call" | custom-call | flops 1300000000 | bytes 6000000 | tf_op jit(solution)/shard_map/spatial/pallas_call | solution.py:276
  132.9 6.0 %all-to-all-done.2 = bf16[32,16,128]{2,1,0:T(8,128)(2,1)S(1)} async-done(((bf16[32,16,128]{2,1,0:T(8,128)(2,1)}), bf16[32,16,128]{2,1,0:T(8,128)(2,1)S(1)}, u32[]{:S(2)}, u32[]{:S(2)}) %all-to-all-start.2) | async-done | bytes 131104 | tf_op jit(solution)/shard_map/all_to_all | solution.py:273
  138.9 1.0 fusion
  139.9 4.0 %collective-permute-start.10 = (bf16[2,512,128]{2,1,0:T(8,128)(2,1)S(1)}, bf16[2,512,128]{2,1,0:T(8,128)(2,1)S(1)}, u32[]{:S(2)}, u32[]{:S(2)}) collective-permute-start(bf16[2,512,128]{2,1,0:T(8,128)(2,1)S(1)} %get-tuple-element.40), channel_id=1, source_target_pairs={{0,4},{4,8},{8,12},{12,0},{1,5},{5,9},{9,13},{13,1},{2,6},{6,10},{... | collective-permute-start | bytes 786440 | tf_op jit(solution)/shard_map/ppermute | solution.py:31
  143.9 4.9 %collective-permute-start.11 = (bf16[2,512,128]{2,1,0:T(8,128)(2,1)S(1)}, bf16[2,512,128]{2,1,0:T(8,128)(2,1)S(1)}, u32[]{:S(2)}, u32[]{:S(2)}) collective-permute-start(bf16[2,512,128]{2,1,0:T(8,128)(2,1)S(1)} %get-tuple-element.40), channel_id=1, source_target_pairs={{0,12},{4,0},{8,4},{12,8},{1,13},{5,1},{9,5},{13,9},{2,14},{6,2},{... | collective-permute-start | bytes 786440 | tf_op jit(solution)/shard_map/ppermute | solution.py:31
  148.8 3.1 %collective-permute-start.12 = (bf16[2,512,128]{2,1,0:T(8,128)(2,1)S(1)}, bf16[2,512,128]{2,1,0:T(8,128)(2,1)S(1)}, u32[]{:S(2)}, u32[]{:S(2)}) collective-permute-start(bf16[2,512,128]{2,1,0:T(8,128)(2,1)S(1)} %get-tuple-element.40), channel_id=1, source_target_pairs={{0,8},{4,12},{8,0},{12,4},{1,9},{5,13},{9,1},{13,5},{2,10},{6,14},... | collective-permute-start | bytes 786440 | tf_op jit(solution)/shard_map/ppermute | solution.py:31
  152.1 5.4 %collective-permute-done.12 = bf16[2,512,128]{2,1,0:T(8,128)(2,1)S(1)} collective-permute-done((bf16[2,512,128]{2,1,0:T(8,128)(2,1)S(1)}, bf16[2,512,128]{2,1,0:T(8,128)(2,1)S(1)}, u32[]{:S(2)}, u32[]{:S(2)}) %collective-permute-start.12) | collective-permute-done | bytes 262176 | tf_op jit(solution)/shard_map/ppermute | solution.py:31
  157.6 11.8 %collective-permute-start.13 = (bf16[4,2,512,128]{3,2,1,0:T(8,128)(2,1)S(1)}, bf16[4,2,512,128]{3,2,1,0:T(8,128)(2,1)S(1)}, u32[]{:S(2)}, u32[]{:S(2)}) collective-permute-start(bf16[4,2,512,128]{3,2,1,0:T(8,128)(2,1)S(1)} %pad_maximum_fusion.heads), channel_id=1, source_target_pairs={{0,2},{2,0},{1,3},{3,1},{4,6},{6,4},{5,7},{7,5},{8,10},{10,8},{9,1... | collective-permute-start | bytes 3145736 | tf_op jit(solution)/shard_map/ppermute | solution.py:39
  169.4 2.2 %share.1 = f32[512,384]{1,0:T(8,128)S(1)} custom-call(s32[4]{0:T(128)S(1)} %copy-done.1, bf16[4,2,512,128]{3,2,1,0:T(8,128)(2,1)S(1)} %pad_maximum_fusion.heads, bf16[8,768,384]{2,1,0:T(8,128)(2,1)} %all-to-all-done.blocks_ref.w_out), custom_call_target="tpu_custom_call" | custom-call | flops 400000000 | bytes 4000000 | tf_op jit(solution)/shard_map/share/pallas_call | solution.py:295
  171.7 2.9 %mixed.1 = bf16[512,384]{1,0:T(8,128)(2,1)} custom-call(s32[4]{0:T(128)S(1)} %copy-done.1, bf16[4,2,512,128]{3,2,1,0:T(8,128)(2,1)S(1)} %collective-permute-done.13.heads, bf16[8,768,384]{2,1,0:T(8,128)(2,1)} %all-to-all-done.blocks_ref.w_out, f32[512,384]{1,0:T(8,128)S(1)} %share.1, bf16[512,384]{1,0:T(8,128)(2,1)S(1)} %copy-done, f32[24,128]{1,0:T(8,128)S(1)} %bitcast.26), custom_call_target="tpu_custom_call" | custom-call | flops 400000000 | bytes 5000000 | tf_op jit(solution)/shard_map/mixed/pallas_call | solution.py:305
  (59 shorter events, 5.6 us)
Async XLA Ops:
  3.4 11.5 %copy-start.11 = (bf16[96,3,2,128]{3,2,1,0:T(2,128)(2,1)S(1)}, bf16[96,3,2,128]{3,2,1,0:T(2,128)(2,1)}, u32[]{:S(2)}) copy-start(bf16[96,3,2,128]{3,2,1,0:T(2,128)(2,1)} %param.11) | copy-start | bytes 442372
  3.5 71.8 %all-to-all-start = ((bf16[8,768,384]{2,1,0:T(8,128)(2,1)}), bf16[8,768,384]{2,1,0:T(8,128)(2,1)}, u32[]{:S(2)}, u32[]{:S(2)}) async-start(bf16[8,768,384]{2,1,0:T(8,128)(2,1)} %sent.1), calls=%async_computation | async-start | bytes 9437184 | tf_op jit(solution)/shard_map/all_to_all | solution.py:211
  42.8 37.8 %copy-start.3 = (bf16[768,384]{1,0:T(8,128)(2,1)}, bf16[768,384]{1,0:T(8,128)(2,1)S(1)}, u32[]{:S(2)}) copy-start(bf16[768,384]{1,0:T(8,128)(2,1)S(1)} %all-gather) | copy-start | bytes 1769476
  42.8 21.6 %collective-permute-start = (bf16[4,192,384]{2,1,0:T(8,128)(2,1)S(1)}, bf16[4,192,384]{2,1,0:T(8,128)(2,1)S(1)}, u32[]{:S(2)}, u32[]{:S(2)}) collective-permute-start(bf16[4,192,384]{2,1,0:T(8,128)(2,1)S(1)} %bitcast.27), channel_id=1, source_target_pairs={{0,16},{16,32},{32,48},{48,64},{64,80},{80,96},{96,112},{112,128},... | collective-permute-start | bytes 1769480 | tf_op jit(solution)/shard_map/ppermute | solution.py:27
  44.7 19.7 %collective-permute-start.1 = (bf16[4,192,384]{2,1,0:T(8,128)(2,1)S(1)}, bf16[4,192,384]{2,1,0:T(8,128)(2,1)S(1)}, u32[]{:S(2)}, u32[]{:S(2)}) collective-permute-start(bf16[4,192,384]{2,1,0:T(8,128)(2,1)S(1)} %bitcast.28), channel_id=1, source_target_pairs={{0,240},{16,0},{32,16},{48,32},{64,48},{80,64},{96,80},{112,96},{1... | collective-permute-start | bytes 1769480 | tf_op jit(solution)/shard_map/ppermute | solution.py:27
  49.5 14.9 %collective-permute-start.3 = (bf16[4,192,384]{2,1,0:T(8,128)(2,1)S(1)}, bf16[4,192,384]{2,1,0:T(8,128)(2,1)S(1)}, u32[]{:S(2)}, u32[]{:S(2)}) collective-permute-start(bf16[4,192,384]{2,1,0:T(8,128)(2,1)S(1)} %bitcast.29), channel_id=1, source_target_pairs={{0,256},{256,1},{1,257},{257,0},{2,258},{258,3},{3,259},{259,2},{4... | collective-permute-start | bytes 1769480 | tf_op jit(solution)/shard_map/ppermute | solution.py:35
  52.8 11.6 %collective-permute-start.2 = (bf16[2,96,384]{2,1,0:T(8,128)(2,1)S(1)}, bf16[2,96,384]{2,1,0:T(8,128)(2,1)S(1)}, u32[]{:S(2)}, u32[]{:S(2)}) collective-permute-start(bf16[2,96,384]{2,1,0:T(8,128)(2,1)S(1)} %get-tuple-element.36), channel_id=1, source_target_pairs={{0,32},{16,48},{32,64},{48,80},{64,96},{80,112},{96,128},{112,144}... | collective-permute-start | bytes 442376 | tf_op jit(solution)/shard_map/ppermute | solution.py:27
  54.7 15.1 %collective-permute-start.4 = (bf16[2,96,384]{2,1,0:T(8,128)(2,1)S(1)}, bf16[2,96,384]{2,1,0:T(8,128)(2,1)S(1)}, u32[]{:S(2)}, u32[]{:S(2)}) collective-permute-start(bf16[2,96,384]{2,1,0:T(8,128)(2,1)S(1)} %get-tuple-element.35), channel_id=1, source_target_pairs={{0,224},{16,240},{32,0},{48,16},{64,32},{80,48},{96,64},{112,80},{... | collective-permute-start | bytes 442376 | tf_op jit(solution)/shard_map/ppermute | solution.py:27
  64.4 16.2 %copy-start.9 = (bf16[2,96,384]{2,1,0:T(8,128)(2,1)}, bf16[2,96,384]{2,1,0:T(8,128)(2,1)S(1)}, u32[]{:S(2)}) copy-start(bf16[2,96,384]{2,1,0:T(8,128)(2,1)S(1)} %collective-permute-done.2.refs_3_) | copy-start | bytes 442372
  64.4 16.2 %copy-start.4 = (bf16[4,192,384]{2,1,0:T(8,128)(2,1)}, bf16[4,192,384]{2,1,0:T(8,128)(2,1)S(1)}, u32[]{:S(2)}) copy-start(bf16[4,192,384]{2,1,0:T(8,128)(2,1)S(1)} %collective-permute-done.refs_1_) | copy-start | bytes 1769476
  64.4 16.2 %copy-start.5 = (bf16[4,192,384]{2,1,0:T(8,128)(2,1)}, bf16[4,192,384]{2,1,0:T(8,128)(2,1)S(1)}, u32[]{:S(2)}) copy-start(bf16[4,192,384]{2,1,0:T(8,128)(2,1)S(1)} %collective-permute-done.1.refs_2_) | copy-start | bytes 1769476
  64.4 16.2 %copy-start.6 = (bf16[4,192,384]{2,1,0:T(8,128)(2,1)}, bf16[4,192,384]{2,1,0:T(8,128)(2,1)S(1)}, u32[]{:S(2)}) copy-start(bf16[4,192,384]{2,1,0:T(8,128)(2,1)S(1)} %collective-permute-done.3.refs_5_) | copy-start | bytes 1769476
  65.4 15.2 %collective-permute-start.6 = (bf16[6,96,384]{2,1,0:T(8,128)(2,1)}, bf16[6,96,384]{2,1,0:T(8,128)(2,1)S(1)}, u32[]{:S(2)}, u32[]{:S(2)}) collective-permute-start(bf16[6,96,384]{2,1,0:T(8,128)(2,1)} %pad_maximum_fusion.2), channel_id=1, source_target_pairs={{0,257},{256,0},{1,256},{257,1},{2,259},{258,2},{3,258},{259,3},{4... | collective-permute-start | bytes 1327112 | tf_op jit(solution)/shard_map/ppermute | solution.py:35
  70.7 10.6 %collective-permute-start.5 = (bf16[6,96,384]{2,1,0:T(8,128)(2,1)}, bf16[6,96,384]{2,1,0:T(8,128)(2,1)}, u32[]{:S(2)}, u32[]{:S(2)}) collective-permute-start(bf16[6,96,384]{2,1,0:T(8,128)(2,1)} %pad_maximum_fusion.1), channel_id=1, source_target_pairs={{0,256},{256,1},{1,257},{257,0},{2,258},{258,3},{3,259},{259,2},{4... | collective-permute-start | bytes 1327112 | tf_op jit(solution)/shard_map/ppermute | solution.py:35
  73.3 14.2 %collective-permute-start.7 = (bf16[4,96,384]{2,1,0:T(8,128)(2,1)}, bf16[4,96,384]{2,1,0:T(8,128)(2,1)S(1)}, u32[]{:S(2)}, u32[]{:S(2)}) collective-permute-start(bf16[4,96,384]{2,1,0:T(8,128)(2,1)} %slice.41), channel_id=1, source_target_pairs={{0,32},{16,48},{32,64},{48,80},{64,96},{80,112},{96,128},{112,144}... | collective-permute-start | bytes 884744 | tf_op jit(solution)/shard_map/ppermute | solution.py:27
  80.6 14.1 %slice-start.1 = ((bf16[4,192,384]{2,1,0:T(8,128)(2,1)}), bf16[4,96,384]{2,1,0:T(8,128)(2,1)S(1)}, s32[]{:S(2)}) async-start(bf16[4,192,384]{2,1,0:T(8,128)(2,1)} %copy-done.5), calls=%async_computation.4 | async-start | bytes 589824 | tf_op jit(solution)/shard_map/slice | solution.py:222
  80.6 19.3 %slice-start = ((bf16[4,192,384]{2,1,0:T(8,128)(2,1)}), bf16[4,96,384]{2,1,0:T(8,128)(2,1)S(1)}, s32[]{:S(2)}) async-start(bf16[4,192,384]{2,1,0:T(8,128)(2,1)} %copy-done.4), calls=%async_computation.3 | async-start | bytes 589824 | tf_op jit(solution)/shard_map/slice | solution.py:223
  87.5 26.0 %all-to-all-start.1 = ((bf16[32,16,384]{2,1,0:T(8,128)(2,1)}), bf16[32,16,384]{2,1,0:T(8,128)(2,1)S(1)}, u32[]{:S(2)}, u32[]{:S(2)}) async-start(bf16[32,16,384]{2,1,0:T(8,128)(2,1)} %bitcast.34), calls=%async_computation.1 | async-start | bytes 786432 | tf_op jit(solution)/shard_map/all_to_all | solution.py:257
  94.7 29.6 %copy-start.7 = (bf16[2,96,384]{2,1,0:T(8,128)(2,1)}, bf16[2,96,384]{2,1,0:T(8,128)(2,1)S(1)}, u32[]{:S(2)}) copy-start(bf16[2,96,384]{2,1,0:T(8,128)(2,1)S(1)} %get-tuple-element.37.refs_3_) | copy-start | bytes 442372
  94.7 29.6 %copy-start.8 = (bf16[2,96,384]{2,1,0:T(8,128)(2,1)}, bf16[2,96,384]{2,1,0:T(8,128)(2,1)S(1)}, u32[]{:S(2)}) copy-start(bf16[2,96,384]{2,1,0:T(8,128)(2,1)S(1)} %get-tuple-element.38.refs_4_) | copy-start | bytes 442372
  94.8 10.5 %collective-permute-start.9 = (bf16[6,96,384]{2,1,0:T(8,128)(2,1)S(1)}, bf16[6,96,384]{2,1,0:T(8,128)(2,1)S(1)}, u32[]{:S(2)}, u32[]{:S(2)}) collective-permute-start(bf16[6,96,384]{2,1,0:T(8,128)(2,1)S(1)} %pad_maximum_fusion.4), channel_id=1, source_target_pairs={{0,257},{256,0},{1,256},{257,1},{2,259},{258,2},{3,258},{259,3},{4... | collective-permute-start | bytes 1327112 | tf_op jit(solution)/shard_map/ppermute | solution.py:35
  100.0 10.6 %collective-permute-start.8 = (bf16[6,96,384]{2,1,0:T(8,128)(2,1)S(1)}, bf16[6,96,384]{2,1,0:T(8,128)(2,1)S(1)}, u32[]{:S(2)}, u32[]{:S(2)}) collective-permute-start(bf16[6,96,384]{2,1,0:T(8,128)(2,1)S(1)} %pad_maximum_fusion.3), channel_id=1, source_target_pairs={{0,256},{256,1},{1,257},{257,0},{2,258},{258,3},{3,259},{259,2},{4... | collective-permute-start | bytes 1327112 | tf_op jit(solution)/shard_map/ppermute | solution.py:35
  105.3 19.0 %copy-start.13 = (bf16[6,96,384]{2,1,0:T(8,128)(2,1)}, bf16[6,96,384]{2,1,0:T(8,128)(2,1)S(1)}, u32[]{:S(2)}) copy-start(bf16[6,96,384]{2,1,0:T(8,128)(2,1)S(1)} %collective-permute-done.9.refs_7_) | copy-start | bytes 1327108
  110.6 13.8 %copy-start.14 = (bf16[6,96,384]{2,1,0:T(8,128)(2,1)}, bf16[6,96,384]{2,1,0:T(8,128)(2,1)S(1)}, u32[]{:S(2)}) copy-start(bf16[6,96,384]{2,1,0:T(8,128)(2,1)S(1)} %collective-permute-done.8.refs_6_) | copy-start | bytes 1327108
  115.7 23.2 %all-to-all-start.2 = ((bf16[32,16,128]{2,1,0:T(8,128)(2,1)}), bf16[32,16,128]{2,1,0:T(8,128)(2,1)S(1)}, u32[]{:S(2)}, u32[]{:S(2)}) async-start(bf16[32,16,128]{2,1,0:T(8,128)(2,1)} %bitcast.11), calls=%async_computation.2 | async-start | bytes 262144 | tf_op jit(solution)/shard_map/all_to_all | solution.py:273
  124.4 45.0 %copy-start.1 = (s32[4]{0:T(128)S(1)}, s32[4]{0:T(128)}, u32[]{:S(2)}) copy-start(s32[4]{0:T(128)} %pad_add_fusion.place) | copy-start | bytes 52
  138.9 32.8 %copy-start = (bf16[512,384]{1,0:T(8,128)(2,1)S(1)}, bf16[512,384]{1,0:T(8,128)(2,1)}, u32[]{:S(2)}) copy-start(bf16[512,384]{1,0:T(8,128)(2,1)} %hidden.3) | copy-start | bytes 1179652
  138.9 32.8 %copy-start.2 = (f32[3072]{0:T(1024)S(1)}, f32[3072]{0:T(1024)}, u32[]{:S(2)}) copy-start(f32[3072]{0:T(1024)} %param.10) | copy-start | bytes 36868
  139.9 12.0 %collective-permute-start.10 = (bf16[2,512,128]{2,1,0:T(8,128)(2,1)S(1)}, bf16[2,512,128]{2,1,0:T(8,128)(2,1)S(1)}, u32[]{:S(2)}, u32[]{:S(2)}) collective-permute-start(bf16[2,512,128]{2,1,0:T(8,128)(2,1)S(1)} %get-tuple-element.40), channel_id=1, source_target_pairs={{0,4},{4,8},{8,12},{12,0},{1,5},{5,9},{9,13},{13,1},{2,6},{6,10},{... | collective-permute-start | bytes 786440 | tf_op jit(solution)/shard_map/ppermute | solution.py:31
  143.9 8.2 %collective-permute-start.11 = (bf16[2,512,128]{2,1,0:T(8,128)(2,1)S(1)}, bf16[2,512,128]{2,1,0:T(8,128)(2,1)S(1)}, u32[]{:S(2)}, u32[]{:S(2)}) collective-permute-start(bf16[2,512,128]{2,1,0:T(8,128)(2,1)S(1)} %get-tuple-element.40), channel_id=1, source_target_pairs={{0,12},{4,0},{8,4},{12,8},{1,13},{5,1},{9,5},{13,9},{2,14},{6,2},{... | collective-permute-start | bytes 786440 | tf_op jit(solution)/shard_map/ppermute | solution.py:31
  148.8 8.7 %collective-permute-start.12 = (bf16[2,512,128]{2,1,0:T(8,128)(2,1)S(1)}, bf16[2,512,128]{2,1,0:T(8,128)(2,1)S(1)}, u32[]{:S(2)}, u32[]{:S(2)}) collective-permute-start(bf16[2,512,128]{2,1,0:T(8,128)(2,1)S(1)} %get-tuple-element.40), channel_id=1, source_target_pairs={{0,8},{4,12},{8,0},{12,4},{1,9},{5,13},{9,1},{13,5},{2,10},{6,14},... | collective-permute-start | bytes 786440 | tf_op jit(solution)/shard_map/ppermute | solution.py:31
  157.6 14.0 %collective-permute-start.13 = (bf16[4,2,512,128]{3,2,1,0:T(8,128)(2,1)S(1)}, bf16[4,2,512,128]{3,2,1,0:T(8,128)(2,1)S(1)}, u32[]{:S(2)}, u32[]{:S(2)}) collective-permute-start(bf16[4,2,512,128]{3,2,1,0:T(8,128)(2,1)S(1)} %pad_maximum_fusion.heads), channel_id=1, source_target_pairs={{0,2},{2,0},{1,3},{3,1},{4,6},{6,4},{5,7},{7,5},{8,10},{10,8},{9,1... | collective-permute-start | bytes 3145736 | tf_op jit(solution)/shard_map/ppermute | solution.py:39
  (2 other events, 12.2 us)

commit v8 on v7

--- a/solution.py
+++ b/solution.py
@@ -57,7 +57,7 @@
             normed[rows, j * 128 : j * 128 + 128] = value.astype(BF16)
         return 0
 
-    lax.fori_loop(0, normed.shape[0] // 16, rows_of, 0, unroll=4)
+    lax.fori_loop(0, normed.shape[0] // 16, rows_of, 0, unroll=8)
 
 
 def project(normed, weight, parts, sems, fetched):

time: 175 us -> 175 us (level)
  no operation moved by 1% of the time
where the time goes in v8:
time: 175 us; the launch traced here: 174 us
  starting transfers between devices  83.5 us (48%)
  Pallas kernels  30.4 us (17%)
  waiting for transfers between devices  27.6 us (16%)
  blocking collectives  27 us (15%)
  other arithmetic  3.66 us (2%)
  local copies, waits for them, and re-layouts  1.81 us (1%)
    all_gather x1, blocking collectives, body(): own = lax.all_gather(shards, 'zh', axis=0)  27 us
    ppermute x5, starting transfers between devices, along_y(): lax.ppermute(value, ('yl', 'dp'), [(Y_PLACE[i], Y_PLACE[(i + step) % 4])...  16.5 us
    ppermute x5, starting transfers between devices, along_z(): lax.ppermute(value, ('zh', 'zl'), [(i, (i + step) % 16) for i in range(16)])  16 us
    ppermute x3, starting transfers between devices, along_x(): return lax.ppermute(value, 'x', [(i, (i + step) % 4) for i in range(4)])  11.9 us
    ppermute x1, starting transfers between devices, other_core(): return lax.ppermute(value, 'c', [(0, 1), (1, 0)])  11.8 us
    all_to_all x1, starting transfers between devices, body(): lax.all_to_all(sent, ('x', 'c'), split_axis=0, concat_axis=0, tiled=True)  11.5 us
    ppermute x5, waiting for transfers between devices, along_y(): lax.ppermute(value, ('yl', 'dp'), [(Y_PLACE[i], Y_PLACE[(i + step) % 4])...  9.43 us
    all_to_all x1, starting transfers between devices, body(): lax.all_to_all(temporal.reshape(32, 16, HD), ('yl', 'zh', 'zl'), split_ax...  8.66 us
  transfers between devices with their start and end apart: 17, of which 9 were waited for; matrix products, arithmetic and copies ran while one was open for 2% of the time, Pallas kernels for 13%

profile of v8, /device:TPU:1, one launch (start us, length us, event | category | flops | bytes accessed | tf_op | source)
XLA Modules:
  0.0 174.3 jit_solution(7463981715435489856)
XLA Ops:
  0.0 3.4 %sent.1 = bf16[8,768,384]{2,1,0:T(8,128)(2,1)} custom-call(bf16[512,384]{1,0:T(8,128)(2,1)} %hidden.3, bf16[2,128,3072]{2,1,0:T(8,128)(2,1)} %w_out.1), custom_call_target="tpu_custom_call" | custom-call | bytes 7000000 | tf_op jit(solution)/shard_map/sent/pallas_call | solution.py:197
  3.5 11.5 %all-to-all-start = ((bf16[8,768,384]{2,1,0:T(8,128)(2,1)}), bf16[8,768,384]{2,1,0:T(8,128)(2,1)}, u32[]{:S(2)}, u32[]{:S(2)}) async-start(bf16[8,768,384]{2,1,0:T(8,128)(2,1)} %sent.1), calls=%async_computation | async-start | bytes 9437184 | tf_op jit(solution)/shard_map/all_to_all | solution.py:211
  15.8 27.0 %all-gather = bf16[768,384]{1,0:T(8,128)(2,1)S(1)} all-gather(bf16[192,384]{1,0:T(8,128)(2,1)S(1)} %pad_maximum_fusion.6), channel_id=2, replica_groups=mesh['yl'=2,'zh'=4,'zl'=4,'x'=4,'c'=2,'dp'=2] {'zh'}, dimensions={0}, use_global_device_ids=true | all-gather | bytes 737280 | tf_op jit(solution)/shard_map/all_gather | solution.py:213
  42.8 1.9 %collective-permute-start = (bf16[4,192,384]{2,1,0:T(8,128)(2,1)S(1)}, bf16[4,192,384]{2,1,0:T(8,128)(2,1)S(1)}, u32[]{:S(2)}, u32[]{:S(2)}) collective-permute-start(bf16[4,192,384]{2,1,0:T(8,128)(2,1)S(1)} %bitcast.27), channel_id=1, source_target_pairs={{0,16},{16,32},{32,48},{48,64},{64,80},{80,96},{96,112},{112,128},... | collective-permute-start | bytes 1769480 | tf_op jit(solution)/shard_map/ppermute | solution.py:27
  44.7 4.8 %collective-permute-start.1 = (bf16[4,192,384]{2,1,0:T(8,128)(2,1)S(1)}, bf16[4,192,384]{2,1,0:T(8,128)(2,1)S(1)}, u32[]{:S(2)}, u32[]{:S(2)}) collective-permute-start(bf16[4,192,384]{2,1,0:T(8,128)(2,1)S(1)} %bitcast.28), channel_id=1, source_target_pairs={{0,240},{16,0},{32,16},{48,32},{64,48},{80,64},{96,80},{112,96},{1... | collective-permute-start | bytes 1769480 | tf_op jit(solution)/shard_map/ppermute | solution.py:27
  49.5 3.2 %collective-permute-start.3 = (bf16[4,192,384]{2,1,0:T(8,128)(2,1)S(1)}, bf16[4,192,384]{2,1,0:T(8,128)(2,1)S(1)}, u32[]{:S(2)}, u32[]{:S(2)}) collective-permute-start(bf16[4,192,384]{2,1,0:T(8,128)(2,1)S(1)} %bitcast.29), channel_id=1, source_target_pairs={{0,256},{256,1},{1,257},{257,0},{2,258},{258,3},{3,259},{259,2},{4... | collective-permute-start | bytes 1769480 | tf_op jit(solution)/shard_map/ppermute | solution.py:35
  52.8 1.9 %collective-permute-start.2 = (bf16[2,96,384]{2,1,0:T(8,128)(2,1)S(1)}, bf16[2,96,384]{2,1,0:T(8,128)(2,1)S(1)}, u32[]{:S(2)}, u32[]{:S(2)}) collective-permute-start(bf16[2,96,384]{2,1,0:T(8,128)(2,1)S(1)} %get-tuple-element.36), channel_id=1, source_target_pairs={{0,32},{16,48},{32,64},{48,80},{64,96},{80,112},{96,128},{112,144}... | collective-permute-start | bytes 442376 | tf_op jit(solution)/shard_map/ppermute | solution.py:27
  54.7 5.5 %collective-permute-start.4 = (bf16[2,96,384]{2,1,0:T(8,128)(2,1)S(1)}, bf16[2,96,384]{2,1,0:T(8,128)(2,1)S(1)}, u32[]{:S(2)}, u32[]{:S(2)}) collective-permute-start(bf16[2,96,384]{2,1,0:T(8,128)(2,1)S(1)} %get-tuple-element.35), channel_id=1, source_target_pairs={{0,224},{16,240},{32,0},{48,16},{64,32},{80,48},{96,64},{112,80},{... | collective-permute-start | bytes 442376 | tf_op jit(solution)/shard_map/ppermute | solution.py:27
  60.8 3.6 %collective-permute-done.2.refs_3_ = bf16[2,96,384]{2,1,0:T(8,128)(2,1)S(1)} collective-permute-done((bf16[2,96,384]{2,1,0:T(8,128)(2,1)S(1)}, bf16[2,96,384]{2,1,0:T(8,128)(2,1)S(1)}, u32[]{:S(2)}, u32[]{:S(2)}) %collective-permute-start.2) | collective-permute-done | bytes 147488 | tf_op jit(solution)/shard_map/ppermute | solution.py:27
  65.4 4.3 %collective-permute-start.6 = (bf16[6,96,384]{2,1,0:T(8,128)(2,1)}, bf16[6,96,384]{2,1,0:T(8,128)(2,1)S(1)}, u32[]{:S(2)}, u32[]{:S(2)}) collective-permute-start(bf16[6,96,384]{2,1,0:T(8,128)(2,1)} %pad_maximum_fusion.2), channel_id=1, source_target_pairs={{0,257},{256,0},{1,256},{257,1},{2,259},{258,2},{3,258},{259,3},{4... | collective-permute-start | bytes 1327112 | tf_op jit(solution)/shard_map/ppermute | solution.py:35
  70.7 1.9 %collective-permute-start.5 = (bf16[6,96,384]{2,1,0:T(8,128)(2,1)}, bf16[6,96,384]{2,1,0:T(8,128)(2,1)}, u32[]{:S(2)}, u32[]{:S(2)}) collective-permute-start(bf16[6,96,384]{2,1,0:T(8,128)(2,1)} %pad_maximum_fusion.1), channel_id=1, source_target_pairs={{0,256},{256,1},{1,257},{257,0},{2,258},{258,3},{3,259},{259,2},{4... | collective-permute-start | bytes 1327112 | tf_op jit(solution)/shard_map/ppermute | solution.py:35
  73.3 1.9 %collective-permute-start.7 = (bf16[4,96,384]{2,1,0:T(8,128)(2,1)}, bf16[4,96,384]{2,1,0:T(8,128)(2,1)S(1)}, u32[]{:S(2)}, u32[]{:S(2)}) collective-permute-start(bf16[4,96,384]{2,1,0:T(8,128)(2,1)} %slice.41), channel_id=1, source_target_pairs={{0,32},{16,48},{32,64},{48,80},{64,96},{80,112},{96,128},{112,144}... | collective-permute-start | bytes 884744 | tf_op jit(solution)/shard_map/ppermute | solution.py:27
  75.2 5.1 %norm.1.refs_8_.refs_9_ = bf16[512,3072]{1,0:T(8,128)(2,1)} custom-call(bf16[8,768,384]{2,1,0:T(8,128)(2,1)} %all-to-all-done.blocks_ref.w_out, f32[24,128]{1,0:T(8,128)} %bitcast.42, f32[24,128]{1,0:T(8,128)} %bitcast.43), custom_call_target="tpu_custom_call" | custom-call | flops 20000000 | bytes 6000000 | tf_op jit(solution)/shard_map/norm/pallas_call | solution.py:228
  81.2 6.1 %temporal_project.1 = bf16[512,384]{1,0:T(8,128)(2,1)} custom-call(s32[4]{0:T(128)} %pad_add_fusion.place, bf16[4,192,384]{2,1,0:T(8,128)(2,1)} %bitcast.32, bf16[4,192,384]{2,1,0:T(8,128)(2,1)} %copy-done.4, bf16[4,192,384]{2,1,0:T(8,128)(2,1)} %copy-done.5, bf16[2,96,384]{2,1,0:T(8,128)(2,1)} %copy-done.9, bf16[2,96,384]{2,1,0:T(8,128)(2,1)} %copy-done.10, ...), custom_call_target="tpu_custom_call" | custom-call | flops 1200000000 | bytes 6000000 | tf_op jit(solution)/shard_map/temporal_project/pallas_call | solution.py:242
  87.3 7.4 %all-to-all-start.1 = ((bf16[32,16,384]{2,1,0:T(8,128)(2,1)}), bf16[32,16,384]{2,1,0:T(8,128)(2,1)S(1)}, u32[]{:S(2)}, u32[]{:S(2)}) async-start(bf16[32,16,384]{2,1,0:T(8,128)(2,1)} %bitcast.34), calls=%async_computation.1 | async-start | bytes 786432 | tf_op jit(solution)/shard_map/all_to_all | solution.py:257
  94.8 5.1 %collective-permute-start.9 = (bf16[6,96,384]{2,1,0:T(8,128)(2,1)S(1)}, bf16[6,96,384]{2,1,0:T(8,128)(2,1)S(1)}, u32[]{:S(2)}, u32[]{:S(2)}) collective-permute-start(bf16[6,96,384]{2,1,0:T(8,128)(2,1)S(1)} %pad_maximum_fusion.4), channel_id=1, source_target_pairs={{0,257},{256,0},{1,256},{257,1},{2,259},{258,2},{3,258},{259,3},{4... | collective-permute-start | bytes 1327112 | tf_op jit(solution)/shard_map/ppermute | solution.py:35
  100.0 1.9 %collective-permute-start.8 = (bf16[6,96,384]{2,1,0:T(8,128)(2,1)S(1)}, bf16[6,96,384]{2,1,0:T(8,128)(2,1)S(1)}, u32[]{:S(2)}, u32[]{:S(2)}) collective-permute-start(bf16[6,96,384]{2,1,0:T(8,128)(2,1)S(1)} %pad_maximum_fusion.3), channel_id=1, source_target_pairs={{0,256},{256,1},{1,257},{257,0},{2,258},{258,3},{3,259},{259,2},{4... | collective-permute-start | bytes 1327112 | tf_op jit(solution)/shard_map/ppermute | solution.py:35
  101.9 3.4 %collective-permute-done.9.refs_7_ = bf16[6,96,384]{2,1,0:T(8,128)(2,1)S(1)} collective-permute-done((bf16[6,96,384]{2,1,0:T(8,128)(2,1)S(1)}, bf16[6,96,384]{2,1,0:T(8,128)(2,1)S(1)}, u32[]{:S(2)}, u32[]{:S(2)}) %collective-permute-start.9) | collective-permute-done | bytes 442400 | tf_op jit(solution)/shard_map/ppermute | solution.py:35
  105.3 5.2 %collective-permute-done.8.refs_6_ = bf16[6,96,384]{2,1,0:T(8,128)(2,1)S(1)} collective-permute-done((bf16[6,96,384]{2,1,0:T(8,128)(2,1)S(1)}, bf16[6,96,384]{2,1,0:T(8,128)(2,1)S(1)}, u32[]{:S(2)}, u32[]{:S(2)}) %collective-permute-start.8) | collective-permute-done | bytes 442400 | tf_op jit(solution)/shard_map/ppermute | solution.py:35
  110.6 2.9 %all-to-all-done.1 = bf16[32,16,384]{2,1,0:T(8,128)(2,1)S(1)} async-done(((bf16[32,16,384]{2,1,0:T(8,128)(2,1)}), bf16[32,16,384]{2,1,0:T(8,128)(2,1)S(1)}, u32[]{:S(2)}, u32[]{:S(2)}) %all-to-all-start.1) | async-done | bytes 393248 | tf_op jit(solution)/shard_map/all_to_all | solution.py:257
  113.5 2.2 %temporal.1 = bf16[512,128]{1,0:T(8,128)(2,1)} custom-call(bf16[512,384]{1,0:T(8,128)(2,1)S(1)} %bitcast.25), custom_call_target="tpu_custom_call" | custom-call | flops 140000000 | bytes 500000 | tf_op jit(solution)/shard_map/temporal/pallas_call | solution.py:265
  115.7 8.7 %all-to-all-start.2 = ((bf16[32,16,128]{2,1,0:T(8,128)(2,1)}), bf16[32,16,128]{2,1,0:T(8,128)(2,1)S(1)}, u32[]{:S(2)}, u32[]{:S(2)}) async-start(bf16[32,16,128]{2,1,0:T(8,128)(2,1)} %bitcast.11), calls=%async_computation.2 | async-start | bytes 262144 | tf_op jit(solution)/shard_map/all_to_all | solution.py:273
  124.4 8.5 %spatial.1 = bf16[512,128]{1,0:T(8,128)(2,1)} custom-call(s32[4]{0:T(128)} %pad_add_fusion.place, bf16[4,192,384]{2,1,0:T(8,128)(2,1)} %bitcast.33, bf16[4,192,384]{2,1,0:T(8,128)(2,1)} %copy-done.4, bf16[4,192,384]{2,1,0:T(8,128)(2,1)} %copy-done.5, bf16[2,96,384]{2,1,0:T(8,128)(2,1)} %copy-done.7, bf16[2,96,384]{2,1,0:T(8,128)(2,1)} %copy-done.8, ...), custom_call_target="tpu_custom_call" | custom-call | flops 1300000000 | bytes 6000000 | tf_op jit(solution)/shard_map/spatial/pallas_call | solution.py:276
  132.9 5.9 %all-to-all-done.2 = bf16[32,16,128]{2,1,0:T(8,128)(2,1)S(1)} async-done(((bf16[32,16,128]{2,1,0:T(8,128)(2,1)}), bf16[32,16,128]{2,1,0:T(8,128)(2,1)S(1)}, u32[]{:S(2)}, u32[]{:S(2)}) %all-to-all-start.2) | async-done | bytes 131104 | tf_op jit(solution)/shard_map/all_to_all | solution.py:273
  138.8 1.0 fusion
  139.8 3.8 %collective-permute-start.10 = (bf16[2,512,128]{2,1,0:T(8,128)(2,1)S(1)}, bf16[2,512,128]{2,1,0:T(8,128)(2,1)S(1)}, u32[]{:S(2)}, u32[]{:S(2)}) collective-permute-start(bf16[2,512,128]{2,1,0:T(8,128)(2,1)S(1)} %get-tuple-element.40), channel_id=1, source_target_pairs={{0,4},{4,8},{8,12},{12,0},{1,5},{5,9},{9,13},{13,1},{2,6},{6,10},{... | collective-permute-start | bytes 786440 | tf_op jit(solution)/shard_map/ppermute | solution.py:31
  143.6 4.9 %collective-permute-start.11 = (bf16[2,512,128]{2,1,0:T(8,128)(2,1)S(1)}, bf16[2,512,128]{2,1,0:T(8,128)(2,1)S(1)}, u32[]{:S(2)}, u32[]{:S(2)}) collective-permute-start(bf16[2,512,128]{2,1,0:T(8,128)(2,1)S(1)} %get-tuple-element.40), channel_id=1, source_target_pairs={{0,12},{4,0},{8,4},{12,8},{1,13},{5,1},{9,5},{13,9},{2,14},{6,2},{... | collective-permute-start | bytes 786440 | tf_op jit(solution)/shard_map/ppermute | solution.py:31
  148.5 3.1 %collective-permute-start.12 = (bf16[2,512,128]{2,1,0:T(8,128)(2,1)S(1)}, bf16[2,512,128]{2,1,0:T(8,128)(2,1)S(1)}, u32[]{:S(2)}, u32[]{:S(2)}) collective-permute-start(bf16[2,512,128]{2,1,0:T(8,128)(2,1)S(1)} %get-tuple-element.40), channel_id=1, source_target_pairs={{0,8},{4,12},{8,0},{12,4},{1,9},{5,13},{9,1},{13,5},{2,10},{6,14},... | collective-permute-start | bytes 786440 | tf_op jit(solution)/shard_map/ppermute | solution.py:31
  151.8 5.4 %collective-permute-done.12 = bf16[2,512,128]{2,1,0:T(8,128)(2,1)S(1)} collective-permute-done((bf16[2,512,128]{2,1,0:T(8,128)(2,1)S(1)}, bf16[2,512,128]{2,1,0:T(8,128)(2,1)S(1)}, u32[]{:S(2)}, u32[]{:S(2)}) %collective-permute-start.12) | collective-permute-done | bytes 262176 | tf_op jit(solution)/shard_map/ppermute | solution.py:31
  157.4 11.8 %collective-permute-start.13 = (bf16[4,2,512,128]{3,2,1,0:T(8,128)(2,1)S(1)}, bf16[4,2,512,128]{3,2,1,0:T(8,128)(2,1)S(1)}, u32[]{:S(2)}, u32[]{:S(2)}) collective-permute-start(bf16[4,2,512,128]{3,2,1,0:T(8,128)(2,1)S(1)} %pad_maximum_fusion.heads), channel_id=1, source_target_pairs={{0,2},{2,0},{1,3},{3,1},{4,6},{6,4},{5,7},{7,5},{8,10},{10,8},{9,1... | collective-permute-start | bytes 3145736 | tf_op jit(solution)/shard_map/ppermute | solution.py:39
  169.2 2.2 %share.1 = f32[512,384]{1,0:T(8,128)S(1)} custom-call(s32[4]{0:T(128)S(1)} %copy-done.1, bf16[4,2,512,128]{3,2,1,0:T(8,128)(2,1)S(1)} %pad_maximum_fusion.heads, bf16[8,768,384]{2,1,0:T(8,128)(2,1)} %all-to-all-done.blocks_ref.w_out), custom_call_target="tpu_custom_call" | custom-call | flops 400000000 | bytes 4000000 | tf_op jit(solution)/shard_map/share/pallas_call | solution.py:295
  171.4 2.9 %mixed.1 = bf16[512,384]{1,0:T(8,128)(2,1)} custom-call(s32[4]{0:T(128)S(1)} %copy-done.1, bf16[4,2,512,128]{3,2,1,0:T(8,128)(2,1)S(1)} %collective-permute-done.13.heads, bf16[8,768,384]{2,1,0:T(8,128)(2,1)} %all-to-all-done.blocks_ref.w_out, f32[512,384]{1,0:T(8,128)S(1)} %share.1, bf16[512,384]{1,0:T(8,128)(2,1)S(1)} %copy-done, f32[24,128]{1,0:T(8,128)S(1)} %bitcast.26), custom_call_target="tpu_custom_call" | custom-call | flops 400000000 | bytes 5000000 | tf_op jit(solution)/shard_map/mixed/pallas_call | solution.py:305
  (59 shorter events, 5.6 us)
Async XLA Ops:
  3.4 11.5 %copy-start.11 = (bf16[96,3,2,128]{3,2,1,0:T(2,128)(2,1)S(1)}, bf16[96,3,2,128]{3,2,1,0:T(2,128)(2,1)}, u32[]{:S(2)}) copy-start(bf16[96,3,2,128]{3,2,1,0:T(2,128)(2,1)} %param.11) | copy-start | bytes 442372
  3.5 71.8 %all-to-all-start = ((bf16[8,768,384]{2,1,0:T(8,128)(2,1)}), bf16[8,768,384]{2,1,0:T(8,128)(2,1)}, u32[]{:S(2)}, u32[]{:S(2)}) async-start(bf16[8,768,384]{2,1,0:T(8,128)(2,1)} %sent.1), calls=%async_computation | async-start | bytes 9437184 | tf_op jit(solution)/shard_map/all_to_all | solution.py:211
  42.8 37.5 %copy-start.3 = (bf16[768,384]{1,0:T(8,128)(2,1)}, bf16[768,384]{1,0:T(8,128)(2,1)S(1)}, u32[]{:S(2)}) copy-start(bf16[768,384]{1,0:T(8,128)(2,1)S(1)} %all-gather) | copy-start | bytes 1769476
  42.8 21.6 %collective-permute-start = (bf16[4,192,384]{2,1,0:T(8,128)(2,1)S(1)}, bf16[4,192,384]{2,1,0:T(8,128)(2,1)S(1)}, u32[]{:S(2)}, u32[]{:S(2)}) collective-permute-start(bf16[4,192,384]{2,1,0:T(8,128)(2,1)S(1)} %bitcast.27), channel_id=1, source_target_pairs={{0,16},{16,32},{32,48},{48,64},{64,80},{80,96},{96,112},{112,128},... | collective-permute-start | bytes 1769480 | tf_op jit(solution)/shard_map/ppermute | solution.py:27
  44.7 19.7 %collective-permute-start.1 = (bf16[4,192,384]{2,1,0:T(8,128)(2,1)S(1)}, bf16[4,192,384]{2,1,0:T(8,128)(2,1)S(1)}, u32[]{:S(2)}, u32[]{:S(2)}) collective-permute-start(bf16[4,192,384]{2,1,0:T(8,128)(2,1)S(1)} %bitcast.28), channel_id=1, source_target_pairs={{0,240},{16,0},{32,16},{48,32},{64,48},{80,64},{96,80},{112,96},{1... | collective-permute-start | bytes 1769480 | tf_op jit(solution)/shard_map/ppermute | solution.py:27
  49.5 14.9 %collective-permute-start.3 = (bf16[4,192,384]{2,1,0:T(8,128)(2,1)S(1)}, bf16[4,192,384]{2,1,0:T(8,128)(2,1)S(1)}, u32[]{:S(2)}, u32[]{:S(2)}) collective-permute-start(bf16[4,192,384]{2,1,0:T(8,128)(2,1)S(1)} %bitcast.29), channel_id=1, source_target_pairs={{0,256},{256,1},{1,257},{257,0},{2,258},{258,3},{3,259},{259,2},{4... | collective-permute-start | bytes 1769480 | tf_op jit(solution)/shard_map/ppermute | solution.py:35
  52.8 11.6 %collective-permute-start.2 = (bf16[2,96,384]{2,1,0:T(8,128)(2,1)S(1)}, bf16[2,96,384]{2,1,0:T(8,128)(2,1)S(1)}, u32[]{:S(2)}, u32[]{:S(2)}) collective-permute-start(bf16[2,96,384]{2,1,0:T(8,128)(2,1)S(1)} %get-tuple-element.36), channel_id=1, source_target_pairs={{0,32},{16,48},{32,64},{48,80},{64,96},{80,112},{96,128},{112,144}... | collective-permute-start | bytes 442376 | tf_op jit(solution)/shard_map/ppermute | solution.py:27
  54.7 15.1 %collective-permute-start.4 = (bf16[2,96,384]{2,1,0:T(8,128)(2,1)S(1)}, bf16[2,96,384]{2,1,0:T(8,128)(2,1)S(1)}, u32[]{:S(2)}, u32[]{:S(2)}) collective-permute-start(bf16[2,96,384]{2,1,0:T(8,128)(2,1)S(1)} %get-tuple-element.35), channel_id=1, source_target_pairs={{0,224},{16,240},{32,0},{48,16},{64,32},{80,48},{96,64},{112,80},{... | collective-permute-start | bytes 442376 | tf_op jit(solution)/shard_map/ppermute | solution.py:27
  64.4 16.0 %copy-start.9 = (bf16[2,96,384]{2,1,0:T(8,128)(2,1)}, bf16[2,96,384]{2,1,0:T(8,128)(2,1)S(1)}, u32[]{:S(2)}) copy-start(bf16[2,96,384]{2,1,0:T(8,128)(2,1)S(1)} %collective-permute-done.2.refs_3_) | copy-start | bytes 442372
  64.4 16.0 %copy-start.4 = (bf16[4,192,384]{2,1,0:T(8,128)(2,1)}, bf16[4,192,384]{2,1,0:T(8,128)(2,1)S(1)}, u32[]{:S(2)}) copy-start(bf16[4,192,384]{2,1,0:T(8,128)(2,1)S(1)} %collective-permute-done.refs_1_) | copy-start | bytes 1769476
  64.4 16.0 %copy-start.5 = (bf16[4,192,384]{2,1,0:T(8,128)(2,1)}, bf16[4,192,384]{2,1,0:T(8,128)(2,1)S(1)}, u32[]{:S(2)}) copy-start(bf16[4,192,384]{2,1,0:T(8,128)(2,1)S(1)} %collective-permute-done.1.refs_2_) | copy-start | bytes 1769476
  64.4 16.0 %copy-start.6 = (bf16[4,192,384]{2,1,0:T(8,128)(2,1)}, bf16[4,192,384]{2,1,0:T(8,128)(2,1)S(1)}, u32[]{:S(2)}) copy-start(bf16[4,192,384]{2,1,0:T(8,128)(2,1)S(1)} %collective-permute-done.3.refs_5_) | copy-start | bytes 1769476
  65.4 14.9 %collective-permute-start.6 = (bf16[6,96,384]{2,1,0:T(8,128)(2,1)}, bf16[6,96,384]{2,1,0:T(8,128)(2,1)S(1)}, u32[]{:S(2)}, u32[]{:S(2)}) collective-permute-start(bf16[6,96,384]{2,1,0:T(8,128)(2,1)} %pad_maximum_fusion.2), channel_id=1, source_target_pairs={{0,257},{256,0},{1,256},{257,1},{2,259},{258,2},{3,258},{259,3},{4... | collective-permute-start | bytes 1327112 | tf_op jit(solution)/shard_map/ppermute | solution.py:35
  70.7 10.6 %collective-permute-start.5 = (bf16[6,96,384]{2,1,0:T(8,128)(2,1)}, bf16[6,96,384]{2,1,0:T(8,128)(2,1)}, u32[]{:S(2)}, u32[]{:S(2)}) collective-permute-start(bf16[6,96,384]{2,1,0:T(8,128)(2,1)} %pad_maximum_fusion.1), channel_id=1, source_target_pairs={{0,256},{256,1},{1,257},{257,0},{2,258},{258,3},{3,259},{259,2},{4... | collective-permute-start | bytes 1327112 | tf_op jit(solution)/shard_map/ppermute | solution.py:35
  73.3 14.0 %collective-permute-start.7 = (bf16[4,96,384]{2,1,0:T(8,128)(2,1)}, bf16[4,96,384]{2,1,0:T(8,128)(2,1)S(1)}, u32[]{:S(2)}, u32[]{:S(2)}) collective-permute-start(bf16[4,96,384]{2,1,0:T(8,128)(2,1)} %slice.41), channel_id=1, source_target_pairs={{0,32},{16,48},{32,64},{48,80},{64,96},{80,112},{96,128},{112,144}... | collective-permute-start | bytes 884744 | tf_op jit(solution)/shard_map/ppermute | solution.py:27
  80.4 14.3 %slice-start.1 = ((bf16[4,192,384]{2,1,0:T(8,128)(2,1)}), bf16[4,96,384]{2,1,0:T(8,128)(2,1)S(1)}, s32[]{:S(2)}) async-start(bf16[4,192,384]{2,1,0:T(8,128)(2,1)} %copy-done.5), calls=%async_computation.4 | async-start | bytes 589824 | tf_op jit(solution)/shard_map/slice | solution.py:222
  80.4 19.5 %slice-start = ((bf16[4,192,384]{2,1,0:T(8,128)(2,1)}), bf16[4,96,384]{2,1,0:T(8,128)(2,1)S(1)}, s32[]{:S(2)}) async-start(bf16[4,192,384]{2,1,0:T(8,128)(2,1)} %copy-done.4), calls=%async_computation.3 | async-start | bytes 589824 | tf_op jit(solution)/shard_map/slice | solution.py:223
  87.3 26.2 %all-to-all-start.1 = ((bf16[32,16,384]{2,1,0:T(8,128)(2,1)}), bf16[32,16,384]{2,1,0:T(8,128)(2,1)S(1)}, u32[]{:S(2)}, u32[]{:S(2)}) async-start(bf16[32,16,384]{2,1,0:T(8,128)(2,1)} %bitcast.34), calls=%async_computation.1 | async-start | bytes 786432 | tf_op jit(solution)/shard_map/all_to_all | solution.py:257
  94.7 29.6 %copy-start.7 = (bf16[2,96,384]{2,1,0:T(8,128)(2,1)}, bf16[2,96,384]{2,1,0:T(8,128)(2,1)S(1)}, u32[]{:S(2)}) copy-start(bf16[2,96,384]{2,1,0:T(8,128)(2,1)S(1)} %get-tuple-element.37.refs_3_) | copy-start | bytes 442372
  94.7 29.6 %copy-start.8 = (bf16[2,96,384]{2,1,0:T(8,128)(2,1)}, bf16[2,96,384]{2,1,0:T(8,128)(2,1)S(1)}, u32[]{:S(2)}) copy-start(bf16[2,96,384]{2,1,0:T(8,128)(2,1)S(1)} %get-tuple-element.38.refs_4_) | copy-start | bytes 442372
  94.8 10.5 %collective-permute-start.9 = (bf16[6,96,384]{2,1,0:T(8,128)(2,1)S(1)}, bf16[6,96,384]{2,1,0:T(8,128)(2,1)S(1)}, u32[]{:S(2)}, u32[]{:S(2)}) collective-permute-start(bf16[6,96,384]{2,1,0:T(8,128)(2,1)S(1)} %pad_maximum_fusion.4), channel_id=1, source_target_pairs={{0,257},{256,0},{1,256},{257,1},{2,259},{258,2},{3,258},{259,3},{4... | collective-permute-start | bytes 1327112 | tf_op jit(solution)/shard_map/ppermute | solution.py:35
  100.0 10.6 %collective-permute-start.8 = (bf16[6,96,384]{2,1,0:T(8,128)(2,1)S(1)}, bf16[6,96,384]{2,1,0:T(8,128)(2,1)S(1)}, u32[]{:S(2)}, u32[]{:S(2)}) collective-permute-start(bf16[6,96,384]{2,1,0:T(8,128)(2,1)S(1)} %pad_maximum_fusion.3), channel_id=1, source_target_pairs={{0,256},{256,1},{1,257},{257,0},{2,258},{258,3},{3,259},{259,2},{4... | collective-permute-start | bytes 1327112 | tf_op jit(solution)/shard_map/ppermute | solution.py:35
  105.3 19.0 %copy-start.13 = (bf16[6,96,384]{2,1,0:T(8,128)(2,1)}, bf16[6,96,384]{2,1,0:T(8,128)(2,1)S(1)}, u32[]{:S(2)}) copy-start(bf16[6,96,384]{2,1,0:T(8,128)(2,1)S(1)} %collective-permute-done.9.refs_7_) | copy-start | bytes 1327108
  110.6 13.8 %copy-start.14 = (bf16[6,96,384]{2,1,0:T(8,128)(2,1)}, bf16[6,96,384]{2,1,0:T(8,128)(2,1)S(1)}, u32[]{:S(2)}) copy-start(bf16[6,96,384]{2,1,0:T(8,128)(2,1)S(1)} %collective-permute-done.8.refs_6_) | copy-start | bytes 1327108
  115.7 23.1 %all-to-all-start.2 = ((bf16[32,16,128]{2,1,0:T(8,128)(2,1)}), bf16[32,16,128]{2,1,0:T(8,128)(2,1)S(1)}, u32[]{:S(2)}, u32[]{:S(2)}) async-start(bf16[32,16,128]{2,1,0:T(8,128)(2,1)} %bitcast.11), calls=%async_computation.2 | async-start | bytes 262144 | tf_op jit(solution)/shard_map/all_to_all | solution.py:273
  124.4 44.8 %copy-start.1 = (s32[4]{0:T(128)S(1)}, s32[4]{0:T(128)}, u32[]{:S(2)}) copy-start(s32[4]{0:T(128)} %pad_add_fusion.place) | copy-start | bytes 52
  138.8 32.7 %copy-start = (bf16[512,384]{1,0:T(8,128)(2,1)S(1)}, bf16[512,384]{1,0:T(8,128)(2,1)}, u32[]{:S(2)}) copy-start(bf16[512,384]{1,0:T(8,128)(2,1)} %hidden.3) | copy-start | bytes 1179652
  138.8 32.7 %copy-start.2 = (f32[3072]{0:T(1024)S(1)}, f32[3072]{0:T(1024)}, u32[]{:S(2)}) copy-start(f32[3072]{0:T(1024)} %param.10) | copy-start | bytes 36868
  139.8 11.9 %collective-permute-start.10 = (bf16[2,512,128]{2,1,0:T(8,128)(2,1)S(1)}, bf16[2,512,128]{2,1,0:T(8,128)(2,1)S(1)}, u32[]{:S(2)}, u32[]{:S(2)}) collective-permute-start(bf16[2,512,128]{2,1,0:T(8,128)(2,1)S(1)} %get-tuple-element.40), channel_id=1, source_target_pairs={{0,4},{4,8},{8,12},{12,0},{1,5},{5,9},{9,13},{13,1},{2,6},{6,10},{... | collective-permute-start | bytes 786440 | tf_op jit(solution)/shard_map/ppermute | solution.py:31
  143.6 8.2 %collective-permute-start.11 = (bf16[2,512,128]{2,1,0:T(8,128)(2,1)S(1)}, bf16[2,512,128]{2,1,0:T(8,128)(2,1)S(1)}, u32[]{:S(2)}, u32[]{:S(2)}) collective-permute-start(bf16[2,512,128]{2,1,0:T(8,128)(2,1)S(1)} %get-tuple-element.40), channel_id=1, source_target_pairs={{0,12},{4,0},{8,4},{12,8},{1,13},{5,1},{9,5},{13,9},{2,14},{6,2},{... | collective-permute-start | bytes 786440 | tf_op jit(solution)/shard_map/ppermute | solution.py:31
  148.5 8.7 %collective-permute-start.12 = (bf16[2,512,128]{2,1,0:T(8,128)(2,1)S(1)}, bf16[2,512,128]{2,1,0:T(8,128)(2,1)S(1)}, u32[]{:S(2)}, u32[]{:S(2)}) collective-permute-start(bf16[2,512,128]{2,1,0:T(8,128)(2,1)S(1)} %get-tuple-element.40), channel_id=1, source_target_pairs={{0,8},{4,12},{8,0},{12,4},{1,9},{5,13},{9,1},{13,5},{2,10},{6,14},... | collective-permute-start | bytes 786440 | tf_op jit(solution)/shard_map/ppermute | solution.py:31
  157.4 14.0 %collective-permute-start.13 = (bf16[4,2,512,128]{3,2,1,0:T(8,128)(2,1)S(1)}, bf16[4,2,512,128]{3,2,1,0:T(8,128)(2,1)S(1)}, u32[]{:S(2)}, u32[]{:S(2)}) collective-permute-start(bf16[4,2,512,128]{3,2,1,0:T(8,128)(2,1)S(1)} %pad_maximum_fusion.heads), channel_id=1, source_target_pairs={{0,2},{2,0},{1,3},{3,1},{4,6},{6,4},{5,7},{7,5},{8,10},{10,8},{9,1... | collective-permute-start | bytes 3145736 | tf_op jit(solution)/shard_map/ppermute | solution.py:39
  (2 other events, 12.3 us)
